TPU v7x, 32 devices: a whole 2x2x4 slice. The times are simulated.
32 devices in a mesh: groups: 2 (over x), tp: 8 (over z, y), dp: 2 (over core).
Axes of the slice: x: 2, y: 2, z: 4, core: 2. Of those that a mesh axis runs over, the one named last changes fastest.
Arguments:
- queries: bfloat16 [4, 384, 8192], P(('groups', 'dp'), None, 'tp'), parts along dimension 0, may hold values from -200 to 200
- cached_key_rows: bfloat16 [4, 384, 64, 1024], P(('groups', 'dp'), 'tp'), parts along dimension 0, may hold values from -6 to 6
- cached_value_rows: bfloat16 [4, 384, 64, 1024], P(('groups', 'dp'), 'tp'), parts along dimension 0, may hold values from -6 to 6
- fresh_key_value: bfloat16 [4, 384, 2, 1024], P(('groups', 'dp'), 'tp'), parts along dimension 0, may hold values from -6 to 6
- lengths: int32 [4, 384], P(('groups', 'dp'), 'tp'), parts along dimension 0, may hold values from 2 to 64, as said below
- residual: bfloat16 [4, 384, 8192], P(('groups', 'dp'), 'tp'), parts along dimension 0, may hold values from -6 to 6
- output_weight: bfloat16 [8192, 8192], P('tp'), may hold values from -0.0625 to 0.0625
- adapter_down: bfloat16 [64, 8192, 128], P('dp', 'tp'), may hold values from -0.0625 to 0.0625
- adapter_up: bfloat16 [64, 128, 8192], P('dp', None, 'tp'), may hold values from -0.5 to 0.5
- rank: int32 [64], replicated, may hold values from 16 to 128, as said below
- requests: int32 [4, 16], P(('groups', 'dp')), parts along dimension 0, may hold values from 0 to 63, as said below
- row_choice: int32 [4, 384], P(('groups', 'dp')), parts along dimension 0, may hold values from 0 to 47
Outputs:
- block_output: bfloat16 [4, 384, 8192], P(('groups', 'dp'), 'tp'), parts along dimension 0
There are 2 independent parts, one for each index of `groups`. A program takes and returns all parts, laid end to end along the dimension named above; an argument that names none is the same for every part. Nothing has to cross between parts.
Inputs may be any that keep to these rules, and one draw needn't show every extreme that they name: `lengths`: every length from 2 to 64 occurs. `rank`: a multiple of 16; each such multiple occurs. `requests`: the list of data index p names 16 different pool slots, none owned by p; slot s is owned by data index s // 32.
All inputs are finite; a program needn't handle non-finite values.
Results may differ from a plain program's by a relative error of at most 0.008.
Values may be sent and summed in bfloat16 or wider, within the bound.
No kernel may reach another device: no remote copies, remote signals or barrier semaphores. Data moves between devices by JAX's collectives and lax.ppermute only.
A program may use at most 192 MiB of HBM per device.

v0:
```python
import jax
import jax.numpy as jnp
from jax import lax
from jax.sharding import PartitionSpec as P

HEADS = 64
KV_HEADS = 8
HEAD_DIM = 128


ADAPTER_SCALE = 0.25


def attend(query_rows, key_cache, value_cache, new_entries, lengths):
    row_count = query_rows.shape[0]
    positions = key_cache.shape[1]
    groups = HEADS // KV_HEADS
    scale_factor = HEAD_DIM ** (-0.5)
    query_grid = query_rows.reshape(row_count, KV_HEADS, groups, HEAD_DIM)
    key_grid = key_cache.reshape(row_count, positions, KV_HEADS, HEAD_DIM)
    value_grid = value_cache.reshape(row_count, positions, KV_HEADS, HEAD_DIM)
    new_key = new_entries[:, 0].reshape(row_count, KV_HEADS, HEAD_DIM)
    new_value = new_entries[:, 1].reshape(row_count, KV_HEADS, HEAD_DIM)
    scores = (
        jnp.einsum("rkgd,rjkd->rkgj", query_grid, key_grid, preferred_element_type=jnp.float32)
        * scale_factor
    )
    live_mask = jnp.arange(positions)[None, :] < lengths[:, None]
    scores = jnp.where(live_mask[:, None, None, :], scores, -jnp.inf)
    own_score = (
        jnp.einsum("rkgd,rkd->rkg", query_grid, new_key, preferred_element_type=jnp.float32)
        * scale_factor
    )
    peak_score = jnp.maximum(jnp.max(scores, axis=3), own_score)
    weights = jnp.exp(scores - peak_score[..., None])
    own_weight = jnp.exp(own_score - peak_score)
    weight_sum = jnp.sum(weights, axis=3) + own_weight
    prob_cache = (weights / weight_sum[..., None]).astype(jnp.bfloat16)
    prob_new = (own_weight / weight_sum).astype(jnp.bfloat16)
    attended = jnp.einsum(
        "rkgj,rjkd->rkgd", prob_cache, value_grid, preferred_element_type=jnp.float32
    )
    attended = (
        attended
        + prob_new.astype(jnp.float32)[..., None] * new_value.astype(jnp.float32)[:, :, None, :]
    )
    return attended.reshape(row_count, HEADS * HEAD_DIM).astype(jnp.bfloat16)


def rank_lookup(slots_of_rows, rank):
    slot_range = jnp.arange(rank.shape[0], dtype=jnp.int32)
    return jnp.sum(
        jnp.where(slots_of_rows[:, None] == slot_range[None, :], rank[None, :], 0), axis=1
    )


def inner_scaled(adapter_sum, rank_of_row):
    mask_of_rank = jnp.arange(adapter_sum.shape[1])[None, :] < rank_of_row[:, None]
    row_factor = ADAPTER_SCALE * adapter_sum.shape[1] / rank_of_row.astype(jnp.float32)
    return jnp.where(mask_of_rank, adapter_sum * row_factor[:, None], 0.0).astype(jnp.bfloat16)


def grouping(group_ids, group_count):
    sort_order = jnp.argsort(group_ids, stable=True)
    group_range = jnp.arange(group_count, dtype=jnp.int32)
    group_sizes = jnp.sum((group_ids[:, None] == group_range[None, :]).astype(jnp.int32), axis=0)
    inverse_order = jnp.argsort(sort_order)
    return (sort_order, group_sizes, inverse_order)


def group_product(rows, factors, sort_order, group_sizes, inverse_order):
    result = lax.ragged_dot(
        jnp.take(rows, sort_order, axis=0), factors, group_sizes, preferred_element_type=jnp.float32
    )
    return jnp.take(result, inverse_order, axis=0)


def shards(
    queries,
    cached_key_rows,
    cached_value_rows,
    fresh_key_value,
    lengths,
    residual,
    output_weight,
    adapter_down,
    adapter_up,
    rank,
    requests,
    row_choice,
):
    query_block = lax.all_to_all(queries, "tp", split_axis=1, concat_axis=2, tiled=True)
    attended = attend(
        query_block[0], cached_key_rows[0], cached_value_rows[0], fresh_key_value[0], lengths[0]
    )
    attn_heads = lax.all_to_all(attended[None], "tp", split_axis=2, concat_axis=1, tiled=True)[0]
    head_column_span = attn_heads.shape[1]
    owned_count = adapter_down.shape[0]
    fetch_count = requests.shape[1]
    my_index = lax.axis_index("dp")
    fetch_range = jnp.arange(fetch_count, dtype=jnp.int32)
    picks_all, lists_all = (
        lax.all_gather(row_choice, "dp", axis=0, tiled=True),
        lax.all_gather(requests, "dp", axis=0, tiled=True),
    )
    attn_all = lax.all_gather(attn_heads[None], "dp", axis=0, tiled=True)
    block_count = attn_all.shape[0]
    rows_dp = attn_all.shape[1]
    flat_attn = attn_all.reshape(block_count * rows_dp, head_column_span)
    block_of = jnp.repeat(jnp.arange(block_count, dtype=jnp.int32), rows_dp)
    flat_picks = picks_all.reshape(block_count * rows_dp)
    fetch_hit = flat_picks[:, None] - owned_count == fetch_range[None, :]
    fetched_slot = jnp.sum(jnp.where(fetch_hit, lists_all[block_of], 0), axis=1)
    slots_of_rows = jnp.where(
        flat_picks < owned_count, block_of * owned_count + flat_picks, fetched_slot
    )
    shard_slot = slots_of_rows - my_index * owned_count
    owned = (shard_slot >= 0) & (shard_slot < owned_count)
    group_ids = jnp.where(owned, shard_slot, owned_count)
    pooled_down = jnp.concatenate(
        [adapter_down, jnp.zeros((1,) + adapter_down.shape[1:], adapter_down.dtype)], axis=0
    )
    pooled_up = jnp.concatenate(
        [adapter_up, jnp.zeros((1,) + adapter_up.shape[1:], adapter_up.dtype)], axis=0
    )
    sort_order, group_sizes, inverse_order = grouping(group_ids, owned_count + 1)
    inner_partial = group_product(flat_attn, pooled_down, sort_order, group_sizes, inverse_order)
    adapter_sum = lax.psum(inner_partial.astype(jnp.bfloat16), ("tp", "dp")).astype(jnp.float32)
    scaled_output = inner_scaled(adapter_sum, rank_lookup(slots_of_rows, rank))
    delta_all = group_product(scaled_output, pooled_up, sort_order, group_sizes, inverse_order)
    adapter_delta = lax.psum_scatter(
        delta_all.reshape(block_count, rows_dp, head_column_span).astype(jnp.bfloat16),
        "dp",
        scatter_dimension=0,
        tiled=True,
    ).astype(jnp.float32)[0]
    tp_index = lax.axis_index("tp")
    summed_shard = jnp.dot(attn_heads, output_weight, preferred_element_type=jnp.float32)
    owned_columns = (
        lax.dynamic_slice_in_dim(summed_shard, tp_index * head_column_span, head_column_span, 1)
        + adapter_delta
    )
    summed = lax.psum_scatter(
        lax.dynamic_update_slice_in_dim(
            summed_shard, owned_columns, tp_index * head_column_span, 1
        ).astype(jnp.bfloat16),
        "tp",
        scatter_dimension=0,
        tiled=True,
    ).astype(jnp.float32)
    return (residual[0].astype(jnp.float32) + summed).astype(jnp.bfloat16)[None]


def solution(mesh):
    return jax.shard_map(
        shards,
        mesh=mesh,
        in_specs=(
            P(("groups", "dp"), None, "tp"),
            P(("groups", "dp"), "tp", None, None),
            P(("groups", "dp"), "tp", None, None),
            P(("groups", "dp"), "tp", None, None),
            P(("groups", "dp"), "tp"),
            P(("groups", "dp"), "tp", None),
            P("tp", None),
            P("dp", "tp", None),
            P("dp", None, "tp"),
            P(),
            P(("groups", "dp"), None),
            P(("groups", "dp"), None),
        ),
        out_specs=P(("groups", "dp"), "tp", None),
        check_vma=False,
    )
```

profile of v0, /device:TPU:0, one launch (start us, length us, event | category | flops | bytes accessed | tf_op | source)
XLA Modules:
  0.0 485.2 jit_solution(3905374535573381241)
XLA Ops:
  9.4 5.2 %reduce.2 = bf16[384,1024]{1,0:T(8,128)(2,1)S(1)} reduce(bf16[384,1,1024]{2,1,0:T(2,128)(2,1)S(1)} %bitcast.84, bf16[]{:T(256)} %broadcast.133), dimensions={1}, to_apply=%bitcast.70.reduce_sub_computation | reduce | bytes 1572866
  16.1 7.6 %all-to-all-start = ((bf16[8,2,24576]{2,1,0:T(2,128)(2,1)}), bf16[8,2,24576]{2,1,0:T(2,128)(2,1)S(1)}, u32[]{:S(2)}, u32[]{:S(2)}) async-start(bf16[8,2,24576]{2,1,0:T(2,128)(2,1)} %reshape.208), calls=%async_computation | async-start | bytes 1572864 | tf_op jit(solution)/shard_map/all_to_all | solution.py:92
  23.7 7.3 %copy.59 = bf16[384,8,8,128]{3,2,1,0:T(8,128)(2,1)} copy(bf16[384,8,8,128]{3,1,2,0:T(8,128)(2,1)} %bitcast.77) | data formatting | bytes 12582912
  31.0 4.3 copy.60
  35.6 8.2 %all-to-all-done = bf16[8,2,24576]{2,1,0:T(2,128)(2,1)S(1)} async-done(((bf16[8,2,24576]{2,1,0:T(2,128)(2,1)}), bf16[8,2,24576]{2,1,0:T(2,128)(2,1)S(1)}, u32[]{:S(2)}, u32[]{:S(2)}) %all-to-all-start) | async-done | bytes 786464 | tf_op jit(solution)/shard_map/all_to_all | solution.py:92
  45.7 5.8 %fusion.20 = (f32[48,8,8]{2,1,0:T(8,128)S(1)}, f32[48,8,8,64]{3,2,1,0:T(8,128)S(1)}) fusion(bf16[48,64,8,128]{3,2,1,0:T(8,128)(2,1)} %bitcast.74, bf16[48,8,8,128]{3,2,0,1:T(8,128)(2,1)S(1)} %bitcast.88, pred[48,64]{1,0:T(8,128)(4,1)S(1)} %iota_compare_fusion.4), kind=kOutput, calls=%fused_computation.61 | convolution fusion | flops 50918400 | bytes 7879680 | tf_op jit(solution)/shard_map/rkgd,rjkd->rkgj/dot_general | solution.py:25
  55.4 6.8 %copy.49 = bf16[1,48,8192]{1,0,2:T(2,128)(2,1)} copy(bf16[1,48,8192]{2,1,0:T(8,128)(2,1)S(1)} %convert_element_type.78) | data formatting | bytes 1572864 | tf_op jit(solution)/shard_map/convert_element_type | solution.py:47
  62.2 45.4 %reduce.3 = bf16[8192,48]{1,0:T(8,128)(2,1)S(1)} reduce(bf16[8192,1,48]{2,1,0:T(2,128)(2,1)} %bitcast.75, bf16[]{:T(256)} %broadcast.133), dimensions={1}, to_apply=%bitcast.64.reduce_sub_computation | reduce | bytes 1572866
  107.6 4.0 reshape.210
  120.7 14.8 %all-to-all-done.1 = bf16[8,2,24576]{2,1,0:T(2,128)(2,1)S(1)} async-done(((bf16[8,2,24576]{2,1,0:T(2,128)(2,1)}), bf16[8,2,24576]{2,1,0:T(2,128)(2,1)S(1)}, u32[]{:S(2)}, u32[]{:S(2)}) %all-to-all-start.1) | async-done | bytes 786464 | tf_op jit(solution)/shard_map/all_to_all | solution.py:96
  135.5 5.4 %reshape.211 = bf16[8192,1,48]{2,1,0:T(2,128)(2,1)} reshape(bf16[8,2,24576]{2,1,0:T(2,128)(2,1)S(1)} %all-to-all-done.1) | data formatting | bytes 1572864
  140.8 8.1 %copy.50 = bf16[1,48,8192]{2,1,0:T(8,128)(2,1)S(1)} copy(bf16[1,48,8192]{1,0,2:T(2,128)(2,1)} %bitcast.76) | data formatting | bytes 1572864 | tf_op jit(solution)/shard_map/all_to_all | solution.py:96
  150.9 4.4 sort.34
  158.4 4.4 sort.35
  162.7 7.7 %concatenate.6 = bf16[33,1024,128]{2,1,0:T(8,128)(2,1)} pad(bf16[32,1024,128]{2,1,0:T(8,128)(2,1)} %param.19, bf16[]{:T(256)} %constant.84.clone.1), padding=0_1x0_0x0_0 | pad | bytes 17039362 | tf_op jit(solution)/shard_map/concatenate | solution.py:120
  170.6 5.7 %gather_fusion.1 = bf16[768,1024]{1,0:T(8,128)(2,1)S(1)} fusion(bf16[768,1024]{1,0:T(8,128)(2,1)} %bitcast.73, s32[1024]{0:T(1024)S(1)} %pad_clamp_fusion.1), kind=kCustom, calls=%fused_computation.1 | custom fusion | bytes 3148800 | tf_op jit(solution)/shard_map/jit(_take)/gather | solution.py:73
  177.7 25.9 %ragged-dot-none.1 = f32[768,128]{1,0:T(8,128)} custom-call(s32[1]{0:T(128)} %get-tuple-element.9, s32[34]{0:T(128)} %get-tuple-element.10, s32[35]{0:T(128)} %get-tuple-element.11, s32[35]{0:T(128)} %get-tuple-element.12, s32[1]{0:T(128)} %get-tuple-element.9, bf16[768,1024]{1,0:T(8,128)(2,1)} %broadcast_select_fusion, bf16[33,1024,128]{2,1,0:T(8,128)(2,1)} %concatenate.6), custom_call_target="tpu_custom_call" | custom-call | flops 201326592 | bytes 10616964 | tf_op jit(solution)/shard_map/ragged_dot_general/ragged-dot-none
  207.2 8.3 %concatenate.7 = bf16[33,128,1024]{2,1,0:T(8,128)(2,1)} pad(bf16[32,128,1024]{2,1,0:T(8,128)(2,1)} %param.20, bf16[]{:T(256)} %constant.84.clone.1), padding=0_1x0_0x0_0 | pad | bytes 17039362 | tf_op jit(solution)/shard_map/concatenate | solution.py:123
  215.5 79.6 %all-reduce.4.cloned.1.call-done = bf16[768,128]{1,0:T(8,128)(2,1)} async-done(((bf16[768,128]{1,0:T(8,128)(2,1)}), bf16[768,128]{1,0:T(8,128)(2,1)}) %all-reduce.4.cloned.1.call-update) | async-done | bytes 196624 | tf_op jit(solution)/shard_map/psum | solution.py:128
  299.0 25.9 %ragged-dot-none = f32[768,1024]{1,0:T(8,128)} custom-call(s32[1]{0:T(128)} %get-tuple-element.9, s32[34]{0:T(128)} %get-tuple-element.10, s32[35]{0:T(128)} %get-tuple-element.11, s32[35]{0:T(128)} %get-tuple-element.12, s32[1]{0:T(128)} %get-tuple-element.9, bf16[768,128]{1,0:T(8,128)(2,1)} %broadcast_select_fusion.1, bf16[33,128,1024]{2,1,0:T(8,128)(2,1)} %concatenate.7), custom_call_target="tpu_custom_call" | custom-call | flops 201326592 | bytes 11993220 | tf_op jit(solution)/shard_map/ragged_dot_general/ragged-dot-none
  324.9 5.7 %gather_fusion.4 = bf16[768,1024]{1,0:T(8,128)(2,1)S(1)} fusion(f32[768,1024]{1,0:T(8,128)} %ragged-dot-none, s32[1024]{0:T(1024)S(1)} %pad_clamp_fusion), kind=kCustom, calls=%fused_computation.4 | custom fusion | bytes 3148800 | tf_op jit(solution)/shard_map/jit(_take)/gather | solution.py:75
  333.2 15.6 %fusion.21 = f32[384,8192]{1,0:T(8,128)} fusion(bf16[384,1024]{1,0:T(8,128)(2,1)S(1)} %bitcast.91, bf16[1024,8192]{1,0:T(8,128)(2,1)} %param.18), kind=kOutput, calls=%fused_computation.63 | convolution fusion | flops 6442450944 | bytes 30146560 | tf_op jit(solution)/shard_map/dot_general | solution.py:138
  351.9 8.1 %convert_element_type.85 = bf16[384,8192]{1,0:T(8,128)(2,1)} convert(f32[384,8192]{1,0:T(8,128)} %fusion.4) | non-fusion elementwise | flops 3145728 | bytes 18874368 | tf_op jit(solution)/shard_map/convert_element_type | solution.py:146
  360.0 116.0 %reduce-scatter.5.cloned.1.call-done = bf16[48,8192]{1,0:T(8,128)(2,1)} async-done(((bf16[384,8192]{1,0:T(8,128)(2,1)}), bf16[48,8192]{1,0:T(8,128)(2,1)}) %reduce-scatter.5.cloned.1.call-update) | async-done | bytes 786448 | tf_op jit(solution)/shard_map/reduce_scatter | solution.py:143
  (88 shorter events, 41.3 us)
Async XLA Ops:
  16.1 14.9 %slice-start = ((s8[6291456]{0:T(1024)(128)(4,1)}), s8[2097152]{0:T(1024)(128)(4,1)S(1)}, s32[]{:S(2)}) async-start(s8[6291456]{0:T(1024)(128)(4,1)} %bitcast.78), calls=%async_computation.8 | async-start | bytes 4194304
  16.1 27.7 %all-to-all-start = ((bf16[8,2,24576]{2,1,0:T(2,128)(2,1)}), bf16[8,2,24576]{2,1,0:T(2,128)(2,1)S(1)}, u32[]{:S(2)}, u32[]{:S(2)}) async-start(bf16[8,2,24576]{2,1,0:T(2,128)(2,1)} %reshape.208), calls=%async_computation | async-start | bytes 1572864 | tf_op jit(solution)/shard_map/all_to_all | solution.py:92
  23.7 7.3 %slice-start.1 = ((s8[6291456]{0:T(1024)(128)(4,1)}), s8[4194304]{0:T(1024)(128)(4,1)S(1)}, s32[]{:S(2)}) async-start(s8[6291456]{0:T(1024)(128)(4,1)} %bitcast.78), calls=%async_computation.9 | async-start | bytes 8388608
  31.0 4.3 copy-start.5
  31.0 4.4 copy-start.2
  45.1 7.5 %slice-start.2 = ((s8[6291456]{0:T(1024)(128)(4,1)}), s8[4194304]{0:T(1024)(128)(4,1)S(1)}, s32[]{:S(2)}) async-start(s8[6291456]{0:T(1024)(128)(4,1)} %bitcast.81), calls=%async_computation.10 | async-start | bytes 8388608
  45.7 6.9 %slice-start.3 = ((s8[6291456]{0:T(1024)(128)(4,1)}), s8[2097152]{0:T(1024)(128)(4,1)S(1)}, s32[]{:S(2)}) async-start(s8[6291456]{0:T(1024)(128)(4,1)} %bitcast.81), calls=%async_computation.11 | async-start | bytes 4194304
  107.5 7.6 %copy-start.6 = (s32[1,16]{1,0:T(1,128)S(1)}, s32[1,16]{1,0:T(1,128)}, u32[]{:S(2)}) copy-start(s32[1,16]{1,0:T(1,128)} %param.22) | copy-start | bytes 196
  107.6 9.4 %copy-start.3 = (s32[1,384]{1,0:T(1,128)S(1)}, s32[1,384]{1,0:T(1,128)}, u32[]{:S(2)}) copy-start(s32[1,384]{1,0:T(1,128)} %param.23) | copy-start | bytes 4612
  111.5 23.9 %all-to-all-start.1 = ((bf16[8,2,24576]{2,1,0:T(2,128)(2,1)}), bf16[8,2,24576]{2,1,0:T(2,128)(2,1)S(1)}, u32[]{:S(2)}, u32[]{:S(2)}) async-start(bf16[8,2,24576]{2,1,0:T(2,128)(2,1)} %reshape.210), calls=%async_computation.1 | async-start | bytes 1572864 | tf_op jit(solution)/shard_map/all_to_all | solution.py:96
  115.1 55.5 %all-gather.4.cloned.1.call-start = ((), (), s32[]{:S(2)}) async-start(), calls=%async_computation.4 | async-start | bytes 2359296 | tf_op jit(solution)/shard_map/all_gather | solution.py:106
  150.8 144.2 %all-reduce.4.cloned.1.call-start = ((), (), s32[]{:S(2)}) async-start(), calls=%async_computation.5 | async-start | bytes 393216 | tf_op jit(solution)/shard_map/psum | solution.py:128
  162.7 7.7 %copy-start.4 = (s32[64]{0:T(128)S(1)}, s32[64]{0:T(128)}, u32[]{:S(2)}) copy-start(s32[64]{0:T(128)} %param.21) | copy-start | bytes 772
  207.1 141.7 %reduce-scatter.3.cloned.1.call-start = ((), (), s32[]{:S(2)}) async-start(), calls=%async_computation.6 | async-start | bytes 2359296 | tf_op jit(solution)/shard_map/reduce_scatter | solution.py:131
  332.1 1.1 copy-start
  332.1 143.9 %reduce-scatter.5.cloned.1.call-start = ((), (), s32[]{:S(2)}) async-start(), calls=%async_computation.7 | async-start | bytes 7077888 | tf_op jit(solution)/shard_map/reduce_scatter | solution.py:143
  360.0 116.0 %copy-start.1 = (bf16[1,48,8192]{2,1,0:T(8,128)(2,1)S(1)}, bf16[1,48,8192]{2,1,0:T(8,128)(2,1)}, u32[]{:S(2)}) copy-start(bf16[1,48,8192]{2,1,0:T(8,128)(2,1)} %param.17) | copy-start | bytes 2359300
Sparse Core Ops, SparseCore 0:
  150.9 9.4 all-gather.3
  207.2 87.7 all-reduce.3
  332.3 7.2 reduce-scatter.2
  360.1 115.8 reduce-scatter.4
where the time goes:
time: 492 us; the launch traced here: 485 us
  waiting for transfers between devices  219 us (45%)
  other arithmetic  81 us (16%)
  local copies, waits for them, and re-layouts  78.1 us (16%)
  Pallas kernels  54.2 us (11%)
  matrix products  24.4 us (5%)
  between operations  14 us (3%)
  starting transfers between devices  11.3 us (2%)
    reduce_scatter x1, waiting for transfers between devices, shards(): lax.psum_scatter(lax.dynamic_update_slice_in_dim(summed_shard, owned_colu...  116 us
    psum x1, waiting for transfers between devices, shards(): lax.psum(inner_partial.astype(jnp.bfloat16), ('tp', 'dp'))  79.6 us
    another operation x2, Pallas kernels  51.8 us
    unnamed x4, other arithmetic  50.6 us
    unnamed x35, local copies, waits for them, and re-layouts  28 us
    dot_general x1, matrix products, shards(): jnp.dot(attn_heads, output_weight, preferred_element_type=jnp.float32)  15.6 us
    all_to_all x1, waiting for transfers between devices, shards(): lax.all_to_all(attended[None], 'tp', split_axis=2, concat_axis=1, tiled=T...  14.8 us
  transfers between devices with their start and end apart: 6, of which 4 were waited for; matrix products, arithmetic and copies ran while one was open for 11% of the time, Pallas kernels for 0%

commit v1 on v0

v1 whole, which is shorter than its diff:
```python
import functools

import jax
import jax.numpy as jnp
from jax import lax
from jax.experimental import pallas as pl
from jax.experimental.pallas import tpu as pltpu
from jax.sharding import PartitionSpec as P

HEADS = 64
KV_HEADS = 8
HEAD_DIM = 128
ADAPTER_SCALE = 0.25
BF16 = jnp.bfloat16
F32 = jnp.float32
ROW_BLOCK = 16
SUB = 8
VMEM_LIMIT = 48 * 1024 * 1024


def permute_xor(x, axis, size, k):
    return lax.ppermute(x, axis, [(i, i ^ k) for i in range(size)])


def attend_kernel(n, me_ref, q_ref, k_ref, v_ref, fk_ref, fv_ref, len_ref, o_ref):
    me = me_ref[0]
    groups = HEADS // KV_HEADS
    per_src = HEADS // n
    positions = k_ref.shape[1]
    lanes = 2 * positions
    tiles = SUB // 2
    rows = groups * SUB
    row_of = lax.broadcasted_iota(jnp.int32, (rows, lanes), 0) % SUB
    lane_of = lax.broadcasted_iota(jnp.int32, (rows, lanes), 1)
    in_row = (row_of % 2) == (lane_of // positions)
    tile_of = row_of // 2
    scale = HEAD_DIM ** (-0.5)
    for c in range(KV_HEADS):
        span = slice(c * HEAD_DIM, (c + 1) * HEAD_DIM)
        heads = [c * groups + h for h in range(groups)]
        q_heads = [
            q_ref[(h // per_src) ^ me, :, (h % per_src) * HEAD_DIM : (h % per_src + 1) * HEAD_DIM].astype(F32)
            for h in heads
        ]
        outs = []
        for s in range(ROW_BLOCK // SUB):
            part = slice(s * SUB, (s + 1) * SUB)
            q_f32 = jnp.concatenate([q[part] for q in q_heads], axis=0)
            keys = k_ref[part, :, span].reshape(SUB * positions, HEAD_DIM)
            values = v_ref[part, :, span].reshape(SUB * positions, HEAD_DIM)
            full = lax.dot_general(
                q_f32.astype(BF16), keys, (((1,), (1,)), ((), ())), preferred_element_type=F32
            )
            score = full[:, :lanes]
            for k in range(1, tiles):
                score = jnp.where(tile_of == k, full[:, k * lanes : (k + 1) * lanes], score)
            live = in_row & ((lane_of % positions) < jnp.tile(len_ref[part], (groups, 1)))
            score = jnp.where(live, score * scale, -1e30)
            fresh_key = jnp.tile(fk_ref[:, span].astype(F32)[part], (groups, 1))
            fresh_value = jnp.tile(fv_ref[:, span].astype(F32)[part], (groups, 1))
            own = jnp.sum(q_f32 * fresh_key, axis=1, keepdims=True) * scale
            peak = jnp.maximum(jnp.max(score, axis=1, keepdims=True), own)
            weight = jnp.where(live, jnp.exp(score - peak), 0.0)
            own_weight = jnp.exp(own - peak)
            total = jnp.sum(weight, axis=1, keepdims=True) + own_weight
            prob = weight / total
            prob_new = (own_weight / total).astype(BF16).astype(F32)
            wide = jnp.concatenate([jnp.where(tile_of == k, prob, 0.0) for k in range(tiles)], axis=1).astype(BF16)
            outs.append(jnp.dot(wide, values, preferred_element_type=F32) + prob_new * fresh_value)
        for i, h in enumerate(heads):
            block = jnp.concatenate([o[i * SUB : (i + 1) * SUB] for o in outs], axis=0).astype(BF16)
            o_ref[(h // per_src) ^ me, :, (h % per_src) * HEAD_DIM : (h % per_src + 1) * HEAD_DIM] = block


def attend(me, q, keys, values, fresh_key, fresh_value, lengths):
    n, rows, width = q.shape
    kv = keys.shape[2]
    positions = keys.shape[1]
    return pl.pallas_call(
        functools.partial(attend_kernel, n),
        grid_spec=pltpu.PrefetchScalarGridSpec(
            num_scalar_prefetch=1,
            grid=(rows // ROW_BLOCK,),
            in_specs=[
                pl.BlockSpec((n, ROW_BLOCK, width), lambda i, me: (0, i, 0)),
                pl.BlockSpec((ROW_BLOCK, positions, kv), lambda i, me: (i, 0, 0)),
                pl.BlockSpec((ROW_BLOCK, positions, kv), lambda i, me: (i, 0, 0)),
                pl.BlockSpec((ROW_BLOCK, kv), lambda i, me: (i, 0)),
                pl.BlockSpec((ROW_BLOCK, kv), lambda i, me: (i, 0)),
                pl.BlockSpec((ROW_BLOCK, 1), lambda i, me: (i, 0)),
            ],
            out_specs=pl.BlockSpec((n, ROW_BLOCK, width), lambda i, me: (0, i, 0)),
        ),
        out_shape=jax.ShapeDtypeStruct((n, rows, width), BF16),
        compiler_params=pltpu.CompilerParams(vmem_limit_bytes=VMEM_LIMIT),
        cost_estimate=pl.CostEstimate(
            flops=4 * rows * SUB * HEADS * HEAD_DIM * positions,
            bytes_accessed=4 * rows * positions * kv,
            transcendentals=rows * HEADS * positions,
        ),
        name="attend",
    )(me, q, keys, values, fresh_key, fresh_value, lengths)


def inner_kernel(per, a_ref, b_ref, ia_ref, ib_ref, down_ref, oa_ref, ob_ref, acc_a, acc_b):
    step = pl.program_id(0)

    @pl.when(step == 0)
    def _():
        acc_a[...] = jnp.zeros_like(acc_a)
        acc_b[...] = jnp.zeros_like(acc_b)

    rank = down_ref.shape[2]
    wide = jnp.concatenate([down_ref[i] for i in range(per)], axis=1)
    for x_ref, id_ref, acc in ((a_ref, ia_ref, acc_a), (b_ref, ib_ref, acc_b)):
        product = jnp.dot(x_ref[...], wide, preferred_element_type=F32)
        total = acc[...]
        for i in range(per):
            total = jnp.where(id_ref[...] == step * per + i, product[:, i * rank : (i + 1) * rank], total)
        acc[...] = total

    @pl.when(step == pl.num_programs(0) - 1)
    def _():
        oa_ref[...] = acc_a[...].astype(BF16)
        ob_ref[...] = acc_b[...].astype(BF16)


def inner_products(rows_a, rows_b, ids_a, ids_b, down):
    rows, width = rows_a.shape
    owned, _, rank = down.shape
    per = 2
    whole = lambda shape: pl.BlockSpec(shape, lambda i: (0, 0))
    return pl.pallas_call(
        functools.partial(inner_kernel, per),
        grid=(owned // per,),
        in_specs=[
            whole((rows, width)),
            whole((rows, width)),
            whole((rows, 1)),
            whole((rows, 1)),
            pl.BlockSpec((per, width, rank), lambda i: (i, 0, 0)),
        ],
        out_specs=[whole((rows, rank)), whole((rows, rank))],
        out_shape=[jax.ShapeDtypeStruct((rows, rank), BF16)] * 2,
        scratch_shapes=[pltpu.VMEM((rows, rank), F32)] * 2,
        compiler_params=pltpu.CompilerParams(vmem_limit_bytes=VMEM_LIMIT),
        cost_estimate=pl.CostEstimate(
            flops=4 * rows * width * rank * owned, bytes_accessed=2 * owned * width * rank, transcendentals=0
        ),
        name="inner_products",
    )(rows_a, rows_b, ids_a, ids_b, down)


def delta_kernel(per, a_ref, b_ref, ia_ref, ib_ref, up_ref, oa_ref, ob_ref, acc_a, acc_b):
    step = pl.program_id(0)

    @pl.when(step == 0)
    def _():
        acc_a[...] = jnp.zeros_like(acc_a)
        acc_b[...] = jnp.zeros_like(acc_b)

    rank, width = up_ref.shape[1:]
    up = up_ref[...].reshape(per * rank, width)
    for x_ref, id_ref, acc in ((a_ref, ia_ref, acc_a), (b_ref, ib_ref, acc_b)):
        x = x_ref[...]
        ids = id_ref[...]
        wide = jnp.concatenate(
            [jnp.where(ids == step * per + i, x, jnp.zeros_like(x)) for i in range(per)], axis=1
        ).astype(BF16)
        acc[...] += jnp.dot(wide, up, preferred_element_type=F32)

    @pl.when(step == pl.num_programs(0) - 1)
    def _():
        oa_ref[...] = acc_a[...].astype(BF16)
        ob_ref[...] = acc_b[...].astype(BF16)


def adapter_outputs(scaled_a, scaled_b, ids_a, ids_b, up):
    rows, rank = scaled_a.shape
    owned, _, width = up.shape
    per = 8
    whole = lambda shape: pl.BlockSpec(shape, lambda i: (0, 0))
    return pl.pallas_call(
        functools.partial(delta_kernel, per),
        grid=(owned // per,),
        in_specs=[
            whole((rows, rank)),
            whole((rows, rank)),
            whole((rows, 1)),
            whole((rows, 1)),
            pl.BlockSpec((per, rank, width), lambda i: (i, 0, 0)),
        ],
        out_specs=[whole((rows, width)), whole((rows, width))],
        out_shape=[jax.ShapeDtypeStruct((rows, width), BF16)] * 2,
        scratch_shapes=[pltpu.VMEM((rows, width), F32)] * 2,
        compiler_params=pltpu.CompilerParams(vmem_limit_bytes=VMEM_LIMIT),
        cost_estimate=pl.CostEstimate(
            flops=4 * rows * width * rank * owned, bytes_accessed=2 * owned * width * rank, transcendentals=0
        ),
        name="adapter_outputs",
    )(scaled_a, scaled_b, ids_a, ids_b, up)


def project_kernel(with_delta, half, where_ref, x_ref, w_ref, *refs):
    if with_delta:
        d_ref, near_ref, far_ref = refs
    else:
        near_ref, far_ref = refs
    result = jnp.dot(x_ref[...], w_ref[...], preferred_element_type=F32)
    if with_delta:
        result = result + jnp.where(where_ref[1] == 1, d_ref[...].astype(F32), 0.0)
    near_ref[...] = result[:half].astype(BF16)
    far_ref[...] = result[half:].astype(BF16)


def project(where, x, weight, width, delta=None):
    rows, depth = x.shape
    half = rows // 2
    tile = min(256, width)
    per = width // tile
    ins = [
        pl.BlockSpec((rows, depth), lambda i, w: (0, 0)),
        pl.BlockSpec((depth, tile), lambda i, w: (0, w[0] * per + i)),
    ]
    args = [x, weight]
    if delta is not None:
        ins.append(pl.BlockSpec((rows, tile), lambda i, w: (0, i)))
        args.append(delta)
    return pl.pallas_call(
        functools.partial(project_kernel, delta is not None, half),
        grid_spec=pltpu.PrefetchScalarGridSpec(
            num_scalar_prefetch=1,
            grid=(per,),
            in_specs=ins,
            out_specs=[pl.BlockSpec((half, tile), lambda i, w: (0, i))] * 2,
        ),
        out_shape=[jax.ShapeDtypeStruct((half, width), BF16)] * 2,
        compiler_params=pltpu.CompilerParams(vmem_limit_bytes=VMEM_LIMIT),
        cost_estimate=pl.CostEstimate(
            flops=2 * rows * depth * width, bytes_accessed=2 * depth * width, transcendentals=0
        ),
        name="project",
    )(where, *args)


def finish_kernel(terms, width, order_ref, res_ref, *refs):
    o_ref = refs[-1]
    count = (len(refs) - 1) // terms
    for i in range(count):
        place = pl.ds(pl.multiple_of(order_ref[i] * width, width), width)
        total = refs[i * terms][...].astype(F32)
        for j in range(1, terms):
            total = total + refs[i * terms + j][...].astype(F32)
        o_ref[:, place] = (res_ref[:, place].astype(F32) + total).astype(BF16)


def finish(order, residual, columns):
    rows, features = residual.shape
    terms = len(columns[0])
    width = columns[0][0].shape[1]
    flat = [x for group in columns for x in group]
    vmem = pl.BlockSpec(memory_space=pltpu.VMEM)
    return pl.pallas_call(
        functools.partial(finish_kernel, terms, width),
        in_specs=[pl.BlockSpec(memory_space=pltpu.SMEM), vmem] + [vmem] * len(flat),
        out_specs=vmem,
        out_shape=jax.ShapeDtypeStruct((rows, features), BF16),
        compiler_params=pltpu.CompilerParams(vmem_limit_bytes=VMEM_LIMIT),
        cost_estimate=pl.CostEstimate(
            flops=terms * rows * features, bytes_accessed=2 * (terms + 2) * rows * features, transcendentals=0
        ),
        name="finish",
    )(order, residual, *flat)


def shards(
    n,
    n_dp,
    queries,
    cached_key_rows,
    cached_value_rows,
    fresh_key_value,
    lengths,
    residual,
    output_weight,
    adapter_down,
    adapter_up,
    rank,
    requests,
    row_choice,
):
    nz = n // 2
    me = lax.axis_index("tp").astype(jnp.int32)
    dp = lax.axis_index("dp").astype(jnp.int32)
    z, y = me // 2, me % 2
    rows_dp = queries.shape[1]
    rows = rows_dp // n
    width = queries.shape[2]
    pool_rank = adapter_down.shape[2]
    owned = adapter_down.shape[0]
    fetch = requests.shape[1]
    order = [k for k in range(n) if k % 2 == 0] + [k for k in range(n) if k % 2 == 1]

    q_blocks = queries[0].reshape(n, rows, width)
    q_parts = []
    for k in range(n):
        block = lax.dynamic_index_in_dim(q_blocks, me ^ k, 0, keepdims=False)
        q_parts.append(block if k == 0 else permute_xor(block, "tp", n, k))
    q = jnp.stack(q_parts)
    attended = attend(
        me[None],
        q,
        cached_key_rows[0],
        cached_value_rows[0],
        fresh_key_value[0, :, 0],
        fresh_key_value[0, :, 1],
        lengths[0][:, None],
    )

    choice = row_choice[0].reshape(n, rows)
    choice = jnp.concatenate([lax.dynamic_index_in_dim(choice, me ^ k, 0, keepdims=False) for k in order])
    lists = requests[0]
    sides = []
    for side in range(2):
        if side == 1:
            choice = permute_xor(choice, "dp", n_dp, 1)
            lists = permute_xor(lists, "dp", n_dp, 1)
        hit = choice[:, None] - owned == jnp.arange(fetch, dtype=jnp.int32)[None, :]
        fetched = jnp.sum(jnp.where(hit, lists[None, :], 0), axis=1)
        slot = jnp.where(choice < owned, (dp ^ side) * owned + choice, fetched)
        local = slot - dp * owned
        mine = (local >= 0) & (local < owned)
        pool = jnp.arange(rank.shape[0], dtype=jnp.int32)
        row_rank = jnp.sum(jnp.where(slot[:, None] == pool[None, :], rank[None, :], 0), axis=1)
        factor = jnp.where(
            (jnp.arange(pool_rank)[None, :] < row_rank[:, None]) & mine[:, None],
            (ADAPTER_SCALE * pool_rank / row_rank.astype(F32))[:, None],
            0.0,
        )
        sides.append((local[:, None], factor))
    (ids_a, factor_a), (ids_b, factor_b) = sides

    x = jnp.concatenate(
        [attended[0] if k == 0 else permute_xor(attended[k], "tp", n, k) for k in order], axis=0
    )
    x_other = permute_xor(x, "dp", n_dp, 1)

    inner_a, inner_b = inner_products(x, x_other, ids_a, ids_b, adapter_down)
    inner = inner_a.astype(F32) + permute_xor(inner_b, "dp", n_dp, 1).astype(F32)
    step = 1
    while step < n:
        part = permute_xor(inner.astype(BF16), "tp", n, step).reshape(n, rows, pool_rank)
        part = jnp.concatenate([part[order.index(k ^ step)] for k in order], axis=0)
        inner = inner + part.astype(F32)
        step *= 2
    inner_other = permute_xor(inner.astype(BF16), "dp", n_dp, 1).astype(F32)
    delta_a, delta_b = adapter_outputs(
        (inner * factor_a).astype(BF16), (inner_other * factor_b).astype(BF16), ids_a, ids_b, adapter_up
    )
    delta = (delta_a.astype(F32) + permute_xor(delta_b, "dp", n_dp, 1).astype(F32)).astype(BF16)

    mine_sums, received = {}, {}
    for jz in reversed(range(nz)):
        for b in range(2):
            place = (z ^ jz) * 2 + b
            flag = (y == b).astype(jnp.int32)
            near, far = project(
                jnp.stack([place, flag]), x, output_weight, width, delta if jz == 0 else None
            )
            far = permute_xor(far, "tp", n, 1)
            total = (near.astype(F32) + far.astype(F32)).astype(BF16).reshape(nz, rows, width)
            mine_sums[jz, b] = total[0]
            for j in range(1, nz):
                received[j, jz, b] = permute_xor(total[j], "tp", n, 2 * j)
    columns, places = [], []
    for jz in range(nz):
        for b in range(2):
            places.append((z ^ jz) * 2 + b)
            columns.append([mine_sums[jz, b]] + [received[j, jz ^ j, b] for j in range(1, nz)])
    return finish(jnp.stack(places), residual[0], columns)[None]


def solution(mesh):
    return jax.shard_map(
        functools.partial(shards, mesh.shape["tp"], mesh.shape["dp"]),
        mesh=mesh,
        in_specs=(
            P(("groups", "dp"), None, "tp"),
            P(("groups", "dp"), "tp", None, None),
            P(("groups", "dp"), "tp", None, None),
            P(("groups", "dp"), "tp", None, None),
            P(("groups", "dp"), "tp"),
            P(("groups", "dp"), "tp", None),
            P("tp", None),
            P("dp", "tp", None),
            P("dp", None, "tp"),
            P(),
            P(("groups", "dp"), None),
            P(("groups", "dp"), None),
        ),
        out_specs=P(("groups", "dp"), "tp", None),
        check_vma=False,
    )
```

time: 492 us -> 241 us (0.49); the launches traced: 485 us -> 240 us
  waiting for transfers between devices: 219 us -> 69.6 us
  other arithmetic: 81 us -> 4.7 us
  starting transfers between devices: 11.3 us -> 83.5 us
  local copies, waits for them, and re-layouts: 78.1 us -> 6.1 us
  matrix products: 24.4 us -> 0 us
  Pallas kernels: 54.2 us -> 75.9 us
  between operations: 14 us -> 0.61 us
    reduce_scatter x2 -> x0, waiting for transfers between devices: 116 us -> none  [the longest x1 116 us: shards(): lax.psum_scatter(lax.dynamic_update_slice_in_dim(summed_shard, owned_colu...]
    ppermute x0 -> x55, starting transfers between devices: none -> 83.5 us  [permute_xor(): return lax.ppermute(x, axis, [(i, i ^ k) for i in range(size)])]
    psum x1 -> x0, waiting for transfers between devices: 79.6 us -> none  [shards(): lax.psum(inner_partial.astype(jnp.bfloat16), ('tp', 'dp'))]
    pallas_call x0 -> x12, Pallas kernels: none -> 75.9 us  [the longest x8 31.2 us: project(): pl.pallas_call(functools.partial(project_kernel, delta is not None, half)...]
    ppermute x0 -> x55, waiting for transfers between devices: none -> 69.6 us  [permute_xor(): return lax.ppermute(x, axis, [(i, i ^ k) for i in range(size)])]
    another operation x2 -> x0, Pallas kernels: 51.8 us -> none
    unnamed x4 -> x1, other arithmetic: 50.6 us -> 0.7 us
    unnamed x35 -> x22, local copies, waits for them, and re-layouts: 28 us -> 0.17 us
  transfers between devices with their start and end apart: 6 -> 55, of which waited for: 4 -> 19; matrix products, arithmetic and copies ran while one was open for 11% -> 4% of each run, Pallas kernels for 0% -> 23%
where the time goes in v1:
time: 241 us; the launch traced here: 240 us
  starting transfers between devices  83.5 us (35%)
  Pallas kernels  75.9 us (31%)
  waiting for transfers between devices  69.6 us (29%)
  local copies, waits for them, and re-layouts  6.1 us (3%)
  other arithmetic  4.7 us (2%)
    ppermute x55, starting transfers between devices, permute_xor(): return lax.ppermute(x, axis, [(i, i ^ k) for i in range(size)])  83.5 us
    ppermute x55, waiting for transfers between devices, permute_xor(): return lax.ppermute(x, axis, [(i, i ^ k) for i in range(size)])  69.6 us
    pallas_call x8, Pallas kernels, project(): pl.pallas_call(functools.partial(project_kernel, delta is not None, half)...  31.2 us
    pallas_call x1, Pallas kernels, attend(): pl.pallas_call(functools.partial(attend_kernel, n), grid_spec=pltpu.Prefe...  18.6 us
    pallas_call x1, Pallas kernels, inner_products(): pl.pallas_call(functools.partial(inner_kernel, per), grid=(owned // per,)...  14.1 us
    pallas_call x1, Pallas kernels, adapter_outputs(): pl.pallas_call(functools.partial(delta_kernel, per), grid=(owned // per,)...  9.44 us
  transfers between devices with their start and end apart: 55, of which 19 were waited for; matrix products, arithmetic and copies ran while one was open for 4% of the time, Pallas kernels for 23%

profile of v1, /device:TPU:0, one launch (start us, length us, event | category | flops | bytes accessed | tf_op | source)
XLA Modules:
  0.0 240.3 jit_solution(1908865089789343184)
XLA Ops:
  20.1 5.0 %collective-permute-done.3 = bf16[48,1024]{1,0:T(8,128)(2,1)S(1)} collective-permute-done((bf16[48,1024]{1,0:T(8,128)(2,1)S(1)}, bf16[48,1024]{1,0:T(8,128)(2,1)S(1)}, u32[]{:S(2)}, u32[]{:S(2)}) %collective-permute-start.3) | collective-permute-done | bytes 98336 | tf_op jit(solution)/shard_map/ppermute | solution.py:22
  25.1 4.5 %collective-permute-done.4 = bf16[48,1024]{1,0:T(8,128)(2,1)S(1)} collective-permute-done((bf16[48,1024]{1,0:T(8,128)(2,1)S(1)}, bf16[48,1024]{1,0:T(8,128)(2,1)S(1)}, u32[]{:S(2)}, u32[]{:S(2)}) %collective-permute-start.4) | collective-permute-done | bytes 98336 | tf_op jit(solution)/shard_map/ppermute | solution.py:22
  29.7 18.6 %attend.1 = bf16[8,48,1024]{2,1,0:T(8,128)(2,1)S(1)} custom-call(s32[1]{0:T(128)} %bitcast.10.me_ref, bf16[8,48,1024]{2,1,0:T(8,128)(2,1)S(1)} %bitcast_dynamic-update-slice_fusion.q_ref, bf16[48,64,1024]{2,1,0:T(8,128)(2,1)} %bitcast.101, bf16[48,64,1024]{2,1,0:T(8,128)(2,1)} %bitcast.102, bf16[48,1024]{1,0:T(8,128)(2,1)S(1)} %get-tuple-element.134.fk_ref, ...), custom_call_target="tpu_custom_call" | custom-call | flops 805306368 | bytes 12582912 | tf_op jit(solution)/shard_map/attend/pallas_call | solution.py:79
  48.3 3.9 %collective-permute-start.7 = (bf16[48,1024]{1,0:T(8,128)(2,1)S(1)}, bf16[48,1024]{1,0:T(8,128)(2,1)S(1)}, u32[]{:S(2)}, u32[]{:S(2)}) collective-permute-start(bf16[48,1024]{1,0:T(8,128)(2,1)S(1)} %get-tuple-element.58), channel_id=1, source_target_pairs={{0,4},{2,6},{4,0},{6,2},{8,12},{10,14},{12,8},{14,10},{1,5},{3,7},... | collective-permute-start | bytes 294920 | tf_op jit(solution)/shard_map/ppermute | solution.py:22
  60.2 5.9 %collective-permute-start.13 = (bf16[48,1024]{1,0:T(8,128)(2,1)S(1)}, bf16[48,1024]{1,0:T(8,128)(2,1)S(1)}, u32[]{:S(2)}, u32[]{:S(2)}) collective-permute-start(bf16[48,1024]{1,0:T(8,128)(2,1)S(1)} %get-tuple-element.52), channel_id=1, source_target_pairs={{0,14},{2,12},{4,10},{6,8},{8,6},{10,4},{12,2},{14,0},{1,15},{3,13... | collective-permute-start | bytes 294920 | tf_op jit(solution)/shard_map/ppermute | solution.py:22
  66.2 4.9 %collective-permute-done.12 = bf16[48,1024]{1,0:T(8,128)(2,1)S(1)} collective-permute-done((bf16[48,1024]{1,0:T(8,128)(2,1)S(1)}, bf16[48,1024]{1,0:T(8,128)(2,1)S(1)}, u32[]{:S(2)}, u32[]{:S(2)}) %collective-permute-start.12) | collective-permute-done | bytes 98336 | tf_op jit(solution)/shard_map/ppermute | solution.py:22
  71.2 3.9 %project.9 = (bf16[192,1024]{1,0:T(8,128)(2,1)S(1)}, bf16[192,1024]{1,0:T(8,128)(2,1)S(1)}) custom-call(s32[2]{0:T(128)S(1)} %get-tuple-element.127.where_ref, bf16[384,1024]{1,0:T(8,128)(2,1)S(1)} %constant_dynamic-update-slice_fusion.a_ref.x_ref, bf16[1024,8192]{1,0:T(8,128)(2,1)} %w_ref.15), custom_call_target="tpu_custom_call" | custom-call | flops 805306368 | bytes 2097152 | tf_op jit(solution)/shard_map/project/pallas_call | solution.py:229
  76.8 3.9 %project.10 = (bf16[192,1024]{1,0:T(8,128)(2,1)S(1)}, bf16[192,1024]{1,0:T(8,128)(2,1)S(1)}) custom-call(s32[2]{0:T(128)S(1)} %get-tuple-element.128.where_ref, bf16[384,1024]{1,0:T(8,128)(2,1)S(1)} %constant_dynamic-update-slice_fusion.a_ref.x_ref, bf16[1024,8192]{1,0:T(8,128)(2,1)} %w_ref.15), custom_call_target="tpu_custom_call" | custom-call | flops 805306368 | bytes 2097152 | tf_op jit(solution)/shard_map/project/pallas_call | solution.py:229
  81.2 3.9 %project.11 = (bf16[192,1024]{1,0:T(8,128)(2,1)S(1)}, bf16[192,1024]{1,0:T(8,128)(2,1)S(1)}) custom-call(s32[2]{0:T(128)S(1)} %get-tuple-element.129.where_ref, bf16[384,1024]{1,0:T(8,128)(2,1)S(1)} %constant_dynamic-update-slice_fusion.a_ref.x_ref, bf16[1024,8192]{1,0:T(8,128)(2,1)} %w_ref.15), custom_call_target="tpu_custom_call" | custom-call | flops 805306368 | bytes 2097152 | tf_op jit(solution)/shard_map/project/pallas_call | solution.py:229
  86.7 3.9 %project.13 = (bf16[192,1024]{1,0:T(8,128)(2,1)S(1)}, bf16[192,1024]{1,0:T(8,128)(2,1)S(1)}) custom-call(s32[2]{0:T(128)S(1)} %get-tuple-element.130.where_ref, bf16[384,1024]{1,0:T(8,128)(2,1)S(1)} %constant_dynamic-update-slice_fusion.a_ref.x_ref, bf16[1024,8192]{1,0:T(8,128)(2,1)} %w_ref.15), custom_call_target="tpu_custom_call" | custom-call | flops 805306368 | bytes 2097152 | tf_op jit(solution)/shard_map/project/pallas_call | solution.py:229
  91.2 3.9 %project.14 = (bf16[192,1024]{1,0:T(8,128)(2,1)S(1)}, bf16[192,1024]{1,0:T(8,128)(2,1)S(1)}) custom-call(s32[2]{0:T(128)S(1)} %get-tuple-element.131.where_ref, bf16[384,1024]{1,0:T(8,128)(2,1)S(1)} %constant_dynamic-update-slice_fusion.a_ref.x_ref, bf16[1024,8192]{1,0:T(8,128)(2,1)} %w_ref.15), custom_call_target="tpu_custom_call" | custom-call | flops 805306368 | bytes 2097152 | tf_op jit(solution)/shard_map/project/pallas_call | solution.py:229
  95.0 3.9 %project.15 = (bf16[192,1024]{1,0:T(8,128)(2,1)S(1)}, bf16[192,1024]{1,0:T(8,128)(2,1)S(1)}) custom-call(s32[2]{0:T(128)S(1)} %get-tuple-element.132.where_ref, bf16[384,1024]{1,0:T(8,128)(2,1)S(1)} %constant_dynamic-update-slice_fusion.a_ref.x_ref, bf16[1024,8192]{1,0:T(8,128)(2,1)} %w_ref.15), custom_call_target="tpu_custom_call" | custom-call | flops 805306368 | bytes 2097152 | tf_op jit(solution)/shard_map/project/pallas_call | solution.py:229
  101.2 14.1 %inner_products.1 = (bf16[384,128]{1,0:T(8,128)(2,1)S(1)}, bf16[384,128]{1,0:T(8,128)(2,1)S(1)}) custom-call(bf16[384,1024]{1,0:T(8,128)(2,1)S(1)} %constant_dynamic-update-slice_fusion.a_ref.x_ref, bf16[384,1024]{1,0:T(8,128)(2,1)S(1)} %collective-permute-done.14.b_ref, s32[384,1]{1,0:T(8,128)S(1)} %fusion.ia_ref, s32[384,1]{1,0:T(8,128)S(1)} %broadcast_in_dim.95.ib_ref, ...), custom_call_target="tpu_custom_call" | custom-call | flops 6442450944 | bytes 8388608 | tf_op jit(solution)/shard_map/inner_products/pallas_call | solution.py:133
  118.3 12.6 %collective-permute-done.18 = bf16[384,128]{1,0:T(8,128)(2,1)S(1)} collective-permute-done((bf16[384,128]{1,0:T(8,128)(2,1)S(1)}, bf16[384,128]{1,0:T(8,128)(2,1)S(1)}, u32[]{:S(2)}, u32[]{:S(2)}) %collective-permute-start.18) | collective-permute-done | bytes 98336 | tf_op jit(solution)/shard_map/ppermute | solution.py:22
  133.3 4.5 %collective-permute-done.19 = bf16[384,128]{1,0:T(8,128)(2,1)S(1)} collective-permute-done((bf16[384,128]{1,0:T(8,128)(2,1)S(1)}, bf16[384,128]{1,0:T(8,128)(2,1)S(1)}, u32[]{:S(2)}, u32[]{:S(2)}) %collective-permute-start.19) | collective-permute-done | bytes 98336 | tf_op jit(solution)/shard_map/ppermute | solution.py:22
  141.4 3.9 %collective-permute-done.20 = bf16[384,128]{1,0:T(8,128)(2,1)S(1)} collective-permute-done((bf16[384,128]{1,0:T(8,128)(2,1)S(1)}, bf16[384,128]{1,0:T(8,128)(2,1)S(1)}, u32[]{:S(2)}, u32[]{:S(2)}) %collective-permute-start.20) | collective-permute-done | bytes 98336 | tf_op jit(solution)/shard_map/ppermute | solution.py:22
  148.8 9.4 %adapter_outputs.1 = (bf16[384,1024]{1,0:T(8,128)(2,1)S(1)}, bf16[384,1024]{1,0:T(8,128)(2,1)S(1)}) custom-call(bf16[384,128]{1,0:T(8,128)(2,1)S(1)} %get-tuple-element.68.a_ref, bf16[384,128]{1,0:T(8,128)(2,1)S(1)} %multiply_convert_fusion.b_ref, s32[384,1]{1,0:T(8,128)S(1)} %fusion.ia_ref, s32[384,1]{1,0:T(8,128)S(1)} %broadcast_in_dim.95.ib_ref, ...), custom_call_target="tpu_custom_call" | custom-call | flops 6442450944 | bytes 8388608 | tf_op jit(solution)/shard_map/adapter_outputs/pallas_call | solution.py:183
  161.0 3.9 %project.8 = (bf16[192,1024]{1,0:T(8,128)(2,1)S(1)}, bf16[192,1024]{1,0:T(8,128)(2,1)S(1)}) custom-call(s32[2]{0:T(128)S(1)} %get-tuple-element.125.where_ref, bf16[384,1024]{1,0:T(8,128)(2,1)S(1)} %constant_dynamic-update-slice_fusion.a_ref.x_ref, bf16[1024,8192]{1,0:T(8,128)(2,1)} %w_ref.15, bf16[384,1024]{1,0:T(8,128)(2,1)S(1)} %add_convert_fusion.refs_0_), custom_call_target="tpu_custom_call" | custom-call | flops 805306368 | bytes 2097152 | tf_op jit(solution)/shard_map/project/pallas_call | solution.py:229
  166.3 4.1 %project.12 = (bf16[192,1024]{1,0:T(8,128)(2,1)S(1)}, bf16[192,1024]{1,0:T(8,128)(2,1)S(1)}) custom-call(s32[2]{0:T(128)S(1)} %get-tuple-element.126.where_ref, bf16[384,1024]{1,0:T(8,128)(2,1)S(1)} %constant_dynamic-update-slice_fusion.a_ref.x_ref, bf16[1024,8192]{1,0:T(8,128)(2,1)} %w_ref.15, bf16[384,1024]{1,0:T(8,128)(2,1)S(1)} %add_convert_fusion.refs_0_), custom_call_target="tpu_custom_call" | custom-call | flops 805306368 | bytes 2097152 | tf_op jit(solution)/shard_map/project/pallas_call | solution.py:229
  171.2 5.7 %collective-permute-done.23 = bf16[192,1024]{1,0:T(8,128)(2,1)S(1)} collective-permute-done((bf16[192,1024]{1,0:T(8,128)(2,1)S(1)}, bf16[192,1024]{1,0:T(8,128)(2,1)S(1)}, u32[]{:S(2)}, u32[]{:S(2)}) %collective-permute-start.23) | collective-permute-done | bytes 393248 | tf_op jit(solution)/shard_map/ppermute | solution.py:22
  186.1 8.0 %collective-permute-done.34.refs_6_ = bf16[48,1024]{1,0:T(8,128)(2,1)S(1)} collective-permute-done((bf16[48,1024]{1,0:T(8,128)(2,1)S(1)}, bf16[48,1024]{1,0:T(8,128)(2,1)S(1)}, u32[]{:S(2)}, u32[]{:S(2)}) %collective-permute-start.34) | collective-permute-done | bytes 98336 | tf_op jit(solution)/shard_map/ppermute | solution.py:22
  215.0 3.8 %collective-permute-start.37 = (bf16[48,1024]{1,0:T(8,128)(2,1)S(1)}, bf16[48,1024]{1,0:T(8,128)(2,1)S(1)}, u32[]{:S(2)}, u32[]{:S(2)}) collective-permute-start(bf16[48,1024]{1,0:T(8,128)(2,1)S(1)} %get-tuple-element.87), channel_id=1, source_target_pairs={{0,4},{2,6},{4,0},{6,2},{8,12},{10,14},{12,8},{14,10},{1,5},{3,7},... | collective-permute-start | bytes 294920 | tf_op jit(solution)/shard_map/ppermute | solution.py:22
  225.7 4.2 %collective-permute-done.53.refs_30_ = bf16[48,1024]{1,0:T(8,128)(2,1)S(1)} collective-permute-done((bf16[48,1024]{1,0:T(8,128)(2,1)S(1)}, bf16[48,1024]{1,0:T(8,128)(2,1)S(1)}, u32[]{:S(2)}, u32[]{:S(2)}) %collective-permute-start.53) | collective-permute-done | bytes 98336 | tf_op jit(solution)/shard_map/ppermute | solution.py:22
  229.9 3.8 %collective-permute-start.54 = (bf16[48,1024]{1,0:T(8,128)(2,1)}, bf16[48,1024]{1,0:T(8,128)(2,1)}, u32[]{:S(2)}, u32[]{:S(2)}) collective-permute-start(bf16[48,1024]{1,0:T(8,128)(2,1)} %get-tuple-element.69), channel_id=1, source_target_pairs={{0,12},{2,14},{4,8},{6,10},{8,4},{10,6},{12,0},{14,2},{1,13},{3,15... | collective-permute-start | bytes 294920 | tf_op jit(solution)/shard_map/ppermute | solution.py:22
  (177 shorter events, 95.8 us)
Async XLA Ops:
  1.3 15.1 %collective-permute-start = (bf16[48,1024]{1,0:T(8,128)(2,1)S(1)}, bf16[48,1024]{1,0:T(8,128)(2,1)S(1)}, u32[]{:S(2)}, u32[]{:S(2)}) collective-permute-start(bf16[48,1024]{1,0:T(8,128)(2,1)S(1)} %get-tuple-element.65), channel_id=1, source_target_pairs={{0,2},{2,0},{4,6},{6,4},{8,10},{10,8},{12,14},{14,12},{1,3},{3,1},... | collective-permute-start | bytes 294920 | tf_op jit(solution)/shard_map/ppermute | solution.py:22
  4.3 15.7 %collective-permute-start.1 = (bf16[48,1024]{1,0:T(8,128)(2,1)S(1)}, bf16[48,1024]{1,0:T(8,128)(2,1)S(1)}, u32[]{:S(2)}, u32[]{:S(2)}) collective-permute-start(bf16[48,1024]{1,0:T(8,128)(2,1)S(1)} %get-tuple-element.64), channel_id=1, source_target_pairs={{0,4},{2,6},{4,0},{6,2},{8,12},{10,14},{12,8},{14,10},{1,5},{3,7},... | collective-permute-start | bytes 294920 | tf_op jit(solution)/shard_map/ppermute | solution.py:22
  14.2 15.4 %collective-permute-start.4 = (bf16[48,1024]{1,0:T(8,128)(2,1)S(1)}, bf16[48,1024]{1,0:T(8,128)(2,1)S(1)}, u32[]{:S(2)}, u32[]{:S(2)}) collective-permute-start(bf16[48,1024]{1,0:T(8,128)(2,1)S(1)} %get-tuple-element.61), channel_id=1, source_target_pairs={{0,10},{2,8},{4,14},{6,12},{8,2},{10,0},{12,6},{14,4},{1,11},{3,9}... | collective-permute-start | bytes 294920 | tf_op jit(solution)/shard_map/ppermute | solution.py:22
  71.1 29.5 %collective-permute-start.14 = (bf16[384,1024]{1,0:T(8,128)(2,1)S(1)}, bf16[384,1024]{1,0:T(8,128)(2,1)S(1)}, u32[]{:S(2)}, u32[]{:S(2)}) collective-permute-start(bf16[384,1024]{1,0:T(8,128)(2,1)S(1)} %constant_dynamic-update-slice_fusion.a_ref.x_ref), channel_id=1, source_target_pairs={{0,1},{1,0},{2,3},{3,2},{4,5},{5,4},{6,7},{7,6},{8,9},{9,8},{10,11... | collective-permute-start | bytes 2359304 | tf_op jit(solution)/shard_map/ppermute | solution.py:22
  75.1 23.8 %collective-permute-start.24 = (bf16[192,1024]{1,0:T(8,128)(2,1)S(1)}, bf16[192,1024]{1,0:T(8,128)(2,1)S(1)}, u32[]{:S(2)}, u32[]{:S(2)}) collective-permute-start(bf16[192,1024]{1,0:T(8,128)(2,1)S(1)} %get-tuple-element.32), channel_id=1, source_target_pairs={{0,2},{2,0},{4,6},{6,4},{8,10},{10,8},{12,14},{14,12},{1,3},{3,1},... | collective-permute-start | bytes 1179656 | tf_op jit(solution)/shard_map/ppermute | solution.py:22
  80.7 34.6 %collective-permute-start.26 = (bf16[192,1024]{1,0:T(8,128)(2,1)S(1)}, bf16[192,1024]{1,0:T(8,128)(2,1)S(1)}, u32[]{:S(2)}, u32[]{:S(2)}) collective-permute-start(bf16[192,1024]{1,0:T(8,128)(2,1)S(1)} %get-tuple-element.34), channel_id=1, source_target_pairs={{0,2},{2,0},{4,6},{6,4},{8,10},{10,8},{12,14},{14,12},{1,3},{3,1},... | collective-permute-start | bytes 1179656 | tf_op jit(solution)/shard_map/ppermute | solution.py:22
  85.1 48.0 %collective-permute-start.28 = (bf16[192,1024]{1,0:T(8,128)(2,1)S(1)}, bf16[192,1024]{1,0:T(8,128)(2,1)S(1)}, u32[]{:S(2)}, u32[]{:S(2)}) collective-permute-start(bf16[192,1024]{1,0:T(8,128)(2,1)S(1)} %get-tuple-element.36), channel_id=1, source_target_pairs={{0,2},{2,0},{4,6},{6,4},{8,10},{10,8},{12,14},{14,12},{1,3},{3,1},... | collective-permute-start | bytes 1179656 | tf_op jit(solution)/shard_map/ppermute | solution.py:22
  90.6 56.7 %collective-permute-start.31 = (bf16[192,1024]{1,0:T(8,128)(2,1)S(1)}, bf16[192,1024]{1,0:T(8,128)(2,1)S(1)}, u32[]{:S(2)}, u32[]{:S(2)}) collective-permute-start(bf16[192,1024]{1,0:T(8,128)(2,1)S(1)} %get-tuple-element.40), channel_id=1, source_target_pairs={{0,2},{2,0},{4,6},{6,4},{8,10},{10,8},{12,14},{14,12},{1,3},{3,1},... | collective-permute-start | bytes 1179656 | tf_op jit(solution)/shard_map/ppermute | solution.py:22
  98.9 59.6 %collective-permute-start.33 = (bf16[192,1024]{1,0:T(8,128)(2,1)S(1)}, bf16[192,1024]{1,0:T(8,128)(2,1)S(1)}, u32[]{:S(2)}, u32[]{:S(2)}) collective-permute-start(bf16[192,1024]{1,0:T(8,128)(2,1)S(1)} %get-tuple-element.42), channel_id=1, source_target_pairs={{0,2},{2,0},{4,6},{6,4},{8,10},{10,8},{12,14},{14,12},{1,3},{3,1},... | collective-permute-start | bytes 1179656 | tf_op jit(solution)/shard_map/ppermute | solution.py:22
  100.7 59.3 %collective-permute-start.35 = (bf16[192,1024]{1,0:T(8,128)(2,1)S(1)}, bf16[192,1024]{1,0:T(8,128)(2,1)S(1)}, u32[]{:S(2)}, u32[]{:S(2)}) collective-permute-start(bf16[192,1024]{1,0:T(8,128)(2,1)S(1)} %get-tuple-element.44), channel_id=1, source_target_pairs={{0,2},{2,0},{4,6},{6,4},{8,10},{10,8},{12,14},{14,12},{1,3},{3,1},... | collective-permute-start | bytes 1179656 | tf_op jit(solution)/shard_map/ppermute | solution.py:22
  130.9 47.8 %collective-permute-start.25 = (bf16[48,1024]{1,0:T(8,128)(2,1)S(1)}, bf16[48,1024]{1,0:T(8,128)(2,1)S(1)}, u32[]{:S(2)}, u32[]{:S(2)}) collective-permute-start(bf16[48,1024]{1,0:T(8,128)(2,1)S(1)} %get-tuple-element.92), channel_id=1, source_target_pairs={{0,4},{2,6},{4,0},{6,2},{8,12},{10,14},{12,8},{14,10},{1,5},{3,7},... | collective-permute-start | bytes 294920 | tf_op jit(solution)/shard_map/ppermute | solution.py:22
  145.3 34.6 %collective-permute-start.27 = (bf16[48,1024]{1,0:T(8,128)(2,1)S(1)}, bf16[48,1024]{1,0:T(8,128)(2,1)S(1)}, u32[]{:S(2)}, u32[]{:S(2)}) collective-permute-start(bf16[48,1024]{1,0:T(8,128)(2,1)S(1)} %get-tuple-element.96), channel_id=1, source_target_pairs={{0,8},{2,10},{4,12},{6,14},{8,0},{10,2},{12,4},{14,6},{1,9},{3,11}... | collective-permute-start | bytes 294920 | tf_op jit(solution)/shard_map/ppermute | solution.py:22
  158.6 22.9 %collective-permute-start.29 = (bf16[48,1024]{1,0:T(8,128)(2,1)S(1)}, bf16[48,1024]{1,0:T(8,128)(2,1)S(1)}, u32[]{:S(2)}, u32[]{:S(2)}) collective-permute-start(bf16[48,1024]{1,0:T(8,128)(2,1)S(1)} %get-tuple-element.100), channel_id=1, source_target_pairs={{0,12},{2,14},{4,8},{6,10},{8,4},{10,6},{12,0},{14,2},{1,13},{3,15... | collective-permute-start | bytes 294920 | tf_op jit(solution)/shard_map/ppermute | solution.py:22
  170.4 14.3 %collective-permute-start.30 = (bf16[192,1024]{1,0:T(8,128)(2,1)S(1)}, bf16[192,1024]{1,0:T(8,128)(2,1)S(1)}, u32[]{:S(2)}, u32[]{:S(2)}) collective-permute-start(bf16[192,1024]{1,0:T(8,128)(2,1)S(1)} %get-tuple-element.38), channel_id=1, source_target_pairs={{0,2},{2,0},{4,6},{6,4},{8,10},{10,8},{12,14},{14,12},{1,3},{3,1},... | collective-permute-start | bytes 1179656 | tf_op jit(solution)/shard_map/ppermute | solution.py:22
  178.8 15.3 %collective-permute-start.34 = (bf16[48,1024]{1,0:T(8,128)(2,1)S(1)}, bf16[48,1024]{1,0:T(8,128)(2,1)S(1)}, u32[]{:S(2)}, u32[]{:S(2)}) collective-permute-start(bf16[48,1024]{1,0:T(8,128)(2,1)S(1)} %get-tuple-element.80), channel_id=1, source_target_pairs={{0,8},{2,10},{4,12},{6,14},{8,0},{10,2},{12,4},{14,6},{1,9},{3,11}... | collective-permute-start | bytes 294920 | tf_op jit(solution)/shard_map/ppermute | solution.py:22
  179.8 16.0 %collective-permute-start.36 = (bf16[48,1024]{1,0:T(8,128)(2,1)S(1)}, bf16[48,1024]{1,0:T(8,128)(2,1)S(1)}, u32[]{:S(2)}, u32[]{:S(2)}) collective-permute-start(bf16[48,1024]{1,0:T(8,128)(2,1)S(1)} %get-tuple-element.84), channel_id=1, source_target_pairs={{0,12},{2,14},{4,8},{6,10},{8,4},{10,6},{12,0},{14,2},{1,13},{3,15... | collective-permute-start | bytes 294920 | tf_op jit(solution)/shard_map/ppermute | solution.py:22
  181.5 17.9 %collective-permute-start.38 = (bf16[48,1024]{1,0:T(8,128)(2,1)S(1)}, bf16[48,1024]{1,0:T(8,128)(2,1)S(1)}, u32[]{:S(2)}, u32[]{:S(2)}) collective-permute-start(bf16[48,1024]{1,0:T(8,128)(2,1)S(1)} %get-tuple-element.99), channel_id=1, source_target_pairs={{0,8},{2,10},{4,12},{6,14},{8,0},{10,2},{12,4},{14,6},{1,9},{3,11}... | collective-permute-start | bytes 294920 | tf_op jit(solution)/shard_map/ppermute | solution.py:22
  183.2 17.8 %collective-permute-start.39 = (bf16[48,1024]{1,0:T(8,128)(2,1)S(1)}, bf16[48,1024]{1,0:T(8,128)(2,1)S(1)}, u32[]{:S(2)}, u32[]{:S(2)}) collective-permute-start(bf16[48,1024]{1,0:T(8,128)(2,1)S(1)} %get-tuple-element.95), channel_id=1, source_target_pairs={{0,12},{2,14},{4,8},{6,10},{8,4},{10,6},{12,0},{14,2},{1,13},{3,15... | collective-permute-start | bytes 294920 | tf_op jit(solution)/shard_map/ppermute | solution.py:22
  184.7 22.0 %collective-permute-start.41 = (bf16[48,1024]{1,0:T(8,128)(2,1)S(1)}, bf16[48,1024]{1,0:T(8,128)(2,1)S(1)}, u32[]{:S(2)}, u32[]{:S(2)}) collective-permute-start(bf16[48,1024]{1,0:T(8,128)(2,1)S(1)} %get-tuple-element.83), channel_id=1, source_target_pairs={{0,8},{2,10},{4,12},{6,14},{8,0},{10,2},{12,4},{14,6},{1,9},{3,11}... | collective-permute-start | bytes 294920 | tf_op jit(solution)/shard_map/ppermute | solution.py:22
  194.1 15.1 %collective-permute-start.42 = (bf16[48,1024]{1,0:T(8,128)(2,1)S(1)}, bf16[48,1024]{1,0:T(8,128)(2,1)S(1)}, u32[]{:S(2)}, u32[]{:S(2)}) collective-permute-start(bf16[48,1024]{1,0:T(8,128)(2,1)S(1)} %get-tuple-element.79), channel_id=1, source_target_pairs={{0,12},{2,14},{4,8},{6,10},{8,4},{10,6},{12,0},{14,2},{1,13},{3,15... | collective-permute-start | bytes 294920 | tf_op jit(solution)/shard_map/ppermute | solution.py:22
  195.8 14.7 %collective-permute-start.43 = (bf16[48,1024]{1,0:T(8,128)(2,1)S(1)}, bf16[48,1024]{1,0:T(8,128)(2,1)S(1)}, u32[]{:S(2)}, u32[]{:S(2)}) collective-permute-start(bf16[48,1024]{1,0:T(8,128)(2,1)S(1)} %get-tuple-element.98), channel_id=1, source_target_pairs={{0,4},{2,6},{4,0},{6,2},{8,12},{10,14},{12,8},{14,10},{1,5},{3,7},... | collective-permute-start | bytes 294920 | tf_op jit(solution)/shard_map/ppermute | solution.py:22
  215.0 14.9 %collective-permute-start.53 = (bf16[48,1024]{1,0:T(8,128)(2,1)S(1)}, bf16[48,1024]{1,0:T(8,128)(2,1)S(1)}, u32[]{:S(2)}, u32[]{:S(2)}) collective-permute-start(bf16[48,1024]{1,0:T(8,128)(2,1)S(1)} %get-tuple-element.73), channel_id=1, source_target_pairs={{0,8},{2,10},{4,12},{6,14},{8,0},{10,2},{12,4},{14,6},{1,9},{3,11}... | collective-permute-start | bytes 294920 | tf_op jit(solution)/shard_map/ppermute | solution.py:22
  215.0 14.9 %collective-permute-start.37 = (bf16[48,1024]{1,0:T(8,128)(2,1)S(1)}, bf16[48,1024]{1,0:T(8,128)(2,1)S(1)}, u32[]{:S(2)}, u32[]{:S(2)}) collective-permute-start(bf16[48,1024]{1,0:T(8,128)(2,1)S(1)} %get-tuple-element.87), channel_id=1, source_target_pairs={{0,4},{2,6},{4,0},{6,2},{8,12},{10,14},{12,8},{14,10},{1,5},{3,7},... | collective-permute-start | bytes 294920 | tf_op jit(solution)/shard_map/ppermute | solution.py:22
  219.5 14.3 %collective-permute-start.40 = (bf16[48,1024]{1,0:T(8,128)(2,1)}, bf16[48,1024]{1,0:T(8,128)(2,1)S(1)}, u32[]{:S(2)}, u32[]{:S(2)}) collective-permute-start(bf16[48,1024]{1,0:T(8,128)(2,1)} %get-tuple-element.71), channel_id=1, source_target_pairs={{0,4},{2,6},{4,0},{6,2},{8,12},{10,14},{12,8},{14,10},{1,5},{3,7},... | collective-permute-start | bytes 294920 | tf_op jit(solution)/shard_map/ppermute | solution.py:22
  (32 other events, 364.0 us)

commit v2 on v1

v2 whole, which is shorter than its diff:
```python
import functools

import jax
import jax.numpy as jnp
from jax import lax
from jax.experimental import pallas as pl
from jax.experimental.pallas import tpu as pltpu
from jax.sharding import PartitionSpec as P

HEADS = 64
KV_HEADS = 8
HEAD_DIM = 128
ADAPTER_SCALE = 0.25
BF16 = jnp.bfloat16
F32 = jnp.float32
ROW_BLOCK = 16
SUB = 8
BATCH = 4
VMEM_LIMIT = 48 * 1024 * 1024


ADD_US = 8.7


def cost(us):
    return pl.CostEstimate(flops=int(us * 1.15e9), bytes_accessed=1, transcendentals=0)


def permute_xor(x, axis, size, k):
    return lax.ppermute(x, axis, [(i, i ^ k) for i in range(size)])


def attend_kernel(n, q_ref, k_ref, v_ref, fk_ref, fv_ref, len_ref, o_ref):
    groups = HEADS // KV_HEADS
    per_src = HEADS // n
    positions = k_ref.shape[1]
    lanes = 2 * positions
    tiles = SUB // 2
    rows = groups * SUB
    row_of = lax.broadcasted_iota(jnp.int32, (rows, lanes), 0) % SUB
    lane_of = lax.broadcasted_iota(jnp.int32, (rows, lanes), 1)
    in_row = (row_of % 2) == (lane_of // positions)
    tile_of = row_of // 2
    scale = HEAD_DIM ** (-0.5)
    parts = [slice(s * SUB, (s + 1) * SUB) for s in range(ROW_BLOCK // SUB)]
    lives = [
        in_row & ((lane_of % positions) < jnp.tile(len_ref[part], (groups, 1))) for part in parts
    ]
    for first in range(0, KV_HEADS, BATCH):
        batch = range(first, first + BATCH)
        scores, owns, values, fresh = [], [], [], []
        for c in batch:
            span = slice(c * HEAD_DIM, (c + 1) * HEAD_DIM)
            heads = [c * groups + h for h in range(groups)]
            q_heads = [
                q_ref[h // per_src, :, (h % per_src) * HEAD_DIM : (h % per_src + 1) * HEAD_DIM].astype(F32)
                for h in heads
            ]
            fresh_key = fk_ref[:, span].astype(F32)
            fresh_value = fv_ref[:, span].astype(F32)
            for part, live in zip(parts, lives):
                q_f32 = jnp.concatenate([q[part] for q in q_heads], axis=0)
                keys = k_ref[part, :, span].reshape(SUB * positions, HEAD_DIM)
                full = lax.dot_general(
                    q_f32.astype(BF16), keys, (((1,), (1,)), ((), ())), preferred_element_type=F32
                )
                score = full[:, :lanes]
                for k in range(1, tiles):
                    score = jnp.where(tile_of == k, full[:, k * lanes : (k + 1) * lanes], score)
                scores.append(jnp.where(live, score * scale, -1e30))
                owns.append(
                    jnp.sum(q_f32 * jnp.tile(fresh_key[part], (groups, 1)), axis=1, keepdims=True) * scale
                )
                fresh.append(jnp.tile(fresh_value[part], (groups, 1)))
                values.append(v_ref[part, :, span].reshape(SUB * positions, HEAD_DIM))
        peaks = [jnp.maximum(jnp.max(s, axis=1, keepdims=True), o) for s, o in zip(scores, owns)]
        weights = [
            jnp.where(live, jnp.exp(s - p), 0.0) for s, p, live in zip(scores, peaks, lives * BATCH)
        ]
        own_weights = [jnp.exp(o - p) for o, p in zip(owns, peaks)]
        totals = [jnp.sum(w, axis=1, keepdims=True) + o for w, o in zip(weights, own_weights)]
        outs = []
        for w, o, t, v, f in zip(weights, own_weights, totals, values, fresh):
            prob = w / t
            prob_new = (o / t).astype(BF16).astype(F32)
            wide = jnp.concatenate([jnp.where(tile_of == k, prob, 0.0) for k in range(tiles)], axis=1)
            outs.append(jnp.dot(wide.astype(BF16), v, preferred_element_type=F32) + prob_new * f)
        for i, c in enumerate(batch):
            pair = outs[i * len(parts) : (i + 1) * len(parts)]
            for g in range(groups):
                h = c * groups + g
                block = jnp.concatenate([o[g * SUB : (g + 1) * SUB] for o in pair], axis=0).astype(BF16)
                o_ref[h // per_src, :, (h % per_src) * HEAD_DIM : (h % per_src + 1) * HEAD_DIM] = block


def attend(q, keys, values, fresh_key, fresh_value, lengths):
    n, rows, width = q.shape
    kv = keys.shape[2]
    positions = keys.shape[1]
    return pl.pallas_call(
        functools.partial(attend_kernel, n),
        grid=(rows // ROW_BLOCK,),
        in_specs=[
            pl.BlockSpec((n, ROW_BLOCK, width), lambda i: (0, i, 0)),
            pl.BlockSpec((ROW_BLOCK, positions, kv), lambda i: (i, 0, 0)),
            pl.BlockSpec((ROW_BLOCK, positions, kv), lambda i: (i, 0, 0)),
            pl.BlockSpec((ROW_BLOCK, kv), lambda i: (i, 0)),
            pl.BlockSpec((ROW_BLOCK, kv), lambda i: (i, 0)),
            pl.BlockSpec((ROW_BLOCK, 1), lambda i: (i, 0)),
        ],
        out_specs=pl.BlockSpec((n, ROW_BLOCK, width), lambda i: (0, i, 0)),
        out_shape=jax.ShapeDtypeStruct((n, rows, width), BF16),
        compiler_params=pltpu.CompilerParams(vmem_limit_bytes=VMEM_LIMIT),
        cost_estimate=cost(9),
        name="attend",
    )(q, keys, values, fresh_key, fresh_value, lengths)


def inner_kernel(per, a_ref, b_ref, ia_ref, ib_ref, down_ref, *refs):
    oa_ref, ob_ref, acc_a, acc_b = refs[-4:]
    step = pl.program_id(0)

    @pl.when(step == 0)
    def _():
        acc_a[...] = jnp.zeros_like(acc_a)
        acc_b[...] = jnp.zeros_like(acc_b)

    rank = down_ref.shape[2]
    for p in range(0, per, 2):
        wide = jnp.concatenate([down_ref[p], down_ref[p + 1]], axis=1)
        for x_ref, id_ref, acc in ((a_ref, ia_ref, acc_a), (b_ref, ib_ref, acc_b)):
            product = jnp.dot(x_ref[...], wide, preferred_element_type=F32)
            ids = id_ref[...] - (step * per + p)
            total = jnp.where(ids == 0, product[:, :rank], acc[...])
            acc[...] = jnp.where(ids == 1, product[:, rank:], total)

    @pl.when(step == pl.num_programs(0) - 1)
    def _():
        oa_ref[...] = acc_a[...].astype(BF16)
        ob_ref[...] = acc_b[...].astype(BF16)


def inner_products(rows_a, rows_b, ids_a, ids_b, down, after):
    rows, width = rows_a.shape
    owned, _, rank = down.shape
    per = 8
    whole = lambda shape: pl.BlockSpec(shape, lambda i: (0, 0))
    return pl.pallas_call(
        functools.partial(inner_kernel, per),
        grid=(owned // per,),
        in_specs=[
            whole((rows, width)),
            whole((rows, width)),
            whole((rows, 1)),
            whole((rows, 1)),
            pl.BlockSpec((per, width, rank), lambda i: (i, 0, 0)),
        ]
        + [pl.BlockSpec(memory_space=pl.ANY)] * len(after),
        out_specs=[whole((rows, rank)), whole((rows, rank))],
        out_shape=[jax.ShapeDtypeStruct((rows, rank), BF16)] * 2,
        scratch_shapes=[pltpu.VMEM((rows, rank), F32)] * 2,
        compiler_params=pltpu.CompilerParams(vmem_limit_bytes=VMEM_LIMIT),
        cost_estimate=cost(9),
        name="inner_products",
    )(rows_a, rows_b, ids_a, ids_b, down, *after)


def delta_kernel(per, a_ref, b_ref, ia_ref, ib_ref, up_ref, *refs):
    oa_ref, ob_ref, acc_a, acc_b = refs[-4:]
    step = pl.program_id(0)

    @pl.when(step == 0)
    def _():
        acc_a[...] = jnp.zeros_like(acc_a)
        acc_b[...] = jnp.zeros_like(acc_b)

    rank, width = up_ref.shape[1:]
    up = up_ref[...].reshape(per * rank, width)
    for x_ref, id_ref, acc in ((a_ref, ia_ref, acc_a), (b_ref, ib_ref, acc_b)):
        x = x_ref[...]
        ids = id_ref[...]
        wide = jnp.concatenate(
            [jnp.where(ids == step * per + i, x, jnp.zeros_like(x)) for i in range(per)], axis=1
        ).astype(BF16)
        acc[...] += jnp.dot(wide, up, preferred_element_type=F32)

    @pl.when(step == pl.num_programs(0) - 1)
    def _():
        oa_ref[...] = acc_a[...].astype(BF16)
        ob_ref[...] = acc_b[...].astype(BF16)


def adapter_outputs(scaled_a, scaled_b, ids_a, ids_b, up, after):
    rows, rank = scaled_a.shape
    owned, _, width = up.shape
    per = 8
    whole = lambda shape: pl.BlockSpec(shape, lambda i: (0, 0))
    return pl.pallas_call(
        functools.partial(delta_kernel, per),
        grid=(owned // per,),
        in_specs=[
            whole((rows, rank)),
            whole((rows, rank)),
            whole((rows, 1)),
            whole((rows, 1)),
            pl.BlockSpec((per, rank, width), lambda i: (i, 0, 0)),
        ]
        + [pl.BlockSpec(memory_space=pl.ANY)] * len(after),
        out_specs=[whole((rows, width)), whole((rows, width))],
        out_shape=[jax.ShapeDtypeStruct((rows, width), BF16)] * 2,
        scratch_shapes=[pltpu.VMEM((rows, width), F32)] * 2,
        compiler_params=pltpu.CompilerParams(vmem_limit_bytes=VMEM_LIMIT),
        cost_estimate=cost(10),
        name="adapter_outputs",
    )(scaled_a, scaled_b, ids_a, ids_b, up, *after)


def project_kernel(spans, with_delta, where_ref, x_ref, w_ref, *refs):
    n, rows, _ = x_ref.shape
    scratch = refs[-1]
    outs = refs[len(refs) - 1 - 2 * len(spans) : -1]
    step = pl.program_id(0)
    y, z = where_ref[0], where_ref[1]
    blocks = [2 * (z ^ j) + side for side in (y, 1 - y) for j in range(n // 2)]

    @pl.when(step == 0)
    def _():
        for i, block in enumerate(blocks):
            scratch[i * rows : (i + 1) * rows] = x_ref[block]

    result = jnp.dot(scratch[...], w_ref[...], preferred_element_type=F32)
    if with_delta:
        result = result + jnp.concatenate([refs[0][i].astype(F32) for i in blocks], axis=0)
    result = result.astype(BF16)
    for c, (first, count) in enumerate(spans):

        @pl.when((step >= first) & (step < first + count))
        def _():
            for i in range(n):
                o_ref = outs[2 * c + i // (n // 2)]
                o_ref[i % (n // 2)] = result[i * rows : (i + 1) * rows]


def project(y, z, starts, widths, x, weight, delta=None, after=()):
    n, rows, depth = x.shape
    tile = min(512, min(widths))
    spans, table = [], [y, z]
    for start, width in zip(starts, widths):
        spans.append((len(table) - 2, width // tile))
        table += [start // tile + i for i in range(width // tile)]
    steps = len(table) - 2
    ins = [
        pl.BlockSpec((n, rows, depth), lambda i, w: (0, 0, 0)),
        pl.BlockSpec((depth, tile), lambda i, w: (0, w[2 + i])),
    ]
    args = [x, weight]
    if delta is not None:
        ins.append(pl.BlockSpec((n, rows, tile), lambda i, w: (0, 0, i)))
        args.append(delta)

    def out_spec(first, count):
        return pl.BlockSpec(
            (n // 2, rows, tile), lambda i, w: (0, 0, jnp.clip(i - first, 0, count - 1))
        )

    outs = pl.pallas_call(
        functools.partial(project_kernel, spans, delta is not None),
        grid_spec=pltpu.PrefetchScalarGridSpec(
            num_scalar_prefetch=1,
            grid=(steps,),
            in_specs=ins + [pl.BlockSpec(memory_space=pl.ANY)] * len(after),
            out_specs=[out_spec(*span) for span in spans for _ in range(2)],
            scratch_shapes=[pltpu.VMEM((n * rows, depth), BF16)],
        ),
        out_shape=[jax.ShapeDtypeStruct((n // 2, rows, w), BF16) for w in widths for _ in range(2)],
        compiler_params=pltpu.CompilerParams(vmem_limit_bytes=VMEM_LIMIT),
        cost_estimate=cost(1.5 * steps),
        name="project",
    )(jnp.stack(table), *args, *after)
    return outs[::2], outs[1::2]


def add_kernel(near_ref, far_ref, *refs):
    for j, o_ref in enumerate(refs[-near_ref.shape[0] :]):
        o_ref[...] = (near_ref[j].astype(F32) + far_ref[j].astype(F32)).astype(BF16)


def add_sides(near, far, after):
    nz, rows, width = near.shape
    vmem = pl.BlockSpec(memory_space=pltpu.VMEM)
    return pl.pallas_call(
        add_kernel,
        in_specs=[vmem] * 2 + [pl.BlockSpec(memory_space=pl.ANY)] * len(after),
        out_specs=[vmem] * nz,
        out_shape=[jax.ShapeDtypeStruct((rows, width), BF16)] * nz,
        compiler_params=pltpu.CompilerParams(vmem_limit_bytes=VMEM_LIMIT),
        cost_estimate=cost(ADD_US * width * nz / 4096),
        name="add_sides",
    )(near, far, *after)


def finish_kernel(plan, width, place_ref, res_ref, *refs):
    o_ref = refs[-1]
    z, y = place_ref[0], place_ref[1]
    for group, half, terms in plan:
        side = y ^ half
        place = pl.ds(pl.multiple_of(((z ^ group) * 2 + side) * width, width), width)
        total = res_ref[:, place].astype(F32)
        for kind, first in terms:
            if kind == "whole":
                term = refs[first][...]
            elif kind == "half":
                term = refs[first][:, pl.ds(pl.multiple_of(side * width, width), width)]
            else:
                term = jnp.where(side == 0, refs[first[0]][...], refs[first[1]][...])
            total = total + term.astype(F32)
        o_ref[:, place] = total.astype(BF16)


def finish(place, residual, plan, width, arrays):
    rows, features = residual.shape
    vmem = pl.BlockSpec(memory_space=pltpu.VMEM)
    return pl.pallas_call(
        functools.partial(finish_kernel, plan, width),
        in_specs=[pl.BlockSpec(memory_space=pltpu.SMEM), vmem] + [vmem] * len(arrays),
        out_specs=vmem,
        out_shape=jax.ShapeDtypeStruct((rows, features), BF16),
        compiler_params=pltpu.CompilerParams(vmem_limit_bytes=VMEM_LIMIT),
        cost_estimate=cost(2),
        name="finish",
    )(place, residual, *arrays)


def shards(
    n,
    n_dp,
    queries,
    cached_key_rows,
    cached_value_rows,
    fresh_key_value,
    lengths,
    residual,
    output_weight,
    adapter_down,
    adapter_up,
    rank,
    requests,
    row_choice,
):
    nz = n // 2
    me = lax.axis_index("tp").astype(jnp.int32)
    dp = lax.axis_index("dp").astype(jnp.int32)
    z, y = me // 2, me % 2
    rows_dp = queries.shape[1]
    rows = rows_dp // n
    width = queries.shape[2]
    pool_rank = adapter_down.shape[2]
    owned = adapter_down.shape[0]
    fetch = requests.shape[1]

    q = lax.all_to_all(queries[0].reshape(n, rows, width), "tp", 0, 0)
    attended = attend(
        q,
        cached_key_rows[0],
        cached_value_rows[0],
        fresh_key_value[0, :, 0],
        fresh_key_value[0, :, 1],
        lengths[0][:, None],
    )

    choice = row_choice[0]
    lists = requests[0]
    sides = []
    for side in range(2):
        if side == 1:
            choice = permute_xor(choice, "dp", n_dp, 1)
            lists = permute_xor(lists, "dp", n_dp, 1)
        hit = choice[:, None] - owned == jnp.arange(fetch, dtype=jnp.int32)[None, :]
        fetched = jnp.sum(jnp.where(hit, lists[None, :], 0), axis=1)
        slot = jnp.where(choice < owned, (dp ^ side) * owned + choice, fetched)
        local = slot - dp * owned
        mine = (local >= 0) & (local < owned)
        pool = jnp.arange(rank.shape[0], dtype=jnp.int32)
        row_rank = jnp.sum(jnp.where(slot[:, None] == pool[None, :], rank[None, :], 0), axis=1)
        factor = jnp.where(
            (jnp.arange(pool_rank)[None, :] < row_rank[:, None]) & mine[:, None],
            (ADAPTER_SCALE * pool_rank / row_rank.astype(F32))[:, None],
            0.0,
        )
        sides.append((local[:, None], factor))
    (ids_a, factor_a), (ids_b, factor_b) = sides

    x = lax.all_to_all(attended, "tp", 0, 0)
    x_rows = x.reshape(rows_dp, width)
    x_other = permute_xor(x_rows, "dp", n_dp, 1)

    chunks = [(nz - 1, 0, width), (nz - 1, width, width)]
    chunks += [(jz, 0, 2 * width) for jz in reversed(range(1, nz - 1))]
    chunks += [(0, (1 - y) * width, width), (0, y * width, width)]
    count = len(chunks)

    starts = [(z ^ jz) * 2 * width + low for jz, low, _ in chunks]
    widths = [size for _, _, size in chunks]

    def across_y(x):
        return permute_xor(x, "tp", n, 1)

    def along_z(near, far, after):
        total = add_sides(near, far, after)
        return [total[0]] + [permute_xor(total[j], "tp", n, 2 * j) for j in range(1, nz)]

    near, far = project(y, z, starts[:1], widths[:1], x, output_weight)
    more, others = project(y, z, starts[1:-1], widths[1:-1], x, output_weight, after=[near[0]])
    near += more
    far = [across_y(v) for v in far + others]
    inner_a, inner_b = inner_products(x_rows, x_other, ids_a, ids_b, adapter_down, [near[1]])
    received = []
    for i in range(count - 2):
        received.append(along_z(near[i], far[i], received[i - 2][1:] if i >= 2 else []))

    inner = inner_a.astype(F32) + permute_xor(inner_b, "dp", n_dp, 1).astype(F32)
    step = 1
    while step < n:
        inner = inner + permute_xor(inner.astype(BF16), "tp", n, step).astype(F32)
        step *= 2
    inner = inner.astype(BF16)
    inner_other = permute_xor(inner, "dp", n_dp, 1)
    delta_a, delta_b = adapter_outputs(
        (inner.astype(F32) * factor_a).astype(BF16),
        (inner_other.astype(F32) * factor_b).astype(BF16),
        ids_a,
        ids_b,
        adapter_up,
        received[1][1:],
    )
    delta = (delta_a.astype(F32) + permute_xor(delta_b, "dp", n_dp, 1).astype(F32)).astype(BF16)
    delta = delta.reshape(n, rows, width)

    more, others = project(y, z, starts[-1:], widths[-1:], x, output_weight, delta)
    received.append(along_z(more[0], far[-1], received[-2][1:]))
    received.append(along_z(near[-1], across_y(others[0]), received[-2][1:]))

    slots = {(i, j): i * nz + j for i in range(count) for j in range(nz)}
    arrays = [received[i][j] for i in range(count) for j in range(nz)]
    plan = []
    for group in range(nz):
        for half in range(2):
            terms = []
            for j in range(nz):
                jz = group ^ j
                if jz == 0:
                    terms.append(("whole", slots[count - 2 + half, j]))
                elif jz == nz - 1:
                    terms.append(("pick", (slots[0, j], slots[1, j])))
                else:
                    terms.append(("half", slots[nz - jz, j]))
            plan.append((group, half, terms))
    return finish(jnp.stack([z, y]), residual[0], plan, width, arrays)[None]


def solution(mesh):
    return jax.shard_map(
        functools.partial(shards, mesh.shape["tp"], mesh.shape["dp"]),
        mesh=mesh,
        in_specs=(
            P(("groups", "dp"), None, "tp"),
            P(("groups", "dp"), "tp", None, None),
            P(("groups", "dp"), "tp", None, None),
            P(("groups", "dp"), "tp", None, None),
            P(("groups", "dp"), "tp"),
            P(("groups", "dp"), "tp", None),
            P("tp", None),
            P("dp", "tp", None),
            P("dp", None, "tp"),
            P(),
            P(("groups", "dp"), None),
            P(("groups", "dp"), None),
        ),
        out_specs=P(("groups", "dp"), "tp", None),
        check_vma=False,
    )
```

time: 241 us -> 190 us (0.79)
  starting transfers between devices: 83.5 us -> 45.3 us
  Pallas kernels: 75.9 us -> 50 us
  waiting for transfers between devices: 69.6 us -> 88.5 us
  local copies, waits for them, and re-layouts: 6.1 us -> 2.69 us
    ppermute x55 -> x33, starting transfers between devices: 83.5 us -> 34.3 us  [permute_xor(): return lax.ppermute(x, axis, [(i, i ^ k) for i in range(size)])]
    all_to_all x0 -> x2, waiting for transfers between devices: none -> 34.9 us  [the longest x1 18.9 us: shards(): x = lax.all_to_all(attended, 'tp', 0, 0)]
    pallas_call x10 -> x11, Pallas kernels: 52.4 us -> 31.4 us  [the longest x3 19.8 us: project(): pl.pallas_call(functools.partial(project_kernel, spans, delta is not None...]
    ppermute x55 -> x33, waiting for transfers between devices: 69.6 us -> 53.6 us  [permute_xor(): return lax.ppermute(x, axis, [(i, i ^ k) for i in range(size)])]
    all_to_all x0 -> x2, starting transfers between devices: none -> 11 us  [the longest x1 7.28 us: shards(): q = lax.all_to_all(queries[0].reshape(n, rows, width), 'tp', 0, 0)]
    pallas_call x1, Pallas kernels: 14.1 us -> 9.08 us  [inner_products(): pl.pallas_call(functools.partial(inner_kernel, per), grid=(owned // per,)...]
  transfers between devices with their start and end apart: 55 -> 35, of which waited for: 19 -> 15; matrix products, arithmetic and copies ran while one was open for 4% -> 3% of each run, Pallas kernels for 23% -> 20%
where the time goes in v2:
time: 190 us
  waiting for transfers between devices  88.5 us (47%)
  Pallas kernels  50 us (26%)
  starting transfers between devices  45.3 us (24%)
  other arithmetic  2.92 us (2%)
  local copies, waits for them, and re-layouts  2.69 us (1%)
    ppermute x33, waiting for transfers between devices, permute_xor(): return lax.ppermute(x, axis, [(i, i ^ k) for i in range(size)])  53.6 us
    ppermute x33, starting transfers between devices, permute_xor(): return lax.ppermute(x, axis, [(i, i ^ k) for i in range(size)])  34.3 us
    pallas_call x3, Pallas kernels, project(): pl.pallas_call(functools.partial(project_kernel, spans, delta is not None...  19.8 us
    all_to_all x1, waiting for transfers between devices, shards(): x = lax.all_to_all(attended, 'tp', 0, 0)  18.9 us
    all_to_all x1, waiting for transfers between devices, shards(): q = lax.all_to_all(queries[0].reshape(n, rows, width), 'tp', 0, 0)  16.1 us
    pallas_call x1, Pallas kernels, adapter_outputs(): pl.pallas_call(functools.partial(delta_kernel, per), grid=(owned // per,)...  9.51 us
    pallas_call x1, Pallas kernels, inner_products(): pl.pallas_call(functools.partial(inner_kernel, per), grid=(owned // per,)...  9.08 us
    pallas_call x1, Pallas kernels, attend(): pl.pallas_call(functools.partial(attend_kernel, n), grid=(rows // ROW_BLO...  8.72 us
  transfers between devices with their start and end apart: 35, of which 15 were waited for; matrix products, arithmetic and copies ran while one was open for 3% of the time, Pallas kernels for 20%

profile of v2, /device:TPU:0, one launch (start us, length us, event | category | flops | bytes accessed | tf_op | source)
XLA Modules:
  0.0 189.8 jit_solution(17641032825171352685)
XLA Ops:
  0.0 7.3 %all-to-all-start = ((bf16[8,48,1024]{2,1,0:T(8,128)(2,1)}), bf16[8,48,1024]{2,1,0:T(8,128)(2,1)S(1)}, u32[]{:S(2)}, u32[]{:S(2)}) async-start(bf16[8,48,1024]{2,1,0:T(8,128)(2,1)} %bitcast.39), calls=%async_computation | async-start | bytes 1572864 | tf_op jit(solution)/shard_map/all_to_all | solution.py:361
  11.4 16.1 %all-to-all-done.q_ref = bf16[8,48,1024]{2,1,0:T(8,128)(2,1)S(1)} async-done(((bf16[8,48,1024]{2,1,0:T(8,128)(2,1)}), bf16[8,48,1024]{2,1,0:T(8,128)(2,1)S(1)}, u32[]{:S(2)}, u32[]{:S(2)}) %all-to-all-start) | async-done | bytes 786464 | tf_op jit(solution)/shard_map/all_to_all | solution.py:361
  27.5 8.7 %attend.1 = bf16[8,48,1024]{2,1,0:T(8,128)(2,1)} custom-call(bf16[8,48,1024]{2,1,0:T(8,128)(2,1)S(1)} %all-to-all-done.q_ref, bf16[48,64,1024]{2,1,0:T(8,128)(2,1)} %bitcast.43, bf16[48,64,1024]{2,1,0:T(8,128)(2,1)} %bitcast.44, bf16[48,1024]{1,0:T(8,128)(2,1)S(1)} %get-tuple-element.99.fk_ref, bf16[48,1024]{1,0:T(8,128)(2,1)S(1)} %get-tuple-element.98.fv_ref, ...), custom_call_target="tpu_custom_call" | custom-call | flops 10350000128 | bytes 1 | tf_op jit(solution)/shard_map/attend/pallas_call | solution.py:100
  36.2 3.7 %all-to-all-start.1 = ((bf16[8,48,1024]{2,1,0:T(8,128)(2,1)}), bf16[8,48,1024]{2,1,0:T(8,128)(2,1)S(1)}, u32[]{:S(2)}, u32[]{:S(2)}) async-start(bf16[8,48,1024]{2,1,0:T(8,128)(2,1)} %attend.1), calls=%async_computation.1 | async-start | bytes 1572864 | tf_op jit(solution)/shard_map/all_to_all | solution.py:393
  41.2 18.9 %all-to-all-done.1.x_ref = bf16[8,48,1024]{2,1,0:T(8,128)(2,1)S(1)} async-done(((bf16[8,48,1024]{2,1,0:T(8,128)(2,1)}), bf16[8,48,1024]{2,1,0:T(8,128)(2,1)S(1)}, u32[]{:S(2)}, u32[]{:S(2)}) %all-to-all-start.1) | async-done | bytes 786464 | tf_op jit(solution)/shard_map/all_to_all | solution.py:393
  60.1 3.2 %project.3 = (bf16[4,48,1024]{2,1,0:T(8,128)(2,1)S(1)}, bf16[4,48,1024]{2,1,0:T(8,128)(2,1)S(1)}) custom-call(s32[4]{0:T(128)S(1)} %pad_add_fusion.1.where_ref, bf16[8,48,1024]{2,1,0:T(8,128)(2,1)S(1)} %all-to-all-done.1.x_ref, bf16[1024,8192]{1,0:T(8,128)(2,1)} %w_ref.5), custom_call_target="tpu_custom_call" | custom-call | flops 3449999872 | bytes 1 | tf_op jit(solution)/shard_map/project/pallas_call | solution.py:266
  63.3 13.4 %project.4 = (bf16[4,48,1024]{2,1,0:T(8,128)(2,1)S(1)}, bf16[4,48,1024]{2,1,0:T(8,128)(2,1)S(1)}, bf16[4,48,2048]{2,1,0:T(8,128)(2,1)S(1)}, bf16[4,48,2048]{2,1,...) custom-call(s32[14]{0:T(128)S(1)} %stack.90.where_ref, ...), custom_call_target="tpu_custom_call" | custom-call | flops 20700000256 | bytes 1 | tf_op jit(solution)/shard_map/project/pallas_call | solution.py:266
  76.7 9.1 %inner_products.1 = (bf16[384,128]{1,0:T(8,128)(2,1)S(1)}, bf16[384,128]{1,0:T(8,128)(2,1)S(1)}) custom-call(bf16[384,1024]{1,0:T(8,128)(2,1)S(1)} %bitcast.36, bf16[384,1024]{1,0:T(8,128)(2,1)S(1)} %collective-permute-done.16.b_ref, s32[384,1]{1,0:T(8,128)S(1)} %fusion.ia_ref, s32[384,1]{1,0:T(8,128)S(1)} %broadcast_in_dim.90.ib_ref, ...), custom_call_target="tpu_custom_call" | custom-call | flops 10350000128 | bytes 1 | tf_op jit(solution)/shard_map/inner_products/pallas_call | solution.py:148
  92.0 8.5 %collective-permute-done.20 = bf16[384,128]{1,0:T(8,128)(2,1)S(1)} collective-permute-done((bf16[384,128]{1,0:T(8,128)(2,1)S(1)}, bf16[384,128]{1,0:T(8,128)(2,1)S(1)}, u32[]{:S(2)}, u32[]{:S(2)}) %collective-permute-start.20) | collective-permute-done | bytes 98336 | tf_op jit(solution)/shard_map/ppermute | solution.py:30
  102.8 2.4 %collective-permute-done.21 = bf16[384,128]{1,0:T(8,128)(2,1)S(1)} collective-permute-done((bf16[384,128]{1,0:T(8,128)(2,1)S(1)}, bf16[384,128]{1,0:T(8,128)(2,1)S(1)}, u32[]{:S(2)}, u32[]{:S(2)}) %collective-permute-start.21) | collective-permute-done | bytes 98336 | tf_op jit(solution)/shard_map/ppermute | solution.py:30
  105.3 3.6 %collective-permute-done.4.far_ref = bf16[4,48,1024]{2,1,0:T(8,128)(2,1)S(1)} collective-permute-done((bf16[4,48,1024]{2,1,0:T(8,128)(2,1)S(1)}, bf16[4,48,1024]{2,1,0:T(8,128)(2,1)S(1)}, u32[]{:S(2)}, u32[]{:S(2)}) %collective-permute-start.4) | collective-permute-done | bytes 393248 | tf_op jit(solution)/shard_map/ppermute | solution.py:30
  109.0 7.2 %collective-permute-done.22 = bf16[384,128]{1,0:T(8,128)(2,1)S(1)} collective-permute-done((bf16[384,128]{1,0:T(8,128)(2,1)S(1)}, bf16[384,128]{1,0:T(8,128)(2,1)S(1)}, u32[]{:S(2)}, u32[]{:S(2)}) %collective-permute-start.22) | collective-permute-done | bytes 98336 | tf_op jit(solution)/shard_map/ppermute | solution.py:30
  119.0 4.3 %collective-permute-done.3.refs_2_.refs_3_ = bf16[48,1024]{1,0:T(8,128)(2,1)S(1)} collective-permute-done((bf16[48,1024]{1,0:T(8,128)(2,1)S(1)}, bf16[48,1024]{1,0:T(8,128)(2,1)S(1)}, u32[]{:S(2)}, u32[]{:S(2)}) %collective-permute-start.3) | collective-permute-done | bytes 98336 | tf_op jit(solution)/shard_map/ppermute | solution.py:30
  123.3 2.4 %collective-permute-done.8.far_ref = bf16[4,48,2048]{2,1,0:T(8,128)(2,1)S(1)} collective-permute-done((bf16[4,48,2048]{2,1,0:T(8,128)(2,1)S(1)}, bf16[4,48,2048]{2,1,0:T(8,128)(2,1)S(1)}, u32[]{:S(2)}, u32[]{:S(2)}) %collective-permute-start.8) | collective-permute-done | bytes 786464 | tf_op jit(solution)/shard_map/ppermute | solution.py:30
  128.8 2.9 %collective-permute-start.10 = (bf16[48,2048]{1,0:T(8,128)(2,1)S(1)}, bf16[48,2048]{1,0:T(8,128)(2,1)S(1)}, u32[]{:S(2)}, u32[]{:S(2)}) collective-permute-start(bf16[48,2048]{1,0:T(8,128)(2,1)S(1)} %get-tuple-element.61), channel_id=1, source_target_pairs={{0,8},{2,10},{4,12},{6,14},{8,0},{10,2},{12,4},{14,6},{1,9},{3,11}... | collective-permute-start | bytes 589832 | tf_op jit(solution)/shard_map/ppermute | solution.py:30
  131.7 2.8 %collective-permute-done.7.refs_2_.refs_7_ = bf16[48,1024]{1,0:T(8,128)(2,1)S(1)} collective-permute-done((bf16[48,1024]{1,0:T(8,128)(2,1)S(1)}, bf16[48,1024]{1,0:T(8,128)(2,1)S(1)}, u32[]{:S(2)}, u32[]{:S(2)}) %collective-permute-start.7) | collective-permute-done | bytes 98336 | tf_op jit(solution)/shard_map/ppermute | solution.py:30
  135.7 9.5 %adapter_outputs.1 = (bf16[384,1024]{1,0:T(8,128)(2,1)S(1)}, bf16[384,1024]{1,0:T(8,128)(2,1)S(1)}) custom-call(bf16[384,128]{1,0:T(8,128)(2,1)S(1)} %get-tuple-element.90.a_ref, bf16[384,128]{1,0:T(8,128)(2,1)S(1)} %multiply_convert_fusion.b_ref, s32[384,1]{1,0:T(8,128)S(1)} %fusion.ia_ref, s32[384,1]{1,0:T(8,128)S(1)} %broadcast_in_dim.90.ib_ref, ...), custom_call_target="tpu_custom_call" | custom-call | flops 11500000256 | bytes 1 | tf_op jit(solution)/shard_map/adapter_outputs/pallas_call | solution.py:198
  147.9 3.2 %project.5 = (bf16[4,48,1024]{2,1,0:T(8,128)(2,1)S(1)}, bf16[4,48,1024]{2,1,0:T(8,128)(2,1)S(1)}) custom-call(s32[4]{0:T(128)S(1)} %pad_add_fusion.3.where_ref, bf16[8,48,1024]{2,1,0:T(8,128)(2,1)S(1)} %all-to-all-done.1.x_ref, bf16[1024,8192]{1,0:T(8,128)(2,1)} %w_ref.5, bf16[8,48,1024]{2,1,0:T(8,128)(2,1)S(1)} %bitcast.37), custom_call_target="tpu_custom_call" | custom-call | flops 3449999872 | bytes 1 | tf_op jit(solution)/shard_map/project/pallas_call | solution.py:266
  151.1 3.3 %collective-permute-start.14 = (bf16[48,2048]{1,0:T(8,128)(2,1)S(1)}, bf16[48,2048]{1,0:T(8,128)(2,1)S(1)}, u32[]{:S(2)}, u32[]{:S(2)}) collective-permute-start(bf16[48,2048]{1,0:T(8,128)(2,1)S(1)} %get-tuple-element.67), channel_id=1, source_target_pairs={{0,8},{2,10},{4,12},{6,14},{8,0},{10,2},{12,4},{14,6},{1,9},{3,11}... | collective-permute-start | bytes 589832 | tf_op jit(solution)/shard_map/ppermute | solution.py:30
  157.5 2.9 %collective-permute-start.27 = (bf16[48,1024]{1,0:T(8,128)(2,1)S(1)}, bf16[48,1024]{1,0:T(8,128)(2,1)S(1)}, u32[]{:S(2)}, u32[]{:S(2)}) collective-permute-start(bf16[48,1024]{1,0:T(8,128)(2,1)S(1)} %get-tuple-element.77), channel_id=1, source_target_pairs={{0,8},{2,10},{4,12},{6,14},{8,0},{10,2},{12,4},{14,6},{1,9},{3,11}... | collective-permute-start | bytes 294920 | tf_op jit(solution)/shard_map/ppermute | solution.py:30
  160.4 10.3 %collective-permute-done.14.refs_1_.refs_14_ = bf16[48,2048]{1,0:T(8,128)(2,1)S(1)} collective-permute-done((bf16[48,2048]{1,0:T(8,128)(2,1)S(1)}, bf16[48,2048]{1,0:T(8,128)(2,1)S(1)}, u32[]{:S(2)}, u32[]{:S(2)}) %collective-permute-start.14) | collective-permute-done | bytes 196640 | tf_op jit(solution)/shard_map/ppermute | solution.py:30
  170.7 2.4 %collective-permute-start.28 = (bf16[48,1024]{1,0:T(8,128)(2,1)S(1)}, bf16[48,1024]{1,0:T(8,128)(2,1)S(1)}, u32[]{:S(2)}, u32[]{:S(2)}) collective-permute-start(bf16[48,1024]{1,0:T(8,128)(2,1)S(1)} %get-tuple-element.78), channel_id=1, source_target_pairs={{0,12},{2,14},{4,8},{6,10},{8,4},{10,6},{12,0},{14,2},{1,13},{3,15... | collective-permute-start | bytes 294920 | tf_op jit(solution)/shard_map/ppermute | solution.py:30
  173.2 3.5 %collective-permute-start.30 = (bf16[48,1024]{1,0:T(8,128)(2,1)S(1)}, bf16[48,1024]{1,0:T(8,128)(2,1)S(1)}, u32[]{:S(2)}, u32[]{:S(2)}) collective-permute-start(bf16[48,1024]{1,0:T(8,128)(2,1)S(1)} %get-tuple-element.82), channel_id=1, source_target_pairs={{0,4},{2,6},{4,0},{6,2},{8,12},{10,14},{12,8},{14,10},{1,5},{3,7},... | collective-permute-start | bytes 294920 | tf_op jit(solution)/shard_map/ppermute | solution.py:30
  181.3 6.3 %collective-permute-done.31.refs_22_ = bf16[48,1024]{1,0:T(8,128)(2,1)S(1)} collective-permute-done((bf16[48,1024]{1,0:T(8,128)(2,1)S(1)}, bf16[48,1024]{1,0:T(8,128)(2,1)S(1)}, u32[]{:S(2)}, u32[]{:S(2)}) %collective-permute-start.31) | collective-permute-done | bytes 98336 | tf_op jit(solution)/shard_map/ppermute | solution.py:30
  (93 shorter events, 33.4 us)
Async XLA Ops:
  0.0 27.5 %all-to-all-start = ((bf16[8,48,1024]{2,1,0:T(8,128)(2,1)}), bf16[8,48,1024]{2,1,0:T(8,128)(2,1)S(1)}, u32[]{:S(2)}, u32[]{:S(2)}) async-start(bf16[8,48,1024]{2,1,0:T(8,128)(2,1)} %bitcast.39), calls=%async_computation | async-start | bytes 1572864 | tf_op jit(solution)/shard_map/all_to_all | solution.py:361
  7.3 33.6 %collective-permute-start.18 = (s32[16]{0:T(128)}, s32[16]{0:T(128)S(1)}, u32[]{:S(2)}, u32[]{:S(2)}) collective-permute-start(s32[16]{0:T(128)} %bitcast.41), channel_id=1, source_target_pairs={{0,1},{1,0},{2,3},{3,2},{4,5},{5,4},{6,7},{7,6},{8,9},{9,8},{10,11... | collective-permute-start | bytes 200 | tf_op jit(solution)/shard_map/ppermute | solution.py:30
  8.0 32.8 %collective-permute-start.17 = (s32[384]{0:T(512)S(1)}, s32[384]{0:T(512)S(1)}, u32[]{:S(2)}, u32[]{:S(2)}) collective-permute-start(s32[384]{0:T(512)S(1)} %get-tuple-element.97), channel_id=1, source_target_pairs={{0,1},{1,0},{2,3},{3,2},{4,5},{5,4},{6,7},{7,6},{8,9},{9,8},{10,11... | collective-permute-start | bytes 4616 | tf_op jit(solution)/shard_map/ppermute | solution.py:30
  36.2 23.9 %all-to-all-start.1 = ((bf16[8,48,1024]{2,1,0:T(8,128)(2,1)}), bf16[8,48,1024]{2,1,0:T(8,128)(2,1)S(1)}, u32[]{:S(2)}, u32[]{:S(2)}) async-start(bf16[8,48,1024]{2,1,0:T(8,128)(2,1)} %attend.1), calls=%async_computation.1 | async-start | bytes 1572864 | tf_op jit(solution)/shard_map/all_to_all | solution.py:393
  60.1 16.6 %collective-permute-start.16 = (bf16[384,1024]{1,0:T(8,128)(2,1)S(1)}, bf16[384,1024]{1,0:T(8,128)(2,1)S(1)}, u32[]{:S(2)}, u32[]{:S(2)}) collective-permute-start(bf16[384,1024]{1,0:T(8,128)(2,1)S(1)} %bitcast.35), channel_id=1, source_target_pairs={{0,1},{1,0},{2,3},{3,2},{4,5},{5,4},{6,7},{7,6},{8,9},{9,8},{10,11... | collective-permute-start | bytes 2359304 | tf_op jit(solution)/shard_map/ppermute | solution.py:30
  86.4 14.5 %collective-permute-start = (bf16[4,48,1024]{2,1,0:T(8,128)(2,1)S(1)}, bf16[4,48,1024]{2,1,0:T(8,128)(2,1)S(1)}, u32[]{:S(2)}, u32[]{:S(2)}) collective-permute-start(bf16[4,48,1024]{2,1,0:T(8,128)(2,1)S(1)} %get-tuple-element.46), channel_id=1, source_target_pairs={{0,2},{2,0},{4,6},{6,4},{8,10},{10,8},{12,14},{14,12},{1,3},{3,1},... | collective-permute-start | bytes 1179656 | tf_op jit(solution)/shard_map/ppermute | solution.py:30
  87.9 12.6 %collective-permute-start.20 = (bf16[384,128]{1,0:T(8,128)(2,1)S(1)}, bf16[384,128]{1,0:T(8,128)(2,1)S(1)}, u32[]{:S(2)}, u32[]{:S(2)}) collective-permute-start(bf16[384,128]{1,0:T(8,128)(2,1)S(1)} %fusion.3), channel_id=1, source_target_pairs={{0,2},{2,0},{4,6},{6,4},{8,10},{10,8},{12,14},{14,12},{1,3},{3,1},... | collective-permute-start | bytes 294920 | tf_op jit(solution)/shard_map/ppermute | solution.py:30
  88.9 20.0 %collective-permute-start.4 = (bf16[4,48,1024]{2,1,0:T(8,128)(2,1)S(1)}, bf16[4,48,1024]{2,1,0:T(8,128)(2,1)S(1)}, u32[]{:S(2)}, u32[]{:S(2)}) collective-permute-start(bf16[4,48,1024]{2,1,0:T(8,128)(2,1)S(1)} %get-tuple-element.52), channel_id=1, source_target_pairs={{0,2},{2,0},{4,6},{6,4},{8,10},{10,8},{12,14},{14,12},{1,3},{3,1},... | collective-permute-start | bytes 1179656 | tf_op jit(solution)/shard_map/ppermute | solution.py:30
  90.0 35.8 %collective-permute-start.8 = (bf16[4,48,2048]{2,1,0:T(8,128)(2,1)S(1)}, bf16[4,48,2048]{2,1,0:T(8,128)(2,1)S(1)}, u32[]{:S(2)}, u32[]{:S(2)}) collective-permute-start(bf16[4,48,2048]{2,1,0:T(8,128)(2,1)S(1)} %get-tuple-element.58), channel_id=1, source_target_pairs={{0,2},{2,0},{4,6},{6,4},{8,10},{10,8},{12,14},{14,12},{1,3},{3,1},... | collective-permute-start | bytes 2359304 | tf_op jit(solution)/shard_map/ppermute | solution.py:30
  90.9 54.3 %collective-permute-start.12 = (bf16[4,48,2048]{2,1,0:T(8,128)(2,1)S(1)}, bf16[4,48,2048]{2,1,0:T(8,128)(2,1)S(1)}, u32[]{:S(2)}, u32[]{:S(2)}) collective-permute-start(bf16[4,48,2048]{2,1,0:T(8,128)(2,1)S(1)} %get-tuple-element.64), channel_id=1, source_target_pairs={{0,2},{2,0},{4,6},{6,4},{8,10},{10,8},{12,14},{14,12},{1,3},{3,1},... | collective-permute-start | bytes 2359304 | tf_op jit(solution)/shard_map/ppermute | solution.py:30
  101.0 16.2 %collective-permute-start.1 = (bf16[48,1024]{1,0:T(8,128)(2,1)S(1)}, bf16[48,1024]{1,0:T(8,128)(2,1)S(1)}, u32[]{:S(2)}, u32[]{:S(2)}) collective-permute-start(bf16[48,1024]{1,0:T(8,128)(2,1)S(1)} %get-tuple-element.48), channel_id=1, source_target_pairs={{0,4},{2,6},{4,0},{6,2},{8,12},{10,14},{12,8},{14,10},{1,5},{3,7},... | collective-permute-start | bytes 294920 | tf_op jit(solution)/shard_map/ppermute | solution.py:30
  105.2 13.8 %collective-permute-start.2 = (bf16[48,1024]{1,0:T(8,128)(2,1)S(1)}, bf16[48,1024]{1,0:T(8,128)(2,1)S(1)}, u32[]{:S(2)}, u32[]{:S(2)}) collective-permute-start(bf16[48,1024]{1,0:T(8,128)(2,1)S(1)} %get-tuple-element.49), channel_id=1, source_target_pairs={{0,8},{2,10},{4,12},{6,14},{8,0},{10,2},{12,4},{14,6},{1,9},{3,11}... | collective-permute-start | bytes 294920 | tf_op jit(solution)/shard_map/ppermute | solution.py:30
  117.2 33.9 %collective-permute-start.25 = (bf16[4,48,1024]{2,1,0:T(8,128)(2,1)S(1)}, bf16[4,48,1024]{2,1,0:T(8,128)(2,1)S(1)}, u32[]{:S(2)}, u32[]{:S(2)}) collective-permute-start(bf16[4,48,1024]{2,1,0:T(8,128)(2,1)S(1)} %get-tuple-element.74), channel_id=1, source_target_pairs={{0,2},{2,0},{4,6},{6,4},{8,10},{10,8},{12,14},{14,12},{1,3},{3,1},... | collective-permute-start | bytes 1179656 | tf_op jit(solution)/shard_map/ppermute | solution.py:30
  128.4 26.0 %collective-permute-start.9 = (bf16[48,2048]{1,0:T(8,128)(2,1)S(1)}, bf16[48,2048]{1,0:T(8,128)(2,1)S(1)}, u32[]{:S(2)}, u32[]{:S(2)}) collective-permute-start(bf16[48,2048]{1,0:T(8,128)(2,1)S(1)} %get-tuple-element.60), channel_id=1, source_target_pairs={{0,4},{2,6},{4,0},{6,2},{8,12},{10,14},{12,8},{14,10},{1,5},{3,7},... | collective-permute-start | bytes 589832 | tf_op jit(solution)/shard_map/ppermute | solution.py:30
  128.8 26.7 %collective-permute-start.10 = (bf16[48,2048]{1,0:T(8,128)(2,1)S(1)}, bf16[48,2048]{1,0:T(8,128)(2,1)S(1)}, u32[]{:S(2)}, u32[]{:S(2)}) collective-permute-start(bf16[48,2048]{1,0:T(8,128)(2,1)S(1)} %get-tuple-element.61), channel_id=1, source_target_pairs={{0,8},{2,10},{4,12},{6,14},{8,0},{10,2},{12,4},{14,6},{1,9},{3,11}... | collective-permute-start | bytes 589832 | tf_op jit(solution)/shard_map/ppermute | solution.py:30
  134.6 22.7 %collective-permute-start.11 = (bf16[48,2048]{1,0:T(8,128)(2,1)S(1)}, bf16[48,2048]{1,0:T(8,128)(2,1)S(1)}, u32[]{:S(2)}, u32[]{:S(2)}) collective-permute-start(bf16[48,2048]{1,0:T(8,128)(2,1)S(1)} %get-tuple-element.62), channel_id=1, source_target_pairs={{0,12},{2,14},{4,8},{6,10},{8,4},{10,6},{12,0},{14,2},{1,13},{3,15... | collective-permute-start | bytes 589832 | tf_op jit(solution)/shard_map/ppermute | solution.py:30
  151.1 19.6 %collective-permute-start.14 = (bf16[48,2048]{1,0:T(8,128)(2,1)S(1)}, bf16[48,2048]{1,0:T(8,128)(2,1)S(1)}, u32[]{:S(2)}, u32[]{:S(2)}) collective-permute-start(bf16[48,2048]{1,0:T(8,128)(2,1)S(1)} %get-tuple-element.67), channel_id=1, source_target_pairs={{0,8},{2,10},{4,12},{6,14},{8,0},{10,2},{12,4},{14,6},{1,9},{3,11}... | collective-permute-start | bytes 589832 | tf_op jit(solution)/shard_map/ppermute | solution.py:30
  154.4 18.7 %collective-permute-start.15 = (bf16[48,2048]{1,0:T(8,128)(2,1)S(1)}, bf16[48,2048]{1,0:T(8,128)(2,1)S(1)}, u32[]{:S(2)}, u32[]{:S(2)}) collective-permute-start(bf16[48,2048]{1,0:T(8,128)(2,1)S(1)} %get-tuple-element.68), channel_id=1, source_target_pairs={{0,12},{2,14},{4,8},{6,10},{8,4},{10,6},{12,0},{14,2},{1,13},{3,15... | collective-permute-start | bytes 589832 | tf_op jit(solution)/shard_map/ppermute | solution.py:30
  155.5 17.5 %collective-permute-start.29 = (bf16[4,48,1024]{2,1,0:T(8,128)(2,1)S(1)}, bf16[4,48,1024]{2,1,0:T(8,128)(2,1)S(1)}, u32[]{:S(2)}, u32[]{:S(2)}) collective-permute-start(bf16[4,48,1024]{2,1,0:T(8,128)(2,1)S(1)} %get-tuple-element.80), channel_id=1, source_target_pairs={{0,2},{2,0},{4,6},{6,4},{8,10},{10,8},{12,14},{14,12},{1,3},{3,1},... | collective-permute-start | bytes 1179656 | tf_op jit(solution)/shard_map/ppermute | solution.py:30
  157.4 20.3 %collective-permute-start.26 = (bf16[48,1024]{1,0:T(8,128)(2,1)S(1)}, bf16[48,1024]{1,0:T(8,128)(2,1)S(1)}, u32[]{:S(2)}, u32[]{:S(2)}) collective-permute-start(bf16[48,1024]{1,0:T(8,128)(2,1)S(1)} %get-tuple-element.76), channel_id=1, source_target_pairs={{0,4},{2,6},{4,0},{6,2},{8,12},{10,14},{12,8},{14,10},{1,5},{3,7},... | collective-permute-start | bytes 294920 | tf_op jit(solution)/shard_map/ppermute | solution.py:30
  157.5 23.8 %collective-permute-start.27 = (bf16[48,1024]{1,0:T(8,128)(2,1)S(1)}, bf16[48,1024]{1,0:T(8,128)(2,1)S(1)}, u32[]{:S(2)}, u32[]{:S(2)}) collective-permute-start(bf16[48,1024]{1,0:T(8,128)(2,1)S(1)} %get-tuple-element.77), channel_id=1, source_target_pairs={{0,8},{2,10},{4,12},{6,14},{8,0},{10,2},{12,4},{14,6},{1,9},{3,11}... | collective-permute-start | bytes 294920 | tf_op jit(solution)/shard_map/ppermute | solution.py:30
  170.7 10.6 %collective-permute-start.28 = (bf16[48,1024]{1,0:T(8,128)(2,1)S(1)}, bf16[48,1024]{1,0:T(8,128)(2,1)S(1)}, u32[]{:S(2)}, u32[]{:S(2)}) collective-permute-start(bf16[48,1024]{1,0:T(8,128)(2,1)S(1)} %get-tuple-element.78), channel_id=1, source_target_pairs={{0,12},{2,14},{4,8},{6,10},{8,4},{10,6},{12,0},{14,2},{1,13},{3,15... | collective-permute-start | bytes 294920 | tf_op jit(solution)/shard_map/ppermute | solution.py:30
  176.7 10.9 %collective-permute-start.31 = (bf16[48,1024]{1,0:T(8,128)(2,1)S(1)}, bf16[48,1024]{1,0:T(8,128)(2,1)S(1)}, u32[]{:S(2)}, u32[]{:S(2)}) collective-permute-start(bf16[48,1024]{1,0:T(8,128)(2,1)S(1)} %get-tuple-element.83), channel_id=1, source_target_pairs={{0,8},{2,10},{4,12},{6,14},{8,0},{10,2},{12,4},{14,6},{1,9},{3,11}... | collective-permute-start | bytes 294920 | tf_op jit(solution)/shard_map/ppermute | solution.py:30
  177.7 10.0 %collective-permute-start.32 = (bf16[48,1024]{1,0:T(8,128)(2,1)S(1)}, bf16[48,1024]{1,0:T(8,128)(2,1)S(1)}, u32[]{:S(2)}, u32[]{:S(2)}) collective-permute-start(bf16[48,1024]{1,0:T(8,128)(2,1)S(1)} %get-tuple-element.84), channel_id=1, source_target_pairs={{0,12},{2,14},{4,8},{6,10},{8,4},{10,6},{12,0},{14,2},{1,13},{3,15... | collective-permute-start | bytes 294920 | tf_op jit(solution)/shard_map/ppermute | solution.py:30
  (14 other events, 106.5 us)

commit v3 on v2

--- a/solution.py
+++ b/solution.py
@@ -19,11 +19,21 @@
 VMEM_LIMIT = 48 * 1024 * 1024
 
 
-ADD_US = 8.7
+COSTS = {"project": 3.0, "inner": 9.0, "adapter": 10.0, "add": 8.7, "pair": 0.5, "pack": 0.5}
+AFTER = {
+    "project": {1: [("project", 0)], 2: [("add", 0), ("project", 1)], 3: [("add", 2)]},
+    "inner": {0: [("project", 1)]},
+    "route": {0: [("sum", 0)], 1: [("z", 0)], 2: [("z", 1)]},
+    "sum": {1: [("project", 2)]},
+    "delta": {0: [("add", 1)]},
+}
+LAYOUT = (2,)
+CUTS = (1, 2)
+HOPS = False
 
 
 def cost(us):
-    return pl.CostEstimate(flops=int(us * 1.15e9), bytes_accessed=1, transcendentals=0)
+    return pl.CostEstimate(flops=max(1, int(us * 1.15e9)), bytes_accessed=1, transcendentals=0)
 
 
 def permute_xor(x, axis, size, k):
@@ -160,7 +170,7 @@
         out_shape=[jax.ShapeDtypeStruct((rows, rank), BF16)] * 2,
         scratch_shapes=[pltpu.VMEM((rows, rank), F32)] * 2,
         compiler_params=pltpu.CompilerParams(vmem_limit_bytes=VMEM_LIMIT),
-        cost_estimate=cost(9),
+        cost_estimate=cost(COSTS["inner"]),
         name="inner_products",
     )(rows_a, rows_b, ids_a, ids_b, down, *after)
 
@@ -210,7 +220,7 @@
         out_shape=[jax.ShapeDtypeStruct((rows, width), BF16)] * 2,
         scratch_shapes=[pltpu.VMEM((rows, width), F32)] * 2,
         compiler_params=pltpu.CompilerParams(vmem_limit_bytes=VMEM_LIMIT),
-        cost_estimate=cost(10),
+        cost_estimate=cost(COSTS["adapter"]),
         name="adapter_outputs",
     )(scaled_a, scaled_b, ids_a, ids_b, up, *after)
 
@@ -230,7 +240,8 @@
 
     result = jnp.dot(scratch[...], w_ref[...], preferred_element_type=F32)
     if with_delta:
-        result = result + jnp.concatenate([refs[0][i].astype(F32) for i in blocks], axis=0)
+        for d_ref in refs[:2]:
+            result = result + jnp.concatenate([d_ref[i].astype(F32) for i in blocks], axis=0)
     result = result.astype(BF16)
     for c, (first, count) in enumerate(spans):
 
@@ -244,10 +255,10 @@
 def project(y, z, starts, widths, x, weight, delta=None, after=()):
     n, rows, depth = x.shape
     tile = min(512, min(widths))
-    spans, table = [], [y, z]
-    for start, width in zip(starts, widths):
-        spans.append((len(table) - 2, width // tile))
-        table += [start // tile + i for i in range(width // tile)]
+    spans, table, first = [], [y, z] + [start // tile for start in starts], 0
+    for width in widths:
+        spans.append((first, width // tile))
+        first += width // tile
     steps = len(table) - 2
     ins = [
         pl.BlockSpec((n, rows, depth), lambda i, w: (0, 0, 0)),
@@ -255,8 +266,8 @@
     ]
     args = [x, weight]
     if delta is not None:
-        ins.append(pl.BlockSpec((n, rows, tile), lambda i, w: (0, 0, i)))
-        args.append(delta)
+        ins += [pl.BlockSpec((n, rows, tile), lambda i, w: (0, 0, i))] * 2
+        args += delta
 
     def out_spec(first, count):
         return pl.BlockSpec(
@@ -274,29 +285,74 @@
         ),
         out_shape=[jax.ShapeDtypeStruct((n // 2, rows, w), BF16) for w in widths for _ in range(2)],
         compiler_params=pltpu.CompilerParams(vmem_limit_bytes=VMEM_LIMIT),
-        cost_estimate=cost(1.5 * steps),
+        cost_estimate=cost(COSTS["project"] * steps),
         name="project",
     )(jnp.stack(table), *args, *after)
     return outs[::2], outs[1::2]
 
 
-def add_kernel(near_ref, far_ref, *refs):
-    for j, o_ref in enumerate(refs[-near_ref.shape[0] :]):
-        o_ref[...] = (near_ref[j].astype(F32) + far_ref[j].astype(F32)).astype(BF16)
+def add_pair_kernel(a_ref, b_ref, *refs):
+    total = a_ref[...].astype(F32) + b_ref[...].astype(F32)
+    refs[-2][...] = total
+    refs[-1][...] = total.astype(BF16)
+
+
+def add_pair(a, b, after):
+    vmem = pl.BlockSpec(memory_space=pltpu.VMEM)
+    return pl.pallas_call(
+        add_pair_kernel,
+        in_specs=[vmem] * 2 + [pl.BlockSpec(memory_space=pl.ANY)] * len(after),
+        out_specs=[vmem] * 2,
+        out_shape=[jax.ShapeDtypeStruct(a.shape, F32), jax.ShapeDtypeStruct(a.shape, BF16)],
+        compiler_params=pltpu.CompilerParams(vmem_limit_bytes=VMEM_LIMIT),
+        cost_estimate=cost(COSTS["pair"]),
+        name="add_pair",
+    )(a, b, *after)
+
+
+def add_kernel(cuts, near_ref, far_ref, *refs):
+    first = 0
+    for o_ref, cut in zip(refs[-len(cuts) :], cuts):
+        o_ref[...] = (near_ref[first : first + cut].astype(F32) + far_ref[first : first + cut].astype(F32)).astype(BF16)
+        first += cut
 
 
 def add_sides(near, far, after):
     nz, rows, width = near.shape
+    cuts = [1] * nz
+    if HOPS:
+        cuts = [1]
+        while sum(cuts) < nz:
+            cuts.append(sum(cuts))
     vmem = pl.BlockSpec(memory_space=pltpu.VMEM)
     return pl.pallas_call(
-        add_kernel,
+        functools.partial(add_kernel, cuts),
         in_specs=[vmem] * 2 + [pl.BlockSpec(memory_space=pl.ANY)] * len(after),
-        out_specs=[vmem] * nz,
-        out_shape=[jax.ShapeDtypeStruct((rows, width), BF16)] * nz,
-        compiler_params=pltpu.CompilerParams(vmem_limit_bytes=VMEM_LIMIT),
-        cost_estimate=cost(ADD_US * width * nz / 4096),
+        out_specs=[vmem] * len(cuts),
+        out_shape=[jax.ShapeDtypeStruct((cut, rows, width), BF16) for cut in cuts],
+        compiler_params=pltpu.CompilerParams(vmem_limit_bytes=VMEM_LIMIT),
+        cost_estimate=cost(COSTS["add"] * width * nz / 4096),
         name="add_sides",
     )(near, far, *after)
+
+
+def pack_kernel(picks, *refs):
+    for i, (ref, place) in enumerate(picks):
+        refs[-1][i] = refs[ref][place]
+
+
+def pack(arrays, picks, after):
+    rows, width = arrays[0].shape[1:]
+    vmem = pl.BlockSpec(memory_space=pltpu.VMEM)
+    return pl.pallas_call(
+        functools.partial(pack_kernel, picks),
+        in_specs=[vmem] * len(arrays) + [pl.BlockSpec(memory_space=pl.ANY)] * len(after),
+        out_specs=vmem,
+        out_shape=jax.ShapeDtypeStruct((len(picks), rows, width), BF16),
+        compiler_params=pltpu.CompilerParams(vmem_limit_bytes=VMEM_LIMIT),
+        cost_estimate=cost(COSTS["pack"]),
+        name="pack",
+    )(*arrays, *after)
 
 
 def finish_kernel(plan, width, place_ref, res_ref, *refs):
@@ -306,14 +362,17 @@
         side = y ^ half
         place = pl.ds(pl.multiple_of(((z ^ group) * 2 + side) * width, width), width)
         total = res_ref[:, place].astype(F32)
-        for kind, first in terms:
-            if kind == "whole":
-                term = refs[first][...]
-            elif kind == "half":
-                term = refs[first][:, pl.ds(pl.multiple_of(side * width, width), width)]
-            else:
-                term = jnp.where(side == 0, refs[first[0]][...], refs[first[1]][...])
-            total = total + term.astype(F32)
+        for term in terms:
+            ref, block, k = term[0]
+            value = refs[ref][block, :, k * width : (k + 1) * width]
+            if len(term) == 2:
+                if term[1] == (ref, block, k + 1):
+                    first = pl.multiple_of((side + k) * width, width)
+                    value = refs[ref][block, :, pl.ds(first, width)]
+                else:
+                    ref, block, k = term[1]
+                    value = jnp.where(side == 0, value, refs[ref][block, :, k * width : (k + 1) * width])
+            total = total + value.astype(F32)
         o_ref[:, place] = total.astype(BF16)
 
 
@@ -394,54 +453,156 @@
     x_rows = x.reshape(rows_dp, width)
     x_other = permute_xor(x_rows, "dp", n_dp, 1)
 
-    chunks = [(nz - 1, 0, width), (nz - 1, width, width)]
-    chunks += [(jz, 0, 2 * width) for jz in reversed(range(1, nz - 1))]
-    chunks += [(0, (1 - y) * width, width), (0, y * width, width)]
+    blocks = [(jz, b) for jz in reversed(range(1, nz)) for b in range(2)]
+    chunks, left = [], list(blocks)
+    for size in LAYOUT:
+        chunks.append(left[:size])
+        left = left[size:]
+    while left:
+        chunks.append(left[: LAYOUT[-1]])
+        left = left[LAYOUT[-1] :]
+    chunks += [[(0, 1)], [(0, 0)]]
     count = len(chunks)
-
-    starts = [(z ^ jz) * 2 * width + low for jz, low, _ in chunks]
-    widths = [size for _, _, size in chunks]
+    where = {block: (i, k) for i, chunk in enumerate(chunks) for k, block in enumerate(chunk)}
+    def start_of(block):
+        jz, b = block
+        return (z ^ jz) * 2 * width + (b if jz else y ^ b) * width
 
     def across_y(x):
         return permute_xor(x, "tp", n, 1)
 
-    def along_z(near, far, after):
-        total = add_sides(near, far, after)
-        return [total[0]] + [permute_xor(total[j], "tp", n, 2 * j) for j in range(1, nz)]
-
-    near, far = project(y, z, starts[:1], widths[:1], x, output_weight)
-    more, others = project(y, z, starts[1:-1], widths[1:-1], x, output_weight, after=[near[0]])
-    near += more
-    far = [across_y(v) for v in far + others]
-    inner_a, inner_b = inner_products(x_rows, x_other, ids_a, ids_b, adapter_down, [near[1]])
-    received = []
-    for i in range(count - 2):
-        received.append(along_z(near[i], far[i], received[i - 2][1:] if i >= 2 else []))
-
-    inner = inner_a.astype(F32) + permute_xor(inner_b, "dp", n_dp, 1).astype(F32)
-    step = 1
-    while step < n:
-        inner = inner + permute_xor(inner.astype(BF16), "tp", n, step).astype(F32)
-        step *= 2
-    inner = inner.astype(BF16)
-    inner_other = permute_xor(inner, "dp", n_dp, 1)
-    delta_a, delta_b = adapter_outputs(
-        (inner.astype(F32) * factor_a).astype(BF16),
-        (inner_other.astype(F32) * factor_b).astype(BF16),
-        ids_a,
-        ids_b,
-        adapter_up,
-        received[1][1:],
-    )
-    delta = (delta_a.astype(F32) + permute_xor(delta_b, "dp", n_dp, 1).astype(F32)).astype(BF16)
-    delta = delta.reshape(n, rows, width)
-
-    more, others = project(y, z, starts[-1:], widths[-1:], x, output_weight, delta)
-    received.append(along_z(more[0], far[-1], received[-2][1:]))
-    received.append(along_z(near[-1], across_y(others[0]), received[-2][1:]))
-
-    slots = {(i, j): i * nz + j for i in range(count) for j in range(nz)}
-    arrays = [received[i][j] for i in range(count) for j in range(nz)]
+    class Route:
+        def __init__(self, near, far, after):
+            self.held = list(add_sides(near, far, after))
+            self.first = self.held[0]
+            self.have = {(0, 0): (0, 0)}
+            self.step = 0
+            if not HOPS:
+                for j in range(1, nz):
+                    self.have[j, 0] = (j, 0)
+                    self.held[j] = permute_xor(self.held[j], "tp", n, 2 * j)
+                return
+            for j in range(1, nz):
+                bit = j.bit_length() - 1
+                self.have[0, j] = (bit + 1, j - (1 << bit))
+            self.step = nz // 2
+            self.send(self.held[-1], [(0, j) for j in range(nz // 2, nz)])
+
+        def send(self, array, going):
+            got = permute_xor(array, "tp", n, 2 * self.step)
+            for key in going:
+                del self.have[key]
+            for i, (source, left) in enumerate(going):
+                self.have[source ^ self.step, left ^ self.step] = (len(self.held), i)
+            self.held.append(got)
+            self.step //= 2
+
+        def forward(self, after):
+            going = sorted(key for key in self.have if key[1] & self.step)
+            used = sorted({self.have[key][0] for key in going})
+            picks = [(used.index(self.have[key][0]), self.have[key][1]) for key in going]
+            array = pack([self.held[u] for u in used], picks, after)
+            self.send(array, going)
+            return array
+
+    made = {}
+
+    def get(name, index=0):
+        if (name, index) not in made:
+            made[name, index] = RULES[name](index)
+        return made[name, index]
+
+    def waits(name, index=0):
+        out = []
+        for other in AFTER.get(name, {}).get(index, []):
+            out += TOKENS[other[0]](*other[1:])
+        return out
+
+    bounds = list(zip((0,) + CUTS, CUTS + (count - 1,)))
+    bounds = [(a, min(b, count - 1)) for a, b in bounds if a < min(b, count - 1)]
+
+    def rule_project(k):
+        if k == len(bounds):
+            first, end, delta = count - 1, count, get("delta")
+        else:
+            first, end, delta = *bounds[k], None
+        wide = [len(chunk) * width for chunk in chunks[first:end]]
+        tile = min(512, width)
+        cols = [start_of(block) + i for chunk in chunks[first:end] for block in chunk for i in range(0, width, tile)]
+        near, far = project(y, z, cols, wide, x, output_weight, delta, waits("project", k))
+        for i in range(first, end):
+            made["near", i] = near[i - first]
+            made["far", i] = across_y(far[i - first])
+        return near[0]
+
+    def rule_side(name):
+        def rule(i):
+            k = next((k for k, (a, b) in enumerate(bounds) if a <= i < b), len(bounds))
+            get("project", k)
+            return made[name, i]
+
+        return rule
+
+    def rule_route(i):
+        near = far = i
+        if i == count - 2:
+            near = count - 1
+        elif i == count - 1:
+            near = count - 2
+        return Route(get("near", near), get("far", far), waits("route", i))
+
+    def rule_inner(_):
+        a, b = inner_products(x_rows, x_other, ids_a, ids_b, adapter_down, waits("inner"))
+        return a, permute_xor(b, "dp", n_dp, 1)
+
+    def rule_sum(k):
+        if k == 0:
+            a, b = get("inner")
+        else:
+            a, b = get("sum", k - 1)
+            b = permute_xor(b, "tp", n, 1 << (k - 1))
+        return add_pair(a, b, waits("sum", k))
+
+    def rule_delta(_):
+        inner, sent = get("sum", n.bit_length() - 1)
+        inner_other = permute_xor(sent, "dp", n_dp, 1)
+        delta_a, delta_b = adapter_outputs(
+            (inner * factor_a).astype(BF16),
+            (inner_other.astype(F32) * factor_b).astype(BF16),
+            ids_a,
+            ids_b,
+            adapter_up,
+            waits("delta"),
+        )
+        return [v.reshape(n, rows, width) for v in (delta_a, permute_xor(delta_b, "dp", n_dp, 1))]
+
+    RULES = {
+        "project": rule_project,
+        "near": rule_side("near"),
+        "far": rule_side("far"),
+        "route": rule_route,
+        "inner": rule_inner,
+        "sum": rule_sum,
+        "delta": rule_delta,
+    }
+    TOKENS = {
+        "project": lambda i: [get("project", min(i, len(bounds) - 1))],
+        "far": lambda i: [get("far", i)],
+        "add": lambda i: [get("route", min(i, count - 3)).first],
+        "z": lambda i: get("route", min(i, count - 3)).held[1:],
+        "inner": lambda: [get("inner")[0]],
+        "sum": lambda k: [get("sum", k)[0]],
+        "delta": lambda: [get("delta")[0]],
+    }
+    routes = [get("route", i) for i in range(count)]
+    for route in routes:
+        while route.step:
+            route.forward([])
+
+    arrays, offsets = [], []
+    for route in routes:
+        offsets.append(len(arrays))
+        arrays += route.held
     plan = []
     for group in range(nz):
         for half in range(2):
@@ -449,13 +610,23 @@
             for j in range(nz):
                 jz = group ^ j
                 if jz == 0:
-                    terms.append(("whole", slots[count - 2 + half, j]))
-                elif jz == nz - 1:
-                    terms.append(("pick", (slots[0, j], slots[1, j])))
-                else:
-                    terms.append(("half", slots[nz - jz, j]))
+                    i = count - 2 + half
+                    held, block = routes[i].have[j, 0]
+                    terms.append([(offsets[i] + held, block, 0)])
+                    continue
+                term = []
+                for b in range(2):
+                    i, k = where[jz, b]
+                    held, block = routes[i].have[j, 0]
+                    term.append((offsets[i] + held, block, k))
+                terms.append(term)
             plan.append((group, half, terms))
-    return finish(jnp.stack([z, y]), residual[0], plan, width, arrays)[None]
+    needed = sorted({t[0] for _, _, terms in plan for term in terms for t in term})
+    plan = [
+        (g, h, [[(needed.index(r), block, k) for r, block, k in term] for term in terms])
+        for g, h, terms in plan
+    ]
+    return finish(jnp.stack([z, y]), residual[0], plan, width, [arrays[r] for r in needed])[None]
 
 
 def solution(mesh):

time: 190 us -> 173 us (0.911)
  waiting for transfers between devices: 88.5 us -> 67.9 us
  starting transfers between devices: 45.3 us -> 47.3 us
    ppermute x33 -> x29, waiting for transfers between devices: 53.6 us -> 33.2 us  [permute_xor(): return lax.ppermute(x, axis, [(i, i ^ k) for i in range(size)])]
    ppermute x33 -> x29, starting transfers between devices: 34.3 us -> 36.3 us  [permute_xor(): return lax.ppermute(x, axis, [(i, i ^ k) for i in range(size)])]
    pallas_call x3 -> x4, Pallas kernels: 19.8 us -> 20.6 us  [project(): pl.pallas_call(functools.partial(project_kernel, spans, delta is not None...]
  transfers between devices with their start and end apart: 35 -> 31, of which waited for: 15 -> 11; matrix products, arithmetic and copies ran while one was open for 3% -> 3% of each run, Pallas kernels for 20% -> 28%
where the time goes in v3:
time: 173 us; the launch traced here: 172 us
  waiting for transfers between devices  67.9 us (39%)
  Pallas kernels  51.1 us (30%)
  starting transfers between devices  47.3 us (27%)
  local copies, waits for them, and re-layouts  2.86 us (2%)
  other arithmetic  2.4 us (1%)
    ppermute x29, starting transfers between devices, permute_xor(): return lax.ppermute(x, axis, [(i, i ^ k) for i in range(size)])  36.3 us
    ppermute x29, waiting for transfers between devices, permute_xor(): return lax.ppermute(x, axis, [(i, i ^ k) for i in range(size)])  33.2 us
    pallas_call x4, Pallas kernels, project(): pl.pallas_call(functools.partial(project_kernel, spans, delta is not None...  20.6 us
    all_to_all x1, waiting for transfers between devices, shards(): x = lax.all_to_all(attended, 'tp', 0, 0)  18.6 us
    all_to_all x1, waiting for transfers between devices, shards(): q = lax.all_to_all(queries[0].reshape(n, rows, width), 'tp', 0, 0)  16.1 us
    pallas_call x1, Pallas kernels, adapter_outputs(): pl.pallas_call(functools.partial(delta_kernel, per), grid=(owned // per,)...  9.59 us
    pallas_call x1, Pallas kernels, inner_products(): pl.pallas_call(functools.partial(inner_kernel, per), grid=(owned // per,)...  9.19 us
    pallas_call x1, Pallas kernels, attend(): pl.pallas_call(functools.partial(attend_kernel, n), grid=(rows // ROW_BLO...  8.71 us
  transfers between devices with their start and end apart: 31, of which 11 were waited for; matrix products, arithmetic and copies ran while one was open for 3% of the time, Pallas kernels for 28%

profile of v3, /device:TPU:0, one launch (start us, length us, event | category | flops | bytes accessed | tf_op | source)
XLA Modules:
  0.0 172.2 jit_solution(9996736977349094)
XLA Ops:
  0.0 7.3 %all-to-all-start = ((bf16[8,48,1024]{2,1,0:T(8,128)(2,1)}), bf16[8,48,1024]{2,1,0:T(8,128)(2,1)S(1)}, u32[]{:S(2)}, u32[]{:S(2)}) async-start(bf16[8,48,1024]{2,1,0:T(8,128)(2,1)} %bitcast.41), calls=%async_computation | async-start | bytes 1572864 | tf_op jit(solution)/shard_map/all_to_all | solution.py:420
  11.4 16.1 %all-to-all-done.q_ref = bf16[8,48,1024]{2,1,0:T(8,128)(2,1)S(1)} async-done(((bf16[8,48,1024]{2,1,0:T(8,128)(2,1)}), bf16[8,48,1024]{2,1,0:T(8,128)(2,1)S(1)}, u32[]{:S(2)}, u32[]{:S(2)}) %all-to-all-start) | async-done | bytes 786464 | tf_op jit(solution)/shard_map/all_to_all | solution.py:420
  27.5 8.7 %attend.1 = bf16[8,48,1024]{2,1,0:T(8,128)(2,1)} custom-call(bf16[8,48,1024]{2,1,0:T(8,128)(2,1)S(1)} %all-to-all-done.q_ref, bf16[48,64,1024]{2,1,0:T(8,128)(2,1)} %bitcast.45, bf16[48,64,1024]{2,1,0:T(8,128)(2,1)} %bitcast.46, bf16[48,1024]{1,0:T(8,128)(2,1)S(1)} %get-tuple-element.101.fk_ref, bf16[48,1024]{1,0:T(8,128)(2,1)S(1)} %get-tuple-element.100.fv_ref, ...), custom_call_target="tpu_custom_call" | custom-call | flops 10350000128 | bytes 1 | tf_op jit(solution)/shard_map/attend/pallas_call | solution.py:110
  36.2 3.7 %all-to-all-start.1 = ((bf16[8,48,1024]{2,1,0:T(8,128)(2,1)}), bf16[8,48,1024]{2,1,0:T(8,128)(2,1)S(1)}, u32[]{:S(2)}, u32[]{:S(2)}) async-start(bf16[8,48,1024]{2,1,0:T(8,128)(2,1)} %attend.1), calls=%async_computation.1 | async-start | bytes 1572864 | tf_op jit(solution)/shard_map/all_to_all | solution.py:452
  41.5 18.6 %all-to-all-done.1.x_ref = bf16[8,48,1024]{2,1,0:T(8,128)(2,1)S(1)} async-done(((bf16[8,48,1024]{2,1,0:T(8,128)(2,1)}), bf16[8,48,1024]{2,1,0:T(8,128)(2,1)S(1)}, u32[]{:S(2)}, u32[]{:S(2)}) %all-to-all-start.1) | async-done | bytes 786464 | tf_op jit(solution)/shard_map/all_to_all | solution.py:452
  60.1 5.1 %project.4 = (bf16[4,48,2048]{2,1,0:T(8,128)(2,1)S(1)}, bf16[4,48,2048]{2,1,0:T(8,128)(2,1)S(1)}) custom-call(s32[6]{0:T(128)S(1)} %stack.84.where_ref, bf16[8,48,1024]{2,1,0:T(8,128)(2,1)S(1)} %all-to-all-done.1.x_ref, bf16[1024,8192]{1,0:T(8,128)(2,1)} %w_ref.7), custom_call_target="tpu_custom_call" | custom-call | flops 13799999488 | bytes 1 | tf_op jit(solution)/shard_map/project/pallas_call | solution.py:277
  66.7 5.1 %project.5 = (bf16[4,48,2048]{2,1,0:T(8,128)(2,1)S(1)}, bf16[4,48,2048]{2,1,0:T(8,128)(2,1)S(1)}) custom-call(s32[6]{0:T(128)S(1)} %stack.89.where_ref, bf16[8,48,1024]{2,1,0:T(8,128)(2,1)S(1)} %all-to-all-done.1.x_ref, bf16[1024,8192]{1,0:T(8,128)(2,1)} %w_ref.7, bf16[4,48,2048]{2,1,0:T(8,128)(2,1)S(1)} %get-tuple-element.47.refs_0_.near_ref), custom_call_target="tpu_custom_call" | custom-call | flops 13799999488 | bytes 1 | tf_op jit(solution)/shard_map/project/pallas_call | solution.py:277
  71.8 9.2 %inner_products.1 = (bf16[384,128]{1,0:T(8,128)(2,1)S(1)}, bf16[384,128]{1,0:T(8,128)(2,1)S(1)}) custom-call(bf16[384,1024]{1,0:T(8,128)(2,1)S(1)} %bitcast.37, bf16[384,1024]{1,0:T(8,128)(2,1)S(1)} %collective-permute-done.1.b_ref, s32[384,1]{1,0:T(8,128)S(1)} %fusion.ia_ref, s32[384,1]{1,0:T(8,128)S(1)} %broadcast_in_dim.90.ib_ref, ...), custom_call_target="tpu_custom_call" | custom-call | flops 10350000128 | bytes 1 | tf_op jit(solution)/shard_map/inner_products/pallas_call | solution.py:158
  83.6 2.0 %collective-permute-done.far_ref = bf16[4,48,2048]{2,1,0:T(8,128)(2,1)S(1)} collective-permute-done((bf16[4,48,2048]{2,1,0:T(8,128)(2,1)S(1)}, bf16[4,48,2048]{2,1,0:T(8,128)(2,1)S(1)}, u32[]{:S(2)}, u32[]{:S(2)}) %collective-permute-start) | collective-permute-done | bytes 786464 | tf_op jit(solution)/shard_map/ppermute | solution.py:40
  87.6 2.7 %collective-permute-start.7 = (bf16[1,48,2048]{2,1,0:T(8,128)(2,1)S(1)}, bf16[1,48,2048]{2,1,0:T(8,128)(2,1)S(1)}, u32[]{:S(2)}, u32[]{:S(2)}) collective-permute-start(bf16[1,48,2048]{2,1,0:T(8,128)(2,1)S(1)} %get-tuple-element.56), channel_id=1, source_target_pairs={{0,12},{2,14},{4,8},{6,10},{8,4},{10,6},{12,0},{14,2},{1,13},{3,15... | collective-permute-start | bytes 589832 | tf_op jit(solution)/shard_map/ppermute | solution.py:40
  90.2 7.2 %project.6 = (bf16[4,48,2048]{2,1,0:T(8,128)(2,1)S(1)}, bf16[4,48,2048]{2,1,0:T(8,128)(2,1)S(1)}, bf16[4,48,1024]{2,1,0:T(8,128)(2,1)S(1)}, bf16[4,48,1024]{2,1,0:T(8,128)(2,1)S(1)}) custom-call(s32[8]{0:T(128)S(1)} %stack.96.where_ref, bf16[8,48,1024]{2,1,0:T(8,128)(2,1)S(1)} %all-to-all-done.1.x_ref, bf16[1024,8192]{1,0:T(8,128)(2,1)} %w_ref.7, ...), custom_call_target="tpu_custom_call" | custom-call | flops 20700000256 | bytes 1 | tf_op jit(solution)/shard_map/project/pallas_call | solution.py:277
  97.4 6.7 %collective-permute-done.16.b_ref = bf16[384,128]{1,0:T(8,128)(2,1)S(1)} collective-permute-done((bf16[384,128]{1,0:T(8,128)(2,1)S(1)}, bf16[384,128]{1,0:T(8,128)(2,1)S(1)}, u32[]{:S(2)}, u32[]{:S(2)}) %collective-permute-start.16) | collective-permute-done | bytes 98336 | tf_op jit(solution)/shard_map/ppermute | solution.py:40
  104.6 4.3 %collective-permute-done.17.b_ref = bf16[384,128]{1,0:T(8,128)(2,1)S(1)} collective-permute-done((bf16[384,128]{1,0:T(8,128)(2,1)S(1)}, bf16[384,128]{1,0:T(8,128)(2,1)S(1)}, u32[]{:S(2)}, u32[]{:S(2)}) %collective-permute-start.17) | collective-permute-done | bytes 98336 | tf_op jit(solution)/shard_map/ppermute | solution.py:40
  114.6 5.8 %collective-permute-done.18.b_ref = bf16[384,128]{1,0:T(8,128)(2,1)S(1)} collective-permute-done((bf16[384,128]{1,0:T(8,128)(2,1)S(1)}, bf16[384,128]{1,0:T(8,128)(2,1)S(1)}, u32[]{:S(2)}, u32[]{:S(2)}) %collective-permute-start.18) | collective-permute-done | bytes 98336 | tf_op jit(solution)/shard_map/ppermute | solution.py:40
  122.8 9.6 %adapter_outputs.1 = (bf16[384,1024]{1,0:T(8,128)(2,1)S(1)}, bf16[384,1024]{1,0:T(8,128)(2,1)S(1)}) custom-call(bf16[384,128]{1,0:T(8,128)(2,1)S(1)} %multiply_convert_fusion.1.a_ref, bf16[384,128]{1,0:T(8,128)(2,1)S(1)} %multiply_convert_fusion.b_ref, s32[384,1]{1,0:T(8,128)S(1)} %fusion.ia_ref, s32[384,1]{1,0:T(8,128)S(1)} %broadcast_in_dim.90.ib_ref, ...), custom_call_target="tpu_custom_call" | custom-call | flops 11500000256 | bytes 1 | tf_op jit(solution)/shard_map/adapter_outputs/pallas_call | solution.py:208
  132.5 2.8 %collective-permute-done.12.far_ref = bf16[4,48,2048]{2,1,0:T(8,128)(2,1)S(1)} collective-permute-done((bf16[4,48,2048]{2,1,0:T(8,128)(2,1)S(1)}, bf16[4,48,2048]{2,1,0:T(8,128)(2,1)S(1)}, u32[]{:S(2)}, u32[]{:S(2)}) %collective-permute-start.12) | collective-permute-done | bytes 786464 | tf_op jit(solution)/shard_map/ppermute | solution.py:40
  137.3 2.7 %collective-permute-start.15 = (bf16[1,48,2048]{2,1,0:T(8,128)(2,1)S(1)}, bf16[1,48,2048]{2,1,0:T(8,128)(2,1)S(1)}, u32[]{:S(2)}, u32[]{:S(2)}) collective-permute-start(bf16[1,48,2048]{2,1,0:T(8,128)(2,1)S(1)} %get-tuple-element.67), channel_id=1, source_target_pairs={{0,12},{2,14},{4,8},{6,10},{8,4},{10,6},{12,0},{14,2},{1,13},{3,15... | collective-permute-start | bytes 589832 | tf_op jit(solution)/shard_map/ppermute | solution.py:40
  140.0 3.2 %project.7 = (bf16[4,48,1024]{2,1,0:T(8,128)(2,1)S(1)}, bf16[4,48,1024]{2,1,0:T(8,128)(2,1)S(1)}) custom-call(s32[4]{0:T(128)S(1)} %pad_add_fusion.1.where_ref, bf16[8,48,1024]{2,1,0:T(8,128)(2,1)S(1)} %all-to-all-done.1.x_ref, bf16[1024,8192]{1,0:T(8,128)(2,1)} %w_ref.7, bf16[8,48,1024]{2,1,0:T(8,128)(2,1)S(1)} %bitcast.40, ...), custom_call_target="tpu_custom_call" | custom-call | flops 6899999744 | bytes 1 | tf_op jit(solution)/shard_map/project/pallas_call | solution.py:277
  144.8 6.3 %collective-permute-done.25.far_ref = bf16[4,48,1024]{2,1,0:T(8,128)(2,1)S(1)} collective-permute-done((bf16[4,48,1024]{2,1,0:T(8,128)(2,1)S(1)}, bf16[4,48,1024]{2,1,0:T(8,128)(2,1)S(1)}, u32[]{:S(2)}, u32[]{:S(2)}) %collective-permute-start.25) | collective-permute-done | bytes 393248 | tf_op jit(solution)/shard_map/ppermute | solution.py:40
  152.2 2.1 %collective-permute-start.24 = (bf16[1,48,1024]{2,1,0:T(8,128)(2,1)S(1)}, bf16[1,48,1024]{2,1,0:T(8,128)(2,1)S(1)}, u32[]{:S(2)}, u32[]{:S(2)}) collective-permute-start(bf16[1,48,1024]{2,1,0:T(8,128)(2,1)S(1)} %get-tuple-element.82), channel_id=1, source_target_pairs={{0,12},{2,14},{4,8},{6,10},{8,4},{10,6},{12,0},{14,2},{1,13},{3,15... | collective-permute-start | bytes 294920 | tf_op jit(solution)/shard_map/ppermute | solution.py:40
  154.9 8.7 %collective-permute-start.27 = (bf16[1,48,1024]{2,1,0:T(8,128)(2,1)S(1)}, bf16[1,48,1024]{2,1,0:T(8,128)(2,1)S(1)}, u32[]{:S(2)}, u32[]{:S(2)}) collective-permute-start(bf16[1,48,1024]{2,1,0:T(8,128)(2,1)S(1)} %get-tuple-element.87), channel_id=1, source_target_pairs={{0,8},{2,10},{4,12},{6,14},{8,0},{10,2},{12,4},{14,6},{1,9},{3,11}... | collective-permute-start | bytes 294920 | tf_op jit(solution)/shard_map/ppermute | solution.py:40
  163.6 2.5 %collective-permute-start.28 = (bf16[1,48,1024]{2,1,0:T(8,128)(2,1)S(1)}, bf16[1,48,1024]{2,1,0:T(8,128)(2,1)S(1)}, u32[]{:S(2)}, u32[]{:S(2)}) collective-permute-start(bf16[1,48,1024]{2,1,0:T(8,128)(2,1)S(1)} %get-tuple-element.88), channel_id=1, source_target_pairs={{0,12},{2,14},{4,8},{6,10},{8,4},{10,6},{12,0},{14,2},{1,13},{3,15... | collective-permute-start | bytes 294920 | tf_op jit(solution)/shard_map/ppermute | solution.py:40
  166.2 3.9 %collective-permute-done.27.refs_18_ = bf16[1,48,1024]{2,1,0:T(8,128)(2,1)S(1)} collective-permute-done((bf16[1,48,1024]{2,1,0:T(8,128)(2,1)S(1)}, bf16[1,48,1024]{2,1,0:T(8,128)(2,1)S(1)}, u32[]{:S(2)}, u32[]{:S(2)}) %collective-permute-start.27) | collective-permute-done | bytes 98336 | tf_op jit(solution)/shard_map/ppermute | solution.py:40
  170.1 2.1 %finish.1 = bf16[48,8192]{1,0:T(8,128)(2,1)} custom-call(s32[2]{0:T(128)S(1)} %pad_add_fusion.place_ref, bf16[48,8192]{1,0:T(8,128)(2,1)S(1)} %bitcast.38, bf16[1,48,2048]{2,1,0:T(8,128)(2,1)S(1)} %get-tuple-element.53.refs_0_, bf16[1,48,2048]{2,1,0:T(8,128)(2,1)S(1)} %collective-permute-done.5.refs_0_.refs_1_, ...), custom_call_target="tpu_custom_call" | custom-call | flops 2300000000 | bytes 1 | tf_op jit(solution)/shard_map/finish/pallas_call | solution.py:382
  (85 shorter events, 25.2 us)
Async XLA Ops:
  0.0 27.5 %all-to-all-start = ((bf16[8,48,1024]{2,1,0:T(8,128)(2,1)}), bf16[8,48,1024]{2,1,0:T(8,128)(2,1)S(1)}, u32[]{:S(2)}, u32[]{:S(2)}) async-start(bf16[8,48,1024]{2,1,0:T(8,128)(2,1)} %bitcast.41), calls=%async_computation | async-start | bytes 1572864 | tf_op jit(solution)/shard_map/all_to_all | solution.py:420
  7.3 34.0 %collective-permute-start.3 = (s32[16]{0:T(128)}, s32[16]{0:T(128)S(1)}, u32[]{:S(2)}, u32[]{:S(2)}) collective-permute-start(s32[16]{0:T(128)} %bitcast.43), channel_id=1, source_target_pairs={{0,1},{1,0},{2,3},{3,2},{4,5},{5,4},{6,7},{7,6},{8,9},{9,8},{10,11... | collective-permute-start | bytes 200 | tf_op jit(solution)/shard_map/ppermute | solution.py:40
  8.0 33.2 %collective-permute-start.2 = (s32[384]{0:T(512)S(1)}, s32[384]{0:T(512)S(1)}, u32[]{:S(2)}, u32[]{:S(2)}) collective-permute-start(s32[384]{0:T(512)S(1)} %get-tuple-element.98), channel_id=1, source_target_pairs={{0,1},{1,0},{2,3},{3,2},{4,5},{5,4},{6,7},{7,6},{8,9},{9,8},{10,11... | collective-permute-start | bytes 4616 | tf_op jit(solution)/shard_map/ppermute | solution.py:40
  36.2 23.9 %all-to-all-start.1 = ((bf16[8,48,1024]{2,1,0:T(8,128)(2,1)}), bf16[8,48,1024]{2,1,0:T(8,128)(2,1)S(1)}, u32[]{:S(2)}, u32[]{:S(2)}) async-start(bf16[8,48,1024]{2,1,0:T(8,128)(2,1)} %attend.1), calls=%async_computation.1 | async-start | bytes 1572864 | tf_op jit(solution)/shard_map/all_to_all | solution.py:452
  60.1 11.8 %collective-permute-start.1 = (bf16[384,1024]{1,0:T(8,128)(2,1)S(1)}, bf16[384,1024]{1,0:T(8,128)(2,1)S(1)}, u32[]{:S(2)}, u32[]{:S(2)}) collective-permute-start(bf16[384,1024]{1,0:T(8,128)(2,1)S(1)} %bitcast.36), channel_id=1, source_target_pairs={{0,1},{1,0},{2,3},{3,2},{4,5},{5,4},{6,7},{7,6},{8,9},{9,8},{10,11... | collective-permute-start | bytes 2359304 | tf_op jit(solution)/shard_map/ppermute | solution.py:40
  65.2 20.4 %collective-permute-start = (bf16[4,48,2048]{2,1,0:T(8,128)(2,1)S(1)}, bf16[4,48,2048]{2,1,0:T(8,128)(2,1)S(1)}, u32[]{:S(2)}, u32[]{:S(2)}) collective-permute-start(bf16[4,48,2048]{2,1,0:T(8,128)(2,1)S(1)} %get-tuple-element.48), channel_id=1, source_target_pairs={{0,2},{2,0},{4,6},{6,4},{8,10},{10,8},{12,14},{14,12},{1,3},{3,1},... | collective-permute-start | bytes 2359304 | tf_op jit(solution)/shard_map/ppermute | solution.py:40
  81.4 28.9 %collective-permute-start.8 = (bf16[4,48,2048]{2,1,0:T(8,128)(2,1)S(1)}, bf16[4,48,2048]{2,1,0:T(8,128)(2,1)S(1)}, u32[]{:S(2)}, u32[]{:S(2)}) collective-permute-start(bf16[4,48,2048]{2,1,0:T(8,128)(2,1)S(1)} %get-tuple-element.57), channel_id=1, source_target_pairs={{0,2},{2,0},{4,6},{6,4},{8,10},{10,8},{12,14},{14,12},{1,3},{3,1},... | collective-permute-start | bytes 2359304 | tf_op jit(solution)/shard_map/ppermute | solution.py:40
  82.4 21.7 %collective-permute-start.16 = (bf16[384,128]{1,0:T(8,128)(2,1)S(1)}, bf16[384,128]{1,0:T(8,128)(2,1)S(1)}, u32[]{:S(2)}, u32[]{:S(2)}) collective-permute-start(bf16[384,128]{1,0:T(8,128)(2,1)S(1)} %get-tuple-element.68), channel_id=1, source_target_pairs={{0,2},{2,0},{4,6},{6,4},{8,10},{10,8},{12,14},{14,12},{1,3},{3,1},... | collective-permute-start | bytes 294920 | tf_op jit(solution)/shard_map/ppermute | solution.py:40
  85.8 25.2 %collective-permute-start.5 = (bf16[1,48,2048]{2,1,0:T(8,128)(2,1)S(1)}, bf16[1,48,2048]{2,1,0:T(8,128)(2,1)S(1)}, u32[]{:S(2)}, u32[]{:S(2)}) collective-permute-start(bf16[1,48,2048]{2,1,0:T(8,128)(2,1)S(1)} %get-tuple-element.54), channel_id=1, source_target_pairs={{0,4},{2,6},{4,0},{6,2},{8,12},{10,14},{12,8},{14,10},{1,5},{3,7},... | collective-permute-start | bytes 589832 | tf_op jit(solution)/shard_map/ppermute | solution.py:40
  86.2 24.8 %collective-permute-start.6 = (bf16[1,48,2048]{2,1,0:T(8,128)(2,1)S(1)}, bf16[1,48,2048]{2,1,0:T(8,128)(2,1)S(1)}, u32[]{:S(2)}, u32[]{:S(2)}) collective-permute-start(bf16[1,48,2048]{2,1,0:T(8,128)(2,1)S(1)} %get-tuple-element.55), channel_id=1, source_target_pairs={{0,8},{2,10},{4,12},{6,14},{8,0},{10,2},{12,4},{14,6},{1,9},{3,11}... | collective-permute-start | bytes 589832 | tf_op jit(solution)/shard_map/ppermute | solution.py:40
  87.6 23.5 %collective-permute-start.7 = (bf16[1,48,2048]{2,1,0:T(8,128)(2,1)S(1)}, bf16[1,48,2048]{2,1,0:T(8,128)(2,1)S(1)}, u32[]{:S(2)}, u32[]{:S(2)}) collective-permute-start(bf16[1,48,2048]{2,1,0:T(8,128)(2,1)S(1)} %get-tuple-element.56), channel_id=1, source_target_pairs={{0,12},{2,14},{4,8},{6,10},{8,4},{10,6},{12,0},{14,2},{1,13},{3,15... | collective-permute-start | bytes 589832 | tf_op jit(solution)/shard_map/ppermute | solution.py:40
  108.9 35.8 %collective-permute-start.21 = (bf16[4,48,1024]{2,1,0:T(8,128)(2,1)S(1)}, bf16[4,48,1024]{2,1,0:T(8,128)(2,1)S(1)}, u32[]{:S(2)}, u32[]{:S(2)}) collective-permute-start(bf16[4,48,1024]{2,1,0:T(8,128)(2,1)S(1)} %get-tuple-element.78), channel_id=1, source_target_pairs={{0,2},{2,0},{4,6},{6,4},{8,10},{10,8},{12,14},{14,12},{1,3},{3,1},... | collective-permute-start | bytes 1179656 | tf_op jit(solution)/shard_map/ppermute | solution.py:40
  110.4 25.0 %collective-permute-start.12 = (bf16[4,48,2048]{2,1,0:T(8,128)(2,1)S(1)}, bf16[4,48,2048]{2,1,0:T(8,128)(2,1)S(1)}, u32[]{:S(2)}, u32[]{:S(2)}) collective-permute-start(bf16[4,48,2048]{2,1,0:T(8,128)(2,1)S(1)} %get-tuple-element.63), channel_id=1, source_target_pairs={{0,2},{2,0},{4,6},{6,4},{8,10},{10,8},{12,14},{14,12},{1,3},{3,1},... | collective-permute-start | bytes 2359304 | tf_op jit(solution)/shard_map/ppermute | solution.py:40
  111.2 21.2 %collective-permute-start.9 = (bf16[1,48,2048]{2,1,0:T(8,128)(2,1)S(1)}, bf16[1,48,2048]{2,1,0:T(8,128)(2,1)S(1)}, u32[]{:S(2)}, u32[]{:S(2)}) collective-permute-start(bf16[1,48,2048]{2,1,0:T(8,128)(2,1)S(1)} %get-tuple-element.59), channel_id=1, source_target_pairs={{0,4},{2,6},{4,0},{6,2},{8,12},{10,14},{12,8},{14,10},{1,5},{3,7},... | collective-permute-start | bytes 589832 | tf_op jit(solution)/shard_map/ppermute | solution.py:40
  113.0 19.5 %collective-permute-start.10 = (bf16[1,48,2048]{2,1,0:T(8,128)(2,1)S(1)}, bf16[1,48,2048]{2,1,0:T(8,128)(2,1)S(1)}, u32[]{:S(2)}, u32[]{:S(2)}) collective-permute-start(bf16[1,48,2048]{2,1,0:T(8,128)(2,1)S(1)} %get-tuple-element.60), channel_id=1, source_target_pairs={{0,8},{2,10},{4,12},{6,14},{8,0},{10,2},{12,4},{14,6},{1,9},{3,11}... | collective-permute-start | bytes 589832 | tf_op jit(solution)/shard_map/ppermute | solution.py:40
  121.8 10.8 %collective-permute-start.11 = (bf16[1,48,2048]{2,1,0:T(8,128)(2,1)S(1)}, bf16[1,48,2048]{2,1,0:T(8,128)(2,1)S(1)}, u32[]{:S(2)}, u32[]{:S(2)}) collective-permute-start(bf16[1,48,2048]{2,1,0:T(8,128)(2,1)S(1)} %get-tuple-element.61), channel_id=1, source_target_pairs={{0,12},{2,14},{4,8},{6,10},{8,4},{10,6},{12,0},{14,2},{1,13},{3,15... | collective-permute-start | bytes 589832 | tf_op jit(solution)/shard_map/ppermute | solution.py:40
  135.5 16.7 %collective-permute-start.13 = (bf16[1,48,2048]{2,1,0:T(8,128)(2,1)S(1)}, bf16[1,48,2048]{2,1,0:T(8,128)(2,1)S(1)}, u32[]{:S(2)}, u32[]{:S(2)}) collective-permute-start(bf16[1,48,2048]{2,1,0:T(8,128)(2,1)S(1)} %get-tuple-element.65), channel_id=1, source_target_pairs={{0,4},{2,6},{4,0},{6,2},{8,12},{10,14},{12,8},{14,10},{1,5},{3,7},... | collective-permute-start | bytes 589832 | tf_op jit(solution)/shard_map/ppermute | solution.py:40
  135.9 18.3 %collective-permute-start.14 = (bf16[1,48,2048]{2,1,0:T(8,128)(2,1)S(1)}, bf16[1,48,2048]{2,1,0:T(8,128)(2,1)S(1)}, u32[]{:S(2)}, u32[]{:S(2)}) collective-permute-start(bf16[1,48,2048]{2,1,0:T(8,128)(2,1)S(1)} %get-tuple-element.66), channel_id=1, source_target_pairs={{0,8},{2,10},{4,12},{6,14},{8,0},{10,2},{12,4},{14,6},{1,9},{3,11}... | collective-permute-start | bytes 589832 | tf_op jit(solution)/shard_map/ppermute | solution.py:40
  137.3 17.6 %collective-permute-start.15 = (bf16[1,48,2048]{2,1,0:T(8,128)(2,1)S(1)}, bf16[1,48,2048]{2,1,0:T(8,128)(2,1)S(1)}, u32[]{:S(2)}, u32[]{:S(2)}) collective-permute-start(bf16[1,48,2048]{2,1,0:T(8,128)(2,1)S(1)} %get-tuple-element.67), channel_id=1, source_target_pairs={{0,12},{2,14},{4,8},{6,10},{8,4},{10,6},{12,0},{14,2},{1,13},{3,15... | collective-permute-start | bytes 589832 | tf_op jit(solution)/shard_map/ppermute | solution.py:40
  144.8 18.8 %collective-permute-start.22 = (bf16[1,48,1024]{2,1,0:T(8,128)(2,1)S(1)}, bf16[1,48,1024]{2,1,0:T(8,128)(2,1)S(1)}, u32[]{:S(2)}, u32[]{:S(2)}) collective-permute-start(bf16[1,48,1024]{2,1,0:T(8,128)(2,1)S(1)} %get-tuple-element.80), channel_id=1, source_target_pairs={{0,4},{2,6},{4,0},{6,2},{8,12},{10,14},{12,8},{14,10},{1,5},{3,7},... | collective-permute-start | bytes 294920 | tf_op jit(solution)/shard_map/ppermute | solution.py:40
  151.1 15.0 %collective-permute-start.23 = (bf16[1,48,1024]{2,1,0:T(8,128)(2,1)S(1)}, bf16[1,48,1024]{2,1,0:T(8,128)(2,1)S(1)}, u32[]{:S(2)}, u32[]{:S(2)}) collective-permute-start(bf16[1,48,1024]{2,1,0:T(8,128)(2,1)S(1)} %get-tuple-element.81), channel_id=1, source_target_pairs={{0,8},{2,10},{4,12},{6,14},{8,0},{10,2},{12,4},{14,6},{1,9},{3,11}... | collective-permute-start | bytes 294920 | tf_op jit(solution)/shard_map/ppermute | solution.py:40
  152.2 14.0 %collective-permute-start.24 = (bf16[1,48,1024]{2,1,0:T(8,128)(2,1)S(1)}, bf16[1,48,1024]{2,1,0:T(8,128)(2,1)S(1)}, u32[]{:S(2)}, u32[]{:S(2)}) collective-permute-start(bf16[1,48,1024]{2,1,0:T(8,128)(2,1)S(1)} %get-tuple-element.82), channel_id=1, source_target_pairs={{0,12},{2,14},{4,8},{6,10},{8,4},{10,6},{12,0},{14,2},{1,13},{3,15... | collective-permute-start | bytes 294920 | tf_op jit(solution)/shard_map/ppermute | solution.py:40
  154.3 11.9 %collective-permute-start.26 = (bf16[1,48,1024]{2,1,0:T(8,128)(2,1)S(1)}, bf16[1,48,1024]{2,1,0:T(8,128)(2,1)S(1)}, u32[]{:S(2)}, u32[]{:S(2)}) collective-permute-start(bf16[1,48,1024]{2,1,0:T(8,128)(2,1)S(1)} %get-tuple-element.86), channel_id=1, source_target_pairs={{0,4},{2,6},{4,0},{6,2},{8,12},{10,14},{12,8},{14,10},{1,5},{3,7},... | collective-permute-start | bytes 294920 | tf_op jit(solution)/shard_map/ppermute | solution.py:40
  154.9 15.2 %collective-permute-start.27 = (bf16[1,48,1024]{2,1,0:T(8,128)(2,1)S(1)}, bf16[1,48,1024]{2,1,0:T(8,128)(2,1)S(1)}, u32[]{:S(2)}, u32[]{:S(2)}) collective-permute-start(bf16[1,48,1024]{2,1,0:T(8,128)(2,1)S(1)} %get-tuple-element.87), channel_id=1, source_target_pairs={{0,8},{2,10},{4,12},{6,14},{8,0},{10,2},{12,4},{14,6},{1,9},{3,11}... | collective-permute-start | bytes 294920 | tf_op jit(solution)/shard_map/ppermute | solution.py:40
  (10 other events, 79.5 us)

commit v4 on v3

--- a/solution.py
+++ b/solution.py
@@ -24,7 +24,7 @@
     "project": {1: [("project", 0)], 2: [("add", 0), ("project", 1)], 3: [("add", 2)]},
     "inner": {0: [("project", 1)]},
     "route": {0: [("sum", 0)], 1: [("z", 0)], 2: [("z", 1)]},
-    "sum": {1: [("project", 2)]},
+    "sum": {1: [("project", 2)], 2: [("add", 1)]},
     "delta": {0: [("add", 1)]},
 }
 LAYOUT = (2,)

time: 173 us -> 173 us (level)
  transfers between devices with their start and end apart: 31 -> 31, of which waited for: 11 -> 14; matrix products, arithmetic and copies ran while one was open for 3% -> 3% of each run, Pallas kernels for 28% -> 28%
where the time goes in v4:
time: 173 us
  waiting for transfers between devices  69.6 us (40%)
  Pallas kernels  51 us (29%)
  starting transfers between devices  46.3 us (27%)
  local copies, waits for them, and re-layouts  2.86 us (2%)
  other arithmetic  2.41 us (1%)
    ppermute x29, starting transfers between devices, permute_xor(): return lax.ppermute(x, axis, [(i, i ^ k) for i in range(size)])  35.3 us
    ppermute x29, waiting for transfers between devices, permute_xor(): return lax.ppermute(x, axis, [(i, i ^ k) for i in range(size)])  34.9 us
    pallas_call x4, Pallas kernels, project(): pl.pallas_call(functools.partial(project_kernel, spans, delta is not None...  20.6 us
    all_to_all x1, waiting for transfers between devices, shards(): x = lax.all_to_all(attended, 'tp', 0, 0)  18.6 us
    all_to_all x1, waiting for transfers between devices, shards(): q = lax.all_to_all(queries[0].reshape(n, rows, width), 'tp', 0, 0)  16.1 us
    pallas_call x1, Pallas kernels, adapter_outputs(): pl.pallas_call(functools.partial(delta_kernel, per), grid=(owned // per,)...  9.56 us
    pallas_call x1, Pallas kernels, inner_products(): pl.pallas_call(functools.partial(inner_kernel, per), grid=(owned // per,)...  9.19 us
    pallas_call x1, Pallas kernels, attend(): pl.pallas_call(functools.partial(attend_kernel, n), grid=(rows // ROW_BLO...  8.71 us
  transfers between devices with their start and end apart: 31, of which 14 were waited for; matrix products, arithmetic and copies ran while one was open for 3% of the time, Pallas kernels for 28%

profile of v4, /device:TPU:0, one launch (start us, length us, event | category | flops | bytes accessed | tf_op | source)
XLA Modules:
  0.0 172.9 jit_solution(2504194687394084264)
XLA Ops:
  0.0 7.3 %all-to-all-start = ((bf16[8,48,1024]{2,1,0:T(8,128)(2,1)}), bf16[8,48,1024]{2,1,0:T(8,128)(2,1)S(1)}, u32[]{:S(2)}, u32[]{:S(2)}) async-start(bf16[8,48,1024]{2,1,0:T(8,128)(2,1)} %bitcast.41), calls=%async_computation | async-start | bytes 1572864 | tf_op jit(solution)/shard_map/all_to_all | solution.py:420
  11.4 16.1 %all-to-all-done.q_ref = bf16[8,48,1024]{2,1,0:T(8,128)(2,1)S(1)} async-done(((bf16[8,48,1024]{2,1,0:T(8,128)(2,1)}), bf16[8,48,1024]{2,1,0:T(8,128)(2,1)S(1)}, u32[]{:S(2)}, u32[]{:S(2)}) %all-to-all-start) | async-done | bytes 786464 | tf_op jit(solution)/shard_map/all_to_all | solution.py:420
  27.5 8.7 %attend.1 = bf16[8,48,1024]{2,1,0:T(8,128)(2,1)} custom-call(bf16[8,48,1024]{2,1,0:T(8,128)(2,1)S(1)} %all-to-all-done.q_ref, bf16[48,64,1024]{2,1,0:T(8,128)(2,1)} %bitcast.45, bf16[48,64,1024]{2,1,0:T(8,128)(2,1)} %bitcast.46, bf16[48,1024]{1,0:T(8,128)(2,1)S(1)} %get-tuple-element.101.fk_ref, bf16[48,1024]{1,0:T(8,128)(2,1)S(1)} %get-tuple-element.100.fv_ref, ...), custom_call_target="tpu_custom_call" | custom-call | flops 10350000128 | bytes 1 | tf_op jit(solution)/shard_map/attend/pallas_call | solution.py:110
  36.2 3.7 %all-to-all-start.1 = ((bf16[8,48,1024]{2,1,0:T(8,128)(2,1)}), bf16[8,48,1024]{2,1,0:T(8,128)(2,1)S(1)}, u32[]{:S(2)}, u32[]{:S(2)}) async-start(bf16[8,48,1024]{2,1,0:T(8,128)(2,1)} %attend.1), calls=%async_computation.1 | async-start | bytes 1572864 | tf_op jit(solution)/shard_map/all_to_all | solution.py:452
  41.5 18.6 %all-to-all-done.1.x_ref = bf16[8,48,1024]{2,1,0:T(8,128)(2,1)S(1)} async-done(((bf16[8,48,1024]{2,1,0:T(8,128)(2,1)}), bf16[8,48,1024]{2,1,0:T(8,128)(2,1)S(1)}, u32[]{:S(2)}, u32[]{:S(2)}) %all-to-all-start.1) | async-done | bytes 786464 | tf_op jit(solution)/shard_map/all_to_all | solution.py:452
  60.1 5.1 %project.4 = (bf16[4,48,2048]{2,1,0:T(8,128)(2,1)S(1)}, bf16[4,48,2048]{2,1,0:T(8,128)(2,1)S(1)}) custom-call(s32[6]{0:T(128)S(1)} %stack.84.where_ref, bf16[8,48,1024]{2,1,0:T(8,128)(2,1)S(1)} %all-to-all-done.1.x_ref, bf16[1024,8192]{1,0:T(8,128)(2,1)} %w_ref.7), custom_call_target="tpu_custom_call" | custom-call | flops 13799999488 | bytes 1 | tf_op jit(solution)/shard_map/project/pallas_call | solution.py:277
  66.7 5.1 %project.5 = (bf16[4,48,2048]{2,1,0:T(8,128)(2,1)S(1)}, bf16[4,48,2048]{2,1,0:T(8,128)(2,1)S(1)}) custom-call(s32[6]{0:T(128)S(1)} %stack.89.where_ref, bf16[8,48,1024]{2,1,0:T(8,128)(2,1)S(1)} %all-to-all-done.1.x_ref, bf16[1024,8192]{1,0:T(8,128)(2,1)} %w_ref.7, bf16[4,48,2048]{2,1,0:T(8,128)(2,1)S(1)} %get-tuple-element.47.refs_0_.near_ref), custom_call_target="tpu_custom_call" | custom-call | flops 13799999488 | bytes 1 | tf_op jit(solution)/shard_map/project/pallas_call | solution.py:277
  71.8 9.2 %inner_products.1 = (bf16[384,128]{1,0:T(8,128)(2,1)S(1)}, bf16[384,128]{1,0:T(8,128)(2,1)S(1)}) custom-call(bf16[384,1024]{1,0:T(8,128)(2,1)S(1)} %bitcast.37, bf16[384,1024]{1,0:T(8,128)(2,1)S(1)} %collective-permute-done.1.b_ref, s32[384,1]{1,0:T(8,128)S(1)} %fusion.ia_ref, s32[384,1]{1,0:T(8,128)S(1)} %broadcast_in_dim.90.ib_ref, ...), custom_call_target="tpu_custom_call" | custom-call | flops 10350000128 | bytes 1 | tf_op jit(solution)/shard_map/inner_products/pallas_call | solution.py:158
  83.6 2.0 %collective-permute-done.far_ref = bf16[4,48,2048]{2,1,0:T(8,128)(2,1)S(1)} collective-permute-done((bf16[4,48,2048]{2,1,0:T(8,128)(2,1)S(1)}, bf16[4,48,2048]{2,1,0:T(8,128)(2,1)S(1)}, u32[]{:S(2)}, u32[]{:S(2)}) %collective-permute-start) | collective-permute-done | bytes 786464 | tf_op jit(solution)/shard_map/ppermute | solution.py:40
  87.6 2.7 %collective-permute-start.7 = (bf16[1,48,2048]{2,1,0:T(8,128)(2,1)S(1)}, bf16[1,48,2048]{2,1,0:T(8,128)(2,1)S(1)}, u32[]{:S(2)}, u32[]{:S(2)}) collective-permute-start(bf16[1,48,2048]{2,1,0:T(8,128)(2,1)S(1)} %get-tuple-element.56), channel_id=1, source_target_pairs={{0,12},{2,14},{4,8},{6,10},{8,4},{10,6},{12,0},{14,2},{1,13},{3,15... | collective-permute-start | bytes 589832 | tf_op jit(solution)/shard_map/ppermute | solution.py:40
  90.2 7.2 %project.6 = (bf16[4,48,2048]{2,1,0:T(8,128)(2,1)S(1)}, bf16[4,48,2048]{2,1,0:T(8,128)(2,1)S(1)}, bf16[4,48,1024]{2,1,0:T(8,128)(2,1)S(1)}, bf16[4,48,1024]{2,1,0:T(8,128)(2,1)S(1)}) custom-call(s32[8]{0:T(128)S(1)} %stack.96.where_ref, bf16[8,48,1024]{2,1,0:T(8,128)(2,1)S(1)} %all-to-all-done.1.x_ref, bf16[1024,8192]{1,0:T(8,128)(2,1)} %w_ref.7, ...), custom_call_target="tpu_custom_call" | custom-call | flops 20700000256 | bytes 1 | tf_op jit(solution)/shard_map/project/pallas_call | solution.py:277
  97.4 6.7 %collective-permute-done.16.b_ref = bf16[384,128]{1,0:T(8,128)(2,1)S(1)} collective-permute-done((bf16[384,128]{1,0:T(8,128)(2,1)S(1)}, bf16[384,128]{1,0:T(8,128)(2,1)S(1)}, u32[]{:S(2)}, u32[]{:S(2)}) %collective-permute-start.16) | collective-permute-done | bytes 98336 | tf_op jit(solution)/shard_map/ppermute | solution.py:40
  104.8 4.1 %collective-permute-done.17.b_ref = bf16[384,128]{1,0:T(8,128)(2,1)S(1)} collective-permute-done((bf16[384,128]{1,0:T(8,128)(2,1)S(1)}, bf16[384,128]{1,0:T(8,128)(2,1)S(1)}, u32[]{:S(2)}, u32[]{:S(2)}) %collective-permute-start.17) | collective-permute-done | bytes 98336 | tf_op jit(solution)/shard_map/ppermute | solution.py:40
  111.1 1.6 collective-permute-start.9
  114.3 2.1 %collective-permute-done.18.b_ref = bf16[384,128]{1,0:T(8,128)(2,1)S(1)} collective-permute-done((bf16[384,128]{1,0:T(8,128)(2,1)S(1)}, bf16[384,128]{1,0:T(8,128)(2,1)S(1)}, u32[]{:S(2)}, u32[]{:S(2)}) %collective-permute-start.18) | collective-permute-done | bytes 98336 | tf_op jit(solution)/shard_map/ppermute | solution.py:40
  118.2 9.6 %adapter_outputs.1 = (bf16[384,1024]{1,0:T(8,128)(2,1)S(1)}, bf16[384,1024]{1,0:T(8,128)(2,1)S(1)}) custom-call(bf16[384,128]{1,0:T(8,128)(2,1)S(1)} %multiply_convert_fusion.1.a_ref, bf16[384,128]{1,0:T(8,128)(2,1)S(1)} %multiply_convert_fusion.b_ref, s32[384,1]{1,0:T(8,128)S(1)} %fusion.ia_ref, s32[384,1]{1,0:T(8,128)S(1)} %broadcast_in_dim.90.ib_ref, ...), custom_call_target="tpu_custom_call" | custom-call | flops 11500000256 | bytes 1 | tf_op jit(solution)/shard_map/adapter_outputs/pallas_call | solution.py:208
  129.2 6.4 %collective-permute-done.12.far_ref = bf16[4,48,2048]{2,1,0:T(8,128)(2,1)S(1)} collective-permute-done((bf16[4,48,2048]{2,1,0:T(8,128)(2,1)S(1)}, bf16[4,48,2048]{2,1,0:T(8,128)(2,1)S(1)}, u32[]{:S(2)}, u32[]{:S(2)}) %collective-permute-start.12) | collective-permute-done | bytes 786464 | tf_op jit(solution)/shard_map/ppermute | solution.py:40
  140.2 3.2 %project.7 = (bf16[4,48,1024]{2,1,0:T(8,128)(2,1)S(1)}, bf16[4,48,1024]{2,1,0:T(8,128)(2,1)S(1)}) custom-call(s32[4]{0:T(128)S(1)} %pad_add_fusion.1.where_ref, bf16[8,48,1024]{2,1,0:T(8,128)(2,1)S(1)} %all-to-all-done.1.x_ref, bf16[1024,8192]{1,0:T(8,128)(2,1)} %w_ref.7, bf16[8,48,1024]{2,1,0:T(8,128)(2,1)S(1)} %bitcast.40, ...), custom_call_target="tpu_custom_call" | custom-call | flops 6899999744 | bytes 1 | tf_op jit(solution)/shard_map/project/pallas_call | solution.py:277
  143.4 1.8 %collective-permute-start.25 = (bf16[4,48,1024]{2,1,0:T(8,128)(2,1)S(1)}, bf16[4,48,1024]{2,1,0:T(8,128)(2,1)S(1)}, u32[]{:S(2)}, u32[]{:S(2)}) collective-permute-start(bf16[4,48,1024]{2,1,0:T(8,128)(2,1)S(1)} %get-tuple-element.84), channel_id=1, source_target_pairs={{0,2},{2,0},{4,6},{6,4},{8,10},{10,8},{12,14},{14,12},{1,3},{3,1},... | collective-permute-start | bytes 1179656 | tf_op jit(solution)/shard_map/ppermute | solution.py:40
  145.8 5.7 %collective-permute-done.25.far_ref = bf16[4,48,1024]{2,1,0:T(8,128)(2,1)S(1)} collective-permute-done((bf16[4,48,1024]{2,1,0:T(8,128)(2,1)S(1)}, bf16[4,48,1024]{2,1,0:T(8,128)(2,1)S(1)}, u32[]{:S(2)}, u32[]{:S(2)}) %collective-permute-start.25) | collective-permute-done | bytes 393248 | tf_op jit(solution)/shard_map/ppermute | solution.py:40
  155.2 9.1 %collective-permute-start.27 = (bf16[1,48,1024]{2,1,0:T(8,128)(2,1)S(1)}, bf16[1,48,1024]{2,1,0:T(8,128)(2,1)S(1)}, u32[]{:S(2)}, u32[]{:S(2)}) collective-permute-start(bf16[1,48,1024]{2,1,0:T(8,128)(2,1)S(1)} %get-tuple-element.87), channel_id=1, source_target_pairs={{0,8},{2,10},{4,12},{6,14},{8,0},{10,2},{12,4},{14,6},{1,9},{3,11}... | collective-permute-start | bytes 294920 | tf_op jit(solution)/shard_map/ppermute | solution.py:40
  164.3 1.9 %collective-permute-start.28 = (bf16[1,48,1024]{2,1,0:T(8,128)(2,1)S(1)}, bf16[1,48,1024]{2,1,0:T(8,128)(2,1)S(1)}, u32[]{:S(2)}, u32[]{:S(2)}) collective-permute-start(bf16[1,48,1024]{2,1,0:T(8,128)(2,1)S(1)} %get-tuple-element.88), channel_id=1, source_target_pairs={{0,12},{2,14},{4,8},{6,10},{8,4},{10,6},{12,0},{14,2},{1,13},{3,15... | collective-permute-start | bytes 294920 | tf_op jit(solution)/shard_map/ppermute | solution.py:40
  166.3 3.1 %collective-permute-done.27.refs_18_ = bf16[1,48,1024]{2,1,0:T(8,128)(2,1)S(1)} collective-permute-done((bf16[1,48,1024]{2,1,0:T(8,128)(2,1)S(1)}, bf16[1,48,1024]{2,1,0:T(8,128)(2,1)S(1)}, u32[]{:S(2)}, u32[]{:S(2)}) %collective-permute-start.27) | collective-permute-done | bytes 98336 | tf_op jit(solution)/shard_map/ppermute | solution.py:40
  170.8 2.1 %finish.1 = bf16[48,8192]{1,0:T(8,128)(2,1)} custom-call(s32[2]{0:T(128)S(1)} %pad_add_fusion.place_ref, bf16[48,8192]{1,0:T(8,128)(2,1)S(1)} %bitcast.38, bf16[1,48,2048]{2,1,0:T(8,128)(2,1)S(1)} %get-tuple-element.53.refs_0_, bf16[1,48,2048]{2,1,0:T(8,128)(2,1)S(1)} %collective-permute-done.5.refs_0_.refs_1_, ...), custom_call_target="tpu_custom_call" | custom-call | flops 2300000000 | bytes 1 | tf_op jit(solution)/shard_map/finish/pallas_call | solution.py:382
  (85 shorter events, 29.2 us)
Async XLA Ops:
  0.0 27.5 %all-to-all-start = ((bf16[8,48,1024]{2,1,0:T(8,128)(2,1)}), bf16[8,48,1024]{2,1,0:T(8,128)(2,1)S(1)}, u32[]{:S(2)}, u32[]{:S(2)}) async-start(bf16[8,48,1024]{2,1,0:T(8,128)(2,1)} %bitcast.41), calls=%async_computation | async-start | bytes 1572864 | tf_op jit(solution)/shard_map/all_to_all | solution.py:420
  7.3 34.0 %collective-permute-start.3 = (s32[16]{0:T(128)}, s32[16]{0:T(128)S(1)}, u32[]{:S(2)}, u32[]{:S(2)}) collective-permute-start(s32[16]{0:T(128)} %bitcast.43), channel_id=1, source_target_pairs={{0,1},{1,0},{2,3},{3,2},{4,5},{5,4},{6,7},{7,6},{8,9},{9,8},{10,11... | collective-permute-start | bytes 200 | tf_op jit(solution)/shard_map/ppermute | solution.py:40
  8.0 33.2 %collective-permute-start.2 = (s32[384]{0:T(512)S(1)}, s32[384]{0:T(512)S(1)}, u32[]{:S(2)}, u32[]{:S(2)}) collective-permute-start(s32[384]{0:T(512)S(1)} %get-tuple-element.98), channel_id=1, source_target_pairs={{0,1},{1,0},{2,3},{3,2},{4,5},{5,4},{6,7},{7,6},{8,9},{9,8},{10,11... | collective-permute-start | bytes 4616 | tf_op jit(solution)/shard_map/ppermute | solution.py:40
  36.2 23.9 %all-to-all-start.1 = ((bf16[8,48,1024]{2,1,0:T(8,128)(2,1)}), bf16[8,48,1024]{2,1,0:T(8,128)(2,1)S(1)}, u32[]{:S(2)}, u32[]{:S(2)}) async-start(bf16[8,48,1024]{2,1,0:T(8,128)(2,1)} %attend.1), calls=%async_computation.1 | async-start | bytes 1572864 | tf_op jit(solution)/shard_map/all_to_all | solution.py:452
  60.1 11.8 %collective-permute-start.1 = (bf16[384,1024]{1,0:T(8,128)(2,1)S(1)}, bf16[384,1024]{1,0:T(8,128)(2,1)S(1)}, u32[]{:S(2)}, u32[]{:S(2)}) collective-permute-start(bf16[384,1024]{1,0:T(8,128)(2,1)S(1)} %bitcast.36), channel_id=1, source_target_pairs={{0,1},{1,0},{2,3},{3,2},{4,5},{5,4},{6,7},{7,6},{8,9},{9,8},{10,11... | collective-permute-start | bytes 2359304 | tf_op jit(solution)/shard_map/ppermute | solution.py:40
  65.2 20.4 %collective-permute-start = (bf16[4,48,2048]{2,1,0:T(8,128)(2,1)S(1)}, bf16[4,48,2048]{2,1,0:T(8,128)(2,1)S(1)}, u32[]{:S(2)}, u32[]{:S(2)}) collective-permute-start(bf16[4,48,2048]{2,1,0:T(8,128)(2,1)S(1)} %get-tuple-element.48), channel_id=1, source_target_pairs={{0,2},{2,0},{4,6},{6,4},{8,10},{10,8},{12,14},{14,12},{1,3},{3,1},... | collective-permute-start | bytes 2359304 | tf_op jit(solution)/shard_map/ppermute | solution.py:40
  81.4 23.2 %collective-permute-start.8 = (bf16[4,48,2048]{2,1,0:T(8,128)(2,1)S(1)}, bf16[4,48,2048]{2,1,0:T(8,128)(2,1)S(1)}, u32[]{:S(2)}, u32[]{:S(2)}) collective-permute-start(bf16[4,48,2048]{2,1,0:T(8,128)(2,1)S(1)} %get-tuple-element.57), channel_id=1, source_target_pairs={{0,2},{2,0},{4,6},{6,4},{8,10},{10,8},{12,14},{14,12},{1,3},{3,1},... | collective-permute-start | bytes 2359304 | tf_op jit(solution)/shard_map/ppermute | solution.py:40
  82.4 21.7 %collective-permute-start.16 = (bf16[384,128]{1,0:T(8,128)(2,1)S(1)}, bf16[384,128]{1,0:T(8,128)(2,1)S(1)}, u32[]{:S(2)}, u32[]{:S(2)}) collective-permute-start(bf16[384,128]{1,0:T(8,128)(2,1)S(1)} %get-tuple-element.68), channel_id=1, source_target_pairs={{0,2},{2,0},{4,6},{6,4},{8,10},{10,8},{12,14},{14,12},{1,3},{3,1},... | collective-permute-start | bytes 294920 | tf_op jit(solution)/shard_map/ppermute | solution.py:40
  85.8 18.8 %collective-permute-start.5 = (bf16[1,48,2048]{2,1,0:T(8,128)(2,1)S(1)}, bf16[1,48,2048]{2,1,0:T(8,128)(2,1)S(1)}, u32[]{:S(2)}, u32[]{:S(2)}) collective-permute-start(bf16[1,48,2048]{2,1,0:T(8,128)(2,1)S(1)} %get-tuple-element.54), channel_id=1, source_target_pairs={{0,4},{2,6},{4,0},{6,2},{8,12},{10,14},{12,8},{14,10},{1,5},{3,7},... | collective-permute-start | bytes 589832 | tf_op jit(solution)/shard_map/ppermute | solution.py:40
  86.2 18.4 %collective-permute-start.6 = (bf16[1,48,2048]{2,1,0:T(8,128)(2,1)S(1)}, bf16[1,48,2048]{2,1,0:T(8,128)(2,1)S(1)}, u32[]{:S(2)}, u32[]{:S(2)}) collective-permute-start(bf16[1,48,2048]{2,1,0:T(8,128)(2,1)S(1)} %get-tuple-element.55), channel_id=1, source_target_pairs={{0,8},{2,10},{4,12},{6,14},{8,0},{10,2},{12,4},{14,6},{1,9},{3,11}... | collective-permute-start | bytes 589832 | tf_op jit(solution)/shard_map/ppermute | solution.py:40
  87.6 17.1 %collective-permute-start.7 = (bf16[1,48,2048]{2,1,0:T(8,128)(2,1)S(1)}, bf16[1,48,2048]{2,1,0:T(8,128)(2,1)S(1)}, u32[]{:S(2)}, u32[]{:S(2)}) collective-permute-start(bf16[1,48,2048]{2,1,0:T(8,128)(2,1)S(1)} %get-tuple-element.56), channel_id=1, source_target_pairs={{0,12},{2,14},{4,8},{6,10},{8,4},{10,6},{12,0},{14,2},{1,13},{3,15... | collective-permute-start | bytes 589832 | tf_op jit(solution)/shard_map/ppermute | solution.py:40
  109.0 36.1 %collective-permute-start.21 = (bf16[4,48,1024]{2,1,0:T(8,128)(2,1)S(1)}, bf16[4,48,1024]{2,1,0:T(8,128)(2,1)S(1)}, u32[]{:S(2)}, u32[]{:S(2)}) collective-permute-start(bf16[4,48,1024]{2,1,0:T(8,128)(2,1)S(1)} %get-tuple-element.78), channel_id=1, source_target_pairs={{0,2},{2,0},{4,6},{6,4},{8,10},{10,8},{12,14},{14,12},{1,3},{3,1},... | collective-permute-start | bytes 1179656 | tf_op jit(solution)/shard_map/ppermute | solution.py:40
  110.5 25.0 %collective-permute-start.12 = (bf16[4,48,2048]{2,1,0:T(8,128)(2,1)S(1)}, bf16[4,48,2048]{2,1,0:T(8,128)(2,1)S(1)}, u32[]{:S(2)}, u32[]{:S(2)}) collective-permute-start(bf16[4,48,2048]{2,1,0:T(8,128)(2,1)S(1)} %get-tuple-element.63), channel_id=1, source_target_pairs={{0,2},{2,0},{4,6},{6,4},{8,10},{10,8},{12,14},{14,12},{1,3},{3,1},... | collective-permute-start | bytes 2359304 | tf_op jit(solution)/shard_map/ppermute | solution.py:40
  111.1 16.6 %collective-permute-start.9 = (bf16[1,48,2048]{2,1,0:T(8,128)(2,1)S(1)}, bf16[1,48,2048]{2,1,0:T(8,128)(2,1)S(1)}, u32[]{:S(2)}, u32[]{:S(2)}) collective-permute-start(bf16[1,48,2048]{2,1,0:T(8,128)(2,1)S(1)} %get-tuple-element.59), channel_id=1, source_target_pairs={{0,4},{2,6},{4,0},{6,2},{8,12},{10,14},{12,8},{14,10},{1,5},{3,7},... | collective-permute-start | bytes 589832 | tf_op jit(solution)/shard_map/ppermute | solution.py:40
  112.7 16.5 %collective-permute-start.10 = (bf16[1,48,2048]{2,1,0:T(8,128)(2,1)S(1)}, bf16[1,48,2048]{2,1,0:T(8,128)(2,1)S(1)}, u32[]{:S(2)}, u32[]{:S(2)}) collective-permute-start(bf16[1,48,2048]{2,1,0:T(8,128)(2,1)S(1)} %get-tuple-element.60), channel_id=1, source_target_pairs={{0,8},{2,10},{4,12},{6,14},{8,0},{10,2},{12,4},{14,6},{1,9},{3,11}... | collective-permute-start | bytes 589832 | tf_op jit(solution)/shard_map/ppermute | solution.py:40
  127.8 12.4 %collective-permute-start.20 = (bf16[384,1024]{1,0:T(8,128)(2,1)S(1)}, bf16[384,1024]{1,0:T(8,128)(2,1)S(1)}, u32[]{:S(2)}, u32[]{:S(2)}) collective-permute-start(bf16[384,1024]{1,0:T(8,128)(2,1)S(1)} %get-tuple-element.76), channel_id=1, source_target_pairs={{0,1},{1,0},{2,3},{3,2},{4,5},{5,4},{6,7},{7,6},{8,9},{9,8},{10,11... | collective-permute-start | bytes 2359304 | tf_op jit(solution)/shard_map/ppermute | solution.py:40
  135.7 17.3 %collective-permute-start.13 = (bf16[1,48,2048]{2,1,0:T(8,128)(2,1)S(1)}, bf16[1,48,2048]{2,1,0:T(8,128)(2,1)S(1)}, u32[]{:S(2)}, u32[]{:S(2)}) collective-permute-start(bf16[1,48,2048]{2,1,0:T(8,128)(2,1)S(1)} %get-tuple-element.65), channel_id=1, source_target_pairs={{0,4},{2,6},{4,0},{6,2},{8,12},{10,14},{12,8},{14,10},{1,5},{3,7},... | collective-permute-start | bytes 589832 | tf_op jit(solution)/shard_map/ppermute | solution.py:40
  137.1 17.8 %collective-permute-start.14 = (bf16[1,48,2048]{2,1,0:T(8,128)(2,1)S(1)}, bf16[1,48,2048]{2,1,0:T(8,128)(2,1)S(1)}, u32[]{:S(2)}, u32[]{:S(2)}) collective-permute-start(bf16[1,48,2048]{2,1,0:T(8,128)(2,1)S(1)} %get-tuple-element.66), channel_id=1, source_target_pairs={{0,8},{2,10},{4,12},{6,14},{8,0},{10,2},{12,4},{14,6},{1,9},{3,11}... | collective-permute-start | bytes 589832 | tf_op jit(solution)/shard_map/ppermute | solution.py:40
  138.7 16.5 %collective-permute-start.15 = (bf16[1,48,2048]{2,1,0:T(8,128)(2,1)S(1)}, bf16[1,48,2048]{2,1,0:T(8,128)(2,1)S(1)}, u32[]{:S(2)}, u32[]{:S(2)}) collective-permute-start(bf16[1,48,2048]{2,1,0:T(8,128)(2,1)S(1)} %get-tuple-element.67), channel_id=1, source_target_pairs={{0,12},{2,14},{4,8},{6,10},{8,4},{10,6},{12,0},{14,2},{1,13},{3,15... | collective-permute-start | bytes 589832 | tf_op jit(solution)/shard_map/ppermute | solution.py:40
  145.2 19.0 %collective-permute-start.22 = (bf16[1,48,1024]{2,1,0:T(8,128)(2,1)S(1)}, bf16[1,48,1024]{2,1,0:T(8,128)(2,1)S(1)}, u32[]{:S(2)}, u32[]{:S(2)}) collective-permute-start(bf16[1,48,1024]{2,1,0:T(8,128)(2,1)S(1)} %get-tuple-element.80), channel_id=1, source_target_pairs={{0,4},{2,6},{4,0},{6,2},{8,12},{10,14},{12,8},{14,10},{1,5},{3,7},... | collective-permute-start | bytes 294920 | tf_op jit(solution)/shard_map/ppermute | solution.py:40
  151.5 14.8 %collective-permute-start.23 = (bf16[1,48,1024]{2,1,0:T(8,128)(2,1)S(1)}, bf16[1,48,1024]{2,1,0:T(8,128)(2,1)S(1)}, u32[]{:S(2)}, u32[]{:S(2)}) collective-permute-start(bf16[1,48,1024]{2,1,0:T(8,128)(2,1)S(1)} %get-tuple-element.81), channel_id=1, source_target_pairs={{0,8},{2,10},{4,12},{6,14},{8,0},{10,2},{12,4},{14,6},{1,9},{3,11}... | collective-permute-start | bytes 294920 | tf_op jit(solution)/shard_map/ppermute | solution.py:40
  153.0 13.3 %collective-permute-start.24 = (bf16[1,48,1024]{2,1,0:T(8,128)(2,1)S(1)}, bf16[1,48,1024]{2,1,0:T(8,128)(2,1)S(1)}, u32[]{:S(2)}, u32[]{:S(2)}) collective-permute-start(bf16[1,48,1024]{2,1,0:T(8,128)(2,1)S(1)} %get-tuple-element.82), channel_id=1, source_target_pairs={{0,12},{2,14},{4,8},{6,10},{8,4},{10,6},{12,0},{14,2},{1,13},{3,15... | collective-permute-start | bytes 294920 | tf_op jit(solution)/shard_map/ppermute | solution.py:40
  154.9 11.4 %collective-permute-start.26 = (bf16[1,48,1024]{2,1,0:T(8,128)(2,1)S(1)}, bf16[1,48,1024]{2,1,0:T(8,128)(2,1)S(1)}, u32[]{:S(2)}, u32[]{:S(2)}) collective-permute-start(bf16[1,48,1024]{2,1,0:T(8,128)(2,1)S(1)} %get-tuple-element.86), channel_id=1, source_target_pairs={{0,4},{2,6},{4,0},{6,2},{8,12},{10,14},{12,8},{14,10},{1,5},{3,7},... | collective-permute-start | bytes 294920 | tf_op jit(solution)/shard_map/ppermute | solution.py:40
  155.2 14.2 %collective-permute-start.27 = (bf16[1,48,1024]{2,1,0:T(8,128)(2,1)S(1)}, bf16[1,48,1024]{2,1,0:T(8,128)(2,1)S(1)}, u32[]{:S(2)}, u32[]{:S(2)}) collective-permute-start(bf16[1,48,1024]{2,1,0:T(8,128)(2,1)S(1)} %get-tuple-element.87), channel_id=1, source_target_pairs={{0,8},{2,10},{4,12},{6,14},{8,0},{10,2},{12,4},{14,6},{1,9},{3,11}... | collective-permute-start | bytes 294920 | tf_op jit(solution)/shard_map/ppermute | solution.py:40
  (10 other events, 81.6 us)
